TPU v7x, 32 devices: a whole 2x2x4 slice. The times are simulated.
32 devices in a mesh: wide: 8 (over y, x, core), narrow: 4 (over z).
Axes of the slice: x: 2, y: 2, z: 4, core: 2. Of those that a mesh axis runs over, the one named last changes fastest.
Arguments:
- amplitudes: bfloat16 [2048, 1024], P('narrow'), may hold values from -6 to 6
- integrals: bfloat16 [64, 128, 128], P('wide', 'narrow'), may hold values from -0.5 to 0.5
- in_tile: int32 [64], P('wide'), may hold values from 0 to 7
- counts: int32 [8], P('wide'), may hold values from 1 to 8, as said below
- out_tile: int32 [64], P('wide'), may hold values from 0 to 15, as said below
- owner_map: int32 [16], replicated, may hold values from 0 to 15, as said below
Outputs:
- residual: float32 [2048, 2048], P('narrow', 'wide')
Inputs may be any that keep to these rules, and one draw needn't show every extreme that they name: `counts`: some home device has exactly 8 live tasks in every draw. `out_tile`: call device owner_map[t] // 2 the owner of tile t. The 8 slots of one home device have tiles of pairwise different owners, and the live tasks of all homes give one owner at most 4 tasks; some owner receives exactly 4 in every draw. `owner_map`: A permutation of the residual tiles.
All inputs are finite; a program needn't handle non-finite values.
Results may differ from a plain program's by a relative error of at most 0.0029.
Values may be sent and summed in bfloat16 or wider, within the bound.
No kernel may reach another device: no remote copies, remote signals or barrier semaphores. Data moves between devices by JAX's collectives and lax.ppermute only.
A program may use at most 64 MiB of HBM per device.

v0:
```python
import jax
import jax.numpy as jnp
from jax import lax
from jax.sharding import PartitionSpec as P


def tile_position(tile_ids, owner_map):
    tile_total = owner_map.shape[0]
    hit = tile_ids[:, None] == jnp.arange(tile_total, dtype=jnp.int32)[None, :]
    return jnp.sum(jnp.where(hit, owner_map[None, :], 0), axis=1)


def shards(amplitudes, integrals, in_tile, counts, out_tile, owner_map):
    slot_count = integrals.shape[0]
    tile_width = integrals.shape[2]
    recv_count = slot_count // 2
    row_count = amplitudes.shape[0]
    tile_count = amplitudes.shape[1] // tile_width
    wide_count = lax.axis_size("wide")
    own_count = owner_map.shape[0] // wide_count
    slot_ids = jnp.arange(slot_count, dtype=jnp.int32)
    is_live = slot_ids < counts[0]
    target = tile_position(out_tile, owner_map) // own_count
    task_label = jnp.where(is_live, out_tile + 1, 0)
    task_meta = jnp.stack([task_label, in_tile], 1).astype(jnp.float32)
    owners = jnp.arange(wide_count, dtype=jnp.int32)[:, None]
    send_match = is_live[None, :] & (target[None, :] == owners)
    send_meta = jnp.dot(send_match.astype(jnp.float32), task_meta).astype(jnp.bfloat16)
    send_rows = jnp.einsum(
        "oh,hrc->orc",
        send_match.astype(jnp.bfloat16),
        integrals,
        preferred_element_type=jnp.float32,
    ).astype(jnp.bfloat16)
    pieces, task_info = (
        lax.all_to_all(send_rows, "wide", split_axis=0, concat_axis=0, tiled=True),
        lax.all_to_all(send_meta, "wide", split_axis=0, concat_axis=0, tiled=True),
    )
    task_info = task_info.astype(jnp.float32)
    is_mine = task_info[:, 0] > 0.5
    compact_rank = jnp.cumsum(is_mine.astype(jnp.int32)) - 1
    pick_rows = (
        is_mine[None, :]
        & (compact_rank[None, :] == jnp.arange(recv_count, dtype=jnp.int32)[:, None])
    ).astype(jnp.bfloat16)
    chosen = jnp.einsum(
        "um,mrc->urc", pick_rows, pieces, preferred_element_type=jnp.float32
    ).astype(jnp.bfloat16)
    chosen_info = jnp.dot(pick_rows.astype(jnp.float32), task_info)
    tile_ids = chosen_info[:, 0].astype(jnp.int32) - 1
    source_tile = chosen_info[:, 1].astype(jnp.int32)
    blocks = amplitudes.reshape(row_count, tile_count, tile_width)
    pick_in = (source_tile[:, None] == jnp.arange(tile_count, dtype=jnp.int32)[None, :]).astype(
        jnp.bfloat16
    )
    selected = jnp.einsum(
        "uk,pkc->upc", pick_in, blocks, preferred_element_type=jnp.float32
    ).astype(jnp.bfloat16)
    products = jnp.einsum(
        "upr,urc->upc",
        selected,
        lax.all_gather(chosen, "narrow", axis=1, tiled=True),
        preferred_element_type=jnp.float32,
    ).astype(jnp.bfloat16)
    local_place = tile_position(tile_ids, owner_map) % own_count
    assign_out = (
        (tile_ids[:, None] >= 0)
        & (local_place[:, None] == jnp.arange(own_count, dtype=jnp.int32)[None, :])
    ).astype(jnp.bfloat16)
    result = jnp.einsum("uj,upc->pjc", assign_out, products, preferred_element_type=jnp.float32)
    return result.reshape(row_count, own_count * tile_width)


def solution(mesh):
    return jax.shard_map(
        shards,
        mesh=mesh,
        in_specs=(
            P("narrow", None),
            P("wide", "narrow", None),
            P("wide"),
            P("wide"),
            P("wide"),
            P(),
        ),
        out_specs=P("narrow", "wide"),
        check_vma=False,
    )
```

profile of v0, /device:TPU:0, one launch (start us, length us, event | category | flops | bytes accessed | tf_op | source)
XLA Modules:
  0.0 36.6 jit_solution(8146587262540934250)
XLA Ops:
  0.7 0.6 %copy-done.1 = s32[8]{0:T(128)S(1)} copy-done((s32[8]{0:T(128)S(1)}, s32[8]{0:T(128)}, u32[]{:S(2)}) %copy-start.1) | copy-done | bytes 56
  1.3 0.0 copy-done.3
  1.4 0.2 select_reduce_fusion
  1.6 0.0 copy-start.2
  1.6 0.6 %copy-done.2 = s32[8]{0:T(128)S(1)} copy-done((s32[8]{0:T(128)S(1)}, s32[8]{0:T(128)}, u32[]{:S(2)}) %copy-start.2) | copy-done | bytes 56
  2.2 0.1 fusion
  2.3 0.7 %copy.15 = bf16[8,1,2]{2,1,0:T(2,128)(2,1)} copy(bf16[8,1,2]{0,2,1:T(2,128)(2,1)S(1)} %fusion) | data formatting | bytes 64 | tf_op jit(solution)/shard_map/all_to_all | solution.py:37
  3.0 5.2 %all-to-all-start = ((bf16[8,1,2]{2,1,0:T(2,128)(2,1)}), bf16[8,1,2]{2,1,0:T(2,128)(2,1)S(1)}, u32[]{:S(2)}, u32[]{:S(2)}) async-start(bf16[8,1,2]{2,1,0:T(2,128)(2,1)} %copy.15), calls=%async_computation | async-start | bytes 8192 | tf_op jit(solution)/shard_map/all_to_all | solution.py:37
  8.2 1.5 %copy.23 = bf16[64,8,8,128]{3,2,1,0:T(8,128)(2,1)S(1)} copy(bf16[64,8,8,128]{3,1,2,0:T(8,128)(2,1)} %bitcast.43) | data formatting | bytes 2097152
  9.7 0.1 convolution_convert_fusion.2
  9.8 0.6 %copy.18 = bf16[8,32,128]{2,1,0:T(8,128)(2,1)} copy(bf16[8,32,128]{2,0,1:T(8,128)(2,1)S(1)} %convolution_convert_fusion.2) | data formatting | bytes 131072 | tf_op jit(solution)/shard_map/convert_element_type | solution.py:34
  10.5 2.4 %all-to-all-done = bf16[8,1,2]{2,1,0:T(2,128)(2,1)S(1)} async-done(((bf16[8,1,2]{2,1,0:T(2,128)(2,1)}), bf16[8,1,2]{2,1,0:T(2,128)(2,1)S(1)}, u32[]{:S(2)}, u32[]{:S(2)}) %all-to-all-start) | async-done | bytes 64 | tf_op jit(solution)/shard_map/all_to_all | solution.py:37
  12.9 3.4 %all-to-all-start.1 = ((bf16[8,32,128]{2,1,0:T(8,128)(2,1)}), bf16[8,32,128]{2,1,0:T(8,128)(2,1)S(1)}, u32[]{:S(2)}, u32[]{:S(2)}) async-start(bf16[8,32,128]{2,1,0:T(8,128)(2,1)} %copy.18), calls=%async_computation.1 | async-start | bytes 131072 | tf_op jit(solution)/shard_map/all_to_all | solution.py:36
  16.2 0.1 copy.16
  16.3 0.2 reduce-window.8
  16.5 0.1 fusion.23
  16.7 0.2 select_reduce_fusion.1
  16.8 0.5 %convolution_convert_fusion.1 = bf16[4,512,128]{2,0,1:T(4,128)(2,1)S(1)} fusion(bf16[512,8,128]{2,1,0:T(8,128)(2,1)S(1)} %bitcast.41, s32[4]{0:T(128)S(1)} %convert_bitcast_fusion), kind=kOutput, calls=%fused_computation.1 | convolution fusion | flops 4456480 | bytes 1572880 | tf_op jit(solution)/shard_map/uk,pkc->upc/dot_general | solution.py:56
  17.4 3.8 %all-to-all-done.1 = bf16[8,32,128]{2,1,0:T(8,128)(2,1)S(1)} async-done(((bf16[8,32,128]{2,1,0:T(8,128)(2,1)}), bf16[8,32,128]{2,1,0:T(8,128)(2,1)S(1)}, u32[]{:S(2)}, u32[]{:S(2)}) %all-to-all-start.1) | async-done | bytes 65568 | tf_op jit(solution)/shard_map/all_to_all | solution.py:36
  21.2 0.1 convolution_convert_fusion.3
  21.3 13.6 %all_gather.3 = bf16[4,128,128]{2,0,1:T(4,128)(2,1)S(1)} all-gather(bf16[4,32,128]{2,0,1:T(4,128)(2,1)S(1)} %convolution_convert_fusion.3), channel_id=1, replica_groups=mesh['wide'=8,'narrow'=4] {'narrow'}, dimensions={1}, use_global_device_ids=true | all-gather | bytes 163840 | tf_op jit(solution)/shard_map/all_gather | solution.py:62
  35.0 0.3 convolution_convert_fusion
  35.3 0.5 %fusion.2 = f32[512,128,2]{1,2,0:T(2,128)S(1)} fusion(bf16[4,512,128]{2,1,0:T(8,128)(2,1)S(1)} %convolution_convert_fusion, pred[4]{0:T(512)(128)(4,1)S(1)} %compare_bitcast_fusion, s32[4]{0:T(128)S(1)} %and_select_fusion), kind=kOutput, calls=%fused_computation.8 | convolution fusion | flops 1048592 | bytes 1048596 | tf_op jit(solution)/shard_map/uj,upc->pjc/dot_general | solution.py:70
  35.8 0.8 %copy.36 = f32[64,8,2,128]{3,1,2,0:T(8,128)} copy(f32[64,8,2,128]{3,2,1,0:T(2,128)S(1)} %bitcast.42) | data formatting | bytes 1048576
  (13 shorter events, 0.1 us)
Async XLA Ops:
  0.0 9.7 %copy-start = (bf16[8,32,128]{2,1,0:T(8,128)(2,1)S(1)}, bf16[8,32,128]{2,1,0:T(8,128)(2,1)}, u32[]{:S(2)}) copy-start(bf16[8,32,128]{2,1,0:T(8,128)(2,1)} %param.7) | copy-start | bytes 196612
  0.7 0.7 %copy-start.1 = (s32[8]{0:T(128)S(1)}, s32[8]{0:T(128)}, u32[]{:S(2)}) copy-start(s32[8]{0:T(128)} %param.10) | copy-start | bytes 100
  0.7 0.7 %copy-start.3 = (s32[16]{0:T(128)S(1)}, s32[16]{0:T(128)}, u32[]{:S(2)}) copy-start(s32[16]{0:T(128)} %param.11) | copy-start | bytes 196
  1.6 0.7 %copy-start.2 = (s32[8]{0:T(128)S(1)}, s32[8]{0:T(128)}, u32[]{:S(2)}) copy-start(s32[8]{0:T(128)} %param.8) | copy-start | bytes 100
  3.0 9.8 %all-to-all-start = ((bf16[8,1,2]{2,1,0:T(2,128)(2,1)}), bf16[8,1,2]{2,1,0:T(2,128)(2,1)S(1)}, u32[]{:S(2)}, u32[]{:S(2)}) async-start(bf16[8,1,2]{2,1,0:T(2,128)(2,1)} %copy.15), calls=%async_computation | async-start | bytes 8192 | tf_op jit(solution)/shard_map/all_to_all | solution.py:37
  12.9 8.3 %all-to-all-start.1 = ((bf16[8,32,128]{2,1,0:T(8,128)(2,1)}), bf16[8,32,128]{2,1,0:T(8,128)(2,1)S(1)}, u32[]{:S(2)}, u32[]{:S(2)}) async-start(bf16[8,32,128]{2,1,0:T(8,128)(2,1)} %copy.18), calls=%async_computation.1 | async-start | bytes 131072 | tf_op jit(solution)/shard_map/all_to_all | solution.py:36
where the time goes:
time: 36.9 us; the launch traced here: 36.6 us
  blocking collectives  13.6 us (37%)
  starting transfers between devices  8.52 us (23%)
  waiting for transfers between devices  6.18 us (17%)
  local copies, waits for them, and re-layouts  5.04 us (14%)
  matrix products  1.81 us (5%)
  between operations  0.78 us (2%)
  other arithmetic  0.61 us (2%)
    all_gather x1, blocking collectives, shards(): lax.all_gather(chosen, 'narrow', axis=1, tiled=True)  13.6 us
    all_to_all x1, starting transfers between devices, shards(): lax.all_to_all(send_meta, 'wide', split_axis=0, concat_axis=0, tiled=True)  5.17 us
    all_to_all x1, waiting for transfers between devices, shards(): lax.all_to_all(send_rows, 'wide', split_axis=0, concat_axis=0, tiled=True)  3.81 us
    unnamed x10, local copies, waits for them, and re-layouts  3.61 us
    all_to_all x1, starting transfers between devices, shards(): lax.all_to_all(send_rows, 'wide', split_axis=0, concat_axis=0, tiled=True)  3.35 us
    all_to_all x1, waiting for transfers between devices, shards(): lax.all_to_all(send_meta, 'wide', split_axis=0, concat_axis=0, tiled=True)  2.36 us
    all_to_all x2, local copies, waits for them, and re-layouts, shards(): lax.all_to_all(send_meta, 'wide', split_axis=0, concat_axis=0, tiled=True)  0.78 us
  transfers between devices with their start and end apart: 2, of which 2 were waited for; matrix products, arithmetic and copies ran while one was open for 9% of the time, Pallas kernels for 0%

commit v1 on v0

v1 whole, which is shorter than its diff:
```python
import functools

import jax
import jax.numpy as jnp
from jax import lax
from jax.experimental import pallas as pl
from jax.experimental.pallas import tpu as pltpu
from jax.sharding import PartitionSpec as P

META = 16


def pack_kernel(own_count, in_tile, counts, out_tile, owner_map, rows_ref, out_ref, slab, sems):
    slot_count, row_count, _ = rows_ref.shape
    depth_count = out_ref.shape[1]
    slab[...] = jnp.zeros_like(slab)
    upper = lax.broadcasted_iota(jnp.int32, (META, slab.shape[2]), 0) < META // 2

    def place(h, _):
        spot = owner_map[out_tile[h]]
        owner = lax.div(spot, own_count)
        code = jnp.where(h < counts[0], lax.rem(spot, own_count) + 1, 0)
        slab[owner, :row_count] = rows_ref[h]
        slab[owner, row_count:] = jnp.where(
            upper, code.astype(jnp.float32), in_tile[h].astype(jnp.float32)
        ).astype(slab.dtype)
        return 0

    lax.fori_loop(0, slot_count, place, 0, unroll=slot_count <= 8)
    copies = [
        pltpu.make_async_copy(slab, out_ref.at[:, z], sems.at[z]) for z in range(depth_count)
    ]
    for copy in copies:
        copy.start()
    for copy in copies:
        copy.wait()


def ladder_kernel(rows, amp_ref, got_ref, out_ref, column, place, source):
    wide_count, depth_count, _, width = got_ref.shape
    padded = got_ref.shape[2] - META

    def list_live(w, found):
        meta = got_ref[w, 0, padded:].astype(jnp.float32)
        code = jnp.max(meta[: META // 2]).astype(jnp.int32)
        tile = jnp.max(meta[META // 2 :]).astype(jnp.int32)

        @pl.when(code > 0)
        def _():
            source[found] = w
            column[found] = tile
            place[found] = code - 1

        return found + (code > 0).astype(jnp.int32)

    live = lax.fori_loop(0, wide_count, list_live, jnp.int32(0), unroll=wide_count <= 8)
    out_ref[...] = jnp.zeros_like(out_ref)

    def add_task(u, _):
        if rows == padded:
            tile = got_ref[source[u], :, :padded].reshape(depth_count * rows, width)
        else:
            tile = got_ref[source[u], :, :padded].astype(jnp.float32)[:, :rows]
            tile = tile.reshape(depth_count * rows, width).astype(got_ref.dtype)
        columns = amp_ref[:, pl.ds(pl.multiple_of(column[u] * width, width), width)]
        spot = pl.ds(pl.multiple_of(place[u] * width, width), width)
        out_ref[:, spot] += jnp.dot(columns, tile, preferred_element_type=jnp.float32)
        return 0

    lax.fori_loop(0, live, add_task, 0)


def shards(amplitudes, integrals, in_tile, counts, out_tile, owner_map):
    slot_count, rows, width = integrals.shape
    wide_count = lax.axis_size("wide")
    depth_count = lax.axis_size("narrow")
    own_count = owner_map.shape[0] // wide_count
    padded = -(-rows // META) * META
    if padded != rows:
        integrals = jnp.pad(integrals, ((0, 0), (0, padded - rows), (0, 0)))
    length = padded + META
    smem = pl.BlockSpec(memory_space=pltpu.SMEM)
    vmem = pl.BlockSpec(memory_space=pltpu.VMEM)
    send = pl.pallas_call(
        functools.partial(pack_kernel, own_count),
        out_shape=jax.ShapeDtypeStruct((wide_count, depth_count, length, width), integrals.dtype),
        in_specs=[smem] * 4 + [vmem],
        out_specs=pl.BlockSpec(memory_space=pl.ANY),
        scratch_shapes=[
            pltpu.VMEM((wide_count, length, width), integrals.dtype),
            pltpu.SemaphoreType.DMA((depth_count,)),
        ],
        name="pack",
    )(in_tile, counts, out_tile, owner_map, integrals)
    got = lax.all_to_all(
        send.reshape(wide_count * depth_count, length, width),
        ("wide", "narrow"),
        split_axis=0,
        concat_axis=0,
        tiled=True,
    ).reshape(wide_count, depth_count, length, width)
    return pl.pallas_call(
        functools.partial(ladder_kernel, rows),
        out_shape=jax.ShapeDtypeStruct((amplitudes.shape[0], own_count * width), jnp.float32),
        in_specs=[vmem, vmem],
        out_specs=vmem,
        scratch_shapes=[pltpu.SMEM((wide_count,), jnp.int32)] * 3,
        compiler_params=pltpu.CompilerParams(vmem_limit_bytes=32 * 2**20),
        name="ladder",
    )(amplitudes, got)


def solution(mesh):
    return jax.shard_map(
        shards,
        mesh=mesh,
        in_specs=(
            P("narrow", None),
            P("wide", "narrow", None),
            P("wide"),
            P("wide"),
            P("wide"),
            P(),
        ),
        out_specs=P("narrow", "wide"),
        check_vma=False,
    )
```

time: 36.9 us -> 24.2 us (0.66)
  the two profiles are of different devices: /device:TPU:0 before, /device:TPU:1 now
where the time goes in v1:
time: 24.2 us; the launch traced here: 24 us
  blocking collectives  19.9 us (82%)
  Pallas kernels  3.35 us (14%)
  between operations  0.75 us (3%)
    all_to_all x1, blocking collectives, shards(): lax.all_to_all(send.reshape(wide_count * depth_count, length, width), ('w...  19.9 us
    pallas_call x1, Pallas kernels, shards(): pl.pallas_call(functools.partial(ladder_kernel, rows), out_shape=jax.Shap...  1.68 us
    pallas_call x1, Pallas kernels, shards(): pl.pallas_call(functools.partial(pack_kernel, own_count), out_shape=jax.S...  1.67 us

profile of v1, /device:TPU:1, one launch (start us, length us, event | category | flops | bytes accessed | tf_op | source)
XLA Modules:
  0.0 24.0 jit_solution(3073862717236603121)
XLA Ops:
  0.0 0.0 copy-start
  0.7 1.7 %pack.1 = bf16[8,4,48,128]{3,2,1,0:T(8,128)(2,1)} custom-call(s32[8]{0:T(128)} %in_tile.1, s32[1]{0:T(128)S(6)} %copy.7.counts, s32[8]{0:T(128)} %out_tile.1, s32[16]{0:T(128)} %owner_map.1, bf16[8,32,128]{2,1,0:T(8,128)(2,1)} %rows_ref.1), custom_call_target="tpu_custom_call" | custom-call | tf_op jit(solution)/shard_map/pack/pallas_call | solution.py:84
  2.4 19.9 %all_to_all.5 = bf16[32,48,128]{2,1,0:T(8,128)(2,1)S(1)} all-to-all(bf16[32,48,128]{2,1,0:T(8,128)(2,1)} %bitcast.3), channel_id=1, replica_groups=mesh['wide'=8,'narrow'=4] {'wide','narrow'}, dimensions={0} | all-to-all | bytes 786432 | tf_op jit(solution)/shard_map/all_to_all | solution.py:95
  22.3 0.0 copy-done
  22.3 1.7 %ladder.1 = f32[512,256]{1,0:T(8,128)} custom-call(bf16[512,1024]{1,0:T(8,128)(2,1)S(1)} %copy-done, bf16[8,4,48,128]{3,2,1,0:T(8,128)(2,1)S(1)} %bitcast.2), custom_call_target="tpu_custom_call" | custom-call | tf_op jit(solution)/shard_map/ladder/pallas_call | solution.py:102
Async XLA Ops:
  0.0 22.3 %copy-start = (bf16[512,1024]{1,0:T(8,128)(2,1)S(1)}, bf16[512,1024]{1,0:T(8,128)(2,1)}, u32[]{:S(2)}) copy-start(bf16[512,1024]{1,0:T(8,128)(2,1)} %amp_ref.1) | copy-start | bytes 3145732

commit v2 on v1

v2 whole, which is shorter than its diff:
```python
import functools

import jax
import jax.numpy as jnp
from jax import lax
from jax.experimental import pallas as pl
from jax.experimental.pallas import tpu as pltpu
from jax.sharding import PartitionSpec as P

META = 16


def pack_kernel(own_count, in_tile, counts, out_tile, owner_map, rows_ref, *outs_and_slab):
    *out_refs, slab = outs_and_slab
    slot_count, row_count, width = rows_ref.shape
    wide_count = len(out_refs)
    me = lax.axis_index("wide")
    slab[...] = jnp.zeros_like(slab)
    upper = lax.broadcasted_iota(jnp.int32, (META, width), 0) < META // 2

    def place(h, _):
        spot = owner_map[out_tile[h]]
        owner = lax.div(spot, own_count)
        step = lax.rem(owner - me + wide_count, wide_count)
        code = jnp.where(h < counts[0], lax.rem(spot, own_count) + 1, 0)
        slab[step, :row_count] = rows_ref[h]
        slab[step, row_count:] = jnp.where(
            upper, code.astype(jnp.float32), in_tile[h].astype(jnp.float32)
        ).astype(slab.dtype)
        return 0

    lax.fori_loop(0, slot_count, place, 0, unroll=slot_count <= 8)
    for step, out_ref in enumerate(out_refs):
        out_ref[...] = slab[step]


def compact_kernel(*refs):
    *got_refs, tiles_ref, column, place = refs
    recv_count, padded, _ = tiles_ref.shape
    tiles_ref[...] = jnp.zeros_like(tiles_ref)
    for u in range(recv_count):
        column[u] = 0
        place[u] = -1
    found = jnp.int32(0)
    for got_ref in got_refs:
        meta = got_ref[padded:].astype(jnp.float32)
        code = jnp.max(meta[: META // 2]).astype(jnp.int32)
        tile = jnp.max(meta[META // 2 :]).astype(jnp.int32)

        @pl.when((code > 0) & (found < recv_count))
        def _():
            tiles_ref[found] = got_ref[:padded]
            column[found] = tile
            place[found] = code - 1

        found += (code > 0).astype(jnp.int32)


def ladder_kernel(rows, column, place, amp_ref, *refs):
    *got_refs, out_ref, tiles = refs
    recv_count, padded, width = got_refs[0].shape
    depth_count = len(got_refs)
    me = lax.axis_index("narrow")
    for step, got_ref in enumerate(got_refs):
        depth = lax.rem(me - step + depth_count, depth_count)
        spot = pl.ds(pl.multiple_of(depth * rows, rows), rows)
        tiles[:, spot] = got_ref[...].astype(tiles.dtype)[:, :rows]
    out_ref[...] = jnp.zeros_like(out_ref)

    def add_task(u, _):
        @pl.when(place[u] >= 0)
        def _():
            columns = amp_ref[:, pl.ds(pl.multiple_of(column[u] * width, width), width)]
            spot = pl.ds(pl.multiple_of(place[u] * width, width), width)
            out_ref[:, spot] += jnp.dot(
                columns, tiles[u].astype(amp_ref.dtype), preferred_element_type=jnp.float32
            )

        return 0

    lax.fori_loop(0, recv_count, add_task, 0)


def shift(value, axis, step):
    count = lax.axis_size(axis)
    return lax.ppermute(value, axis, [(d, (d + step) % count) for d in range(count)])


def shards(amplitudes, integrals, in_tile, counts, out_tile, owner_map):
    slot_count, rows, width = integrals.shape
    wide_count = lax.axis_size("wide")
    depth_count = lax.axis_size("narrow")
    own_count = owner_map.shape[0] // wide_count
    recv_count = slot_count // 2
    padded = -(-rows // META) * META
    if padded != rows:
        integrals = jnp.pad(integrals, ((0, 0), (0, padded - rows), (0, 0)))
    kind = integrals.dtype
    smem = pl.BlockSpec(memory_space=pltpu.SMEM)
    vmem = pl.BlockSpec(memory_space=pltpu.VMEM)
    sent = pl.pallas_call(
        functools.partial(pack_kernel, own_count),
        out_shape=[jax.ShapeDtypeStruct((padded + META, width), kind)] * wide_count,
        in_specs=[smem] * 4 + [vmem],
        out_specs=[vmem] * wide_count,
        scratch_shapes=[pltpu.VMEM((wide_count, padded + META, width), kind)],
        name="pack",
    )(in_tile, counts, out_tile, owner_map, integrals)
    got = [sent[0]] + [shift(sent[step], "wide", step) for step in range(1, wide_count)]
    tiles, column, place = pl.pallas_call(
        compact_kernel,
        out_shape=[
            jax.ShapeDtypeStruct((recv_count, padded, width), kind),
            jax.ShapeDtypeStruct((recv_count,), jnp.int32),
            jax.ShapeDtypeStruct((recv_count,), jnp.int32),
        ],
        in_specs=[vmem] * wide_count,
        out_specs=[vmem, smem, smem],
        name="compact",
    )(*got)
    parts = [tiles] + [shift(tiles, "narrow", step) for step in range(1, depth_count)]
    whole_kind = kind if rows % META == 0 else jnp.float32
    return pl.pallas_call(
        functools.partial(ladder_kernel, rows),
        out_shape=jax.ShapeDtypeStruct((amplitudes.shape[0], own_count * width), jnp.float32),
        in_specs=[smem, smem, vmem] + [vmem] * depth_count,
        out_specs=vmem,
        scratch_shapes=[pltpu.VMEM((recv_count, depth_count * rows, width), whole_kind)],
        compiler_params=pltpu.CompilerParams(vmem_limit_bytes=32 * 2**20),
        name="ladder",
    )(column, place, amplitudes, *parts)


def solution(mesh):
    return jax.shard_map(
        shards,
        mesh=mesh,
        in_specs=(
            P("narrow", None),
            P("wide", "narrow", None),
            P("wide"),
            P("wide"),
            P("wide"),
            P(),
        ),
        out_specs=P("narrow", "wide"),
        check_vma=False,
    )
```

time: 24.2 us -> 31.2 us (1.29)
  the two profiles are of different devices: /device:TPU:1 before, /device:TPU:0 now
where the time goes in v2:
time: 31.2 us; the launch traced here: 30.9 us
  starting transfers between devices  14.5 us (46%)
  waiting for transfers between devices  6.29 us (20%)
  Pallas kernels  6.1 us (20%)
  local copies, waits for them, and re-layouts  3.24 us (10%)
  between operations  0.73 us (2%)
    ppermute x10, starting transfers between devices, shift(): lax.ppermute(value, axis, [(d, (d + step) % count) for d in range(count)])  14.5 us
    ppermute x10, waiting for transfers between devices, shift(): lax.ppermute(value, axis, [(d, (d + step) % count) for d in range(count)])  6.29 us
    unnamed x24, local copies, waits for them, and re-layouts  3.24 us
    pallas_call x1, Pallas kernels, shards(): pl.pallas_call(compact_kernel, out_shape=[jax.ShapeDtypeStruct((recv_coun...  2.44 us
    pallas_call x1, Pallas kernels, shards(): pl.pallas_call(functools.partial(ladder_kernel, rows), out_shape=jax.Shap...  2.11 us
    pallas_call x1, Pallas kernels, shards(): pl.pallas_call(functools.partial(pack_kernel, own_count), out_shape=[jax....  1.55 us
  transfers between devices with their start and end apart: 10, of which 5 were waited for; matrix products, arithmetic and copies ran while one was open for 0% of the time, Pallas kernels for 0%

profile of v2, /device:TPU:0, one launch (start us, length us, event | category | flops | bytes accessed | tf_op | source)
XLA Modules:
  0.0 30.9 jit_solution(17364945168706262331)
XLA Ops:
  0.7 1.5 %pack.1 = (bf16[48,128]{1,0:T(8,128)(2,1)}, bf16[48,128]{1,0:T(8,128)(2,1)}, bf16[48,128]{1,0:T(8,128)(2,1)}, bf16[48,128]{1,0:T(8,128)(2,1)}, bf16[48,128]{1,0:...) custom-call(s32[8]{0:T(128)} %in_tile.1, s32[1]{0:T(128)S(6)} %copy.7.counts, ...), custom_call_target="tpu_custom_call" | custom-call | tf_op jit(solution)/shard_map/pack/pallas_call | solution.py:101
  2.2 0.5 %collective-permute-start = (bf16[48,128]{1,0:T(8,128)(2,1)}, bf16[48,128]{1,0:T(8,128)(2,1)S(1)}, u32[]{:S(2)}, u32[]{:S(2)}) collective-permute-start(bf16[48,128]{1,0:T(8,128)(2,1)} %get-tuple-element.17), channel_id=1, source_target_pairs={{0,4},{4,8},{8,12},{12,16},{16,20},{20,24},{24,28},{28,0},{1,5},{5... | collective-permute-start | bytes 36872 | tf_op jit(solution)/shard_map/ppermute | solution.py:86
  2.7 2.6 %collective-permute-start.1 = (bf16[48,128]{1,0:T(8,128)(2,1)}, bf16[48,128]{1,0:T(8,128)(2,1)S(1)}, u32[]{:S(2)}, u32[]{:S(2)}) collective-permute-start(bf16[48,128]{1,0:T(8,128)(2,1)} %get-tuple-element.18), channel_id=1, source_target_pairs={{0,8},{4,12},{8,16},{12,20},{16,24},{20,28},{24,0},{28,4},{1,9},{5... | collective-permute-start | bytes 36872 | tf_op jit(solution)/shard_map/ppermute | solution.py:86
  5.3 2.4 %collective-permute-start.2 = (bf16[48,128]{1,0:T(8,128)(2,1)}, bf16[48,128]{1,0:T(8,128)(2,1)S(1)}, u32[]{:S(2)}, u32[]{:S(2)}) collective-permute-start(bf16[48,128]{1,0:T(8,128)(2,1)} %get-tuple-element.19), channel_id=1, source_target_pairs={{0,12},{4,16},{8,20},{12,24},{16,28},{20,0},{24,4},{28,8},{1,13},{... | collective-permute-start | bytes 36872 | tf_op jit(solution)/shard_map/ppermute | solution.py:86
  7.6 0.5 %collective-permute-start.3 = (bf16[48,128]{1,0:T(8,128)(2,1)}, bf16[48,128]{1,0:T(8,128)(2,1)S(1)}, u32[]{:S(2)}, u32[]{:S(2)}) collective-permute-start(bf16[48,128]{1,0:T(8,128)(2,1)} %get-tuple-element.20), channel_id=1, source_target_pairs={{0,16},{4,20},{8,24},{12,28},{16,0},{20,4},{24,8},{28,12},{1,17},{... | collective-permute-start | bytes 36872 | tf_op jit(solution)/shard_map/ppermute | solution.py:86
  8.1 0.1 collective-permute-start.4
  8.2 0.0 collective-permute-done.refs_1_
  8.3 1.4 %collective-permute-start.5 = (bf16[48,128]{1,0:T(8,128)(2,1)}, bf16[48,128]{1,0:T(8,128)(2,1)S(1)}, u32[]{:S(2)}, u32[]{:S(2)}) collective-permute-start(bf16[48,128]{1,0:T(8,128)(2,1)} %get-tuple-element.22), channel_id=1, source_target_pairs={{0,24},{4,28},{8,0},{12,4},{16,8},{20,12},{24,16},{28,20},{1,25},{... | collective-permute-start | bytes 36872 | tf_op jit(solution)/shard_map/ppermute | solution.py:86
  9.7 2.3 %collective-permute-start.6 = (bf16[48,128]{1,0:T(8,128)(2,1)S(1)}, bf16[48,128]{1,0:T(8,128)(2,1)S(1)}, u32[]{:S(2)}, u32[]{:S(2)}) collective-permute-start(bf16[48,128]{1,0:T(8,128)(2,1)S(1)} %copy-done.11), channel_id=1, source_target_pairs={{0,28},{4,0},{8,4},{12,8},{16,12},{20,16},{24,20},{28,24},{1,29},{... | collective-permute-start | bytes 36872 | tf_op jit(solution)/shard_map/ppermute | solution.py:86
  12.0 0.0 collective-permute-done.2.refs_3_
  12.0 0.0 collective-permute-done.3.refs_4_
  12.1 0.1 collective-permute-done.5.refs_6_
  12.2 1.3 %collective-permute-done.6.refs_7_ = bf16[48,128]{1,0:T(8,128)(2,1)S(1)} collective-permute-done((bf16[48,128]{1,0:T(8,128)(2,1)S(1)}, bf16[48,128]{1,0:T(8,128)(2,1)S(1)}, u32[]{:S(2)}, u32[]{:S(2)}) %collective-permute-start.6) | collective-permute-done | bytes 12320 | tf_op jit(solution)/shard_map/ppermute | solution.py:86
  13.5 0.5 %copy-done.10 = bf16[48,128]{1,0:T(8,128)(2,1)} copy-done((bf16[48,128]{1,0:T(8,128)(2,1)}, bf16[48,128]{1,0:T(8,128)(2,1)S(1)}, u32[]{:S(2)}) %copy-start.10) | copy-done | bytes 12312
  14.0 2.4 %compact.1 = (bf16[4,32,128]{2,1,0:T(8,128)(2,1)}, s32[4]{0:T(128)}, s32[4]{0:T(128)}) custom-call(bf16[48,128]{1,0:T(8,128)(2,1)} %get-tuple-element.16.refs_0_, bf16[48,128]{1,0:T(8,128)(2,1)} %copy-done.4, bf16[48,128]{1,0:T(8,128)(2,1)} %copy-done.5, bf16[48,128]{1,0:T(8,128)(2,1)} %copy-done.6, bf16[48,128]{1,0:T(8,128)(2,1)} %copy-done.7, ...), custom_call_target="tpu_custom_call" | custom-call | tf_op jit(solution)/shard_map/compact/pallas_call | solution.py:110
  16.5 3.7 %collective-permute-start.9 = (bf16[4,32,128]{2,1,0:T(8,128)(2,1)}, bf16[4,32,128]{2,1,0:T(8,128)(2,1)S(1)}, u32[]{:S(2)}, u32[]{:S(2)}) collective-permute-start(bf16[4,32,128]{2,1,0:T(8,128)(2,1)} %get-tuple-element.26.refs_0_), channel_id=1, source_target_pairs={{0,3},{1,0},{2,1},{3,2},{4,7},{5,4},{6,5},{7,6},{8,11},{9,8},{10,9... | collective-permute-start | bytes 98312 | tf_op jit(solution)/shard_map/ppermute | solution.py:86
  20.1 1.0 %collective-permute-start.7 = (bf16[4,32,128]{2,1,0:T(8,128)(2,1)}, bf16[4,32,128]{2,1,0:T(8,128)(2,1)S(1)}, u32[]{:S(2)}, u32[]{:S(2)}) collective-permute-start(bf16[4,32,128]{2,1,0:T(8,128)(2,1)} %get-tuple-element.26.refs_0_), channel_id=1, source_target_pairs={{0,1},{1,2},{2,3},{3,0},{4,5},{5,6},{6,7},{7,4},{8,9},{9,10},{10,1... | collective-permute-start | bytes 98312 | tf_op jit(solution)/shard_map/ppermute | solution.py:86
  21.2 1.1 %collective-permute-done.9.refs_3_ = bf16[4,32,128]{2,1,0:T(8,128)(2,1)S(1)} collective-permute-done((bf16[4,32,128]{2,1,0:T(8,128)(2,1)}, bf16[4,32,128]{2,1,0:T(8,128)(2,1)S(1)}, u32[]{:S(2)}, u32[]{:S(2)}) %collective-permute-start.9) | collective-permute-done | bytes 32800 | tf_op jit(solution)/shard_map/ppermute | solution.py:86
  22.3 2.9 %collective-permute-done.8.refs_2_ = bf16[4,32,128]{2,1,0:T(8,128)(2,1)S(1)} collective-permute-done((bf16[4,32,128]{2,1,0:T(8,128)(2,1)}, bf16[4,32,128]{2,1,0:T(8,128)(2,1)S(1)}, u32[]{:S(2)}, u32[]{:S(2)}) %collective-permute-start.8) | collective-permute-done | bytes 32800 | tf_op jit(solution)/shard_map/ppermute | solution.py:86
  25.2 0.9 %collective-permute-done.7.refs_1_ = bf16[4,32,128]{2,1,0:T(8,128)(2,1)S(1)} collective-permute-done((bf16[4,32,128]{2,1,0:T(8,128)(2,1)}, bf16[4,32,128]{2,1,0:T(8,128)(2,1)S(1)}, u32[]{:S(2)}, u32[]{:S(2)}) %collective-permute-start.7) | collective-permute-done | bytes 32800 | tf_op jit(solution)/shard_map/ppermute | solution.py:86
  26.1 0.7 %copy-done.2 = s32[4]{0:T(128)S(1)} copy-done((s32[4]{0:T(128)S(1)}, s32[4]{0:T(128)}, u32[]{:S(2)}) %copy-start.2) | copy-done | bytes 40
  26.8 1.2 %copy-done = bf16[512,1024]{1,0:T(8,128)(2,1)S(1)} copy-done((bf16[512,1024]{1,0:T(8,128)(2,1)S(1)}, bf16[512,1024]{1,0:T(8,128)(2,1)}, u32[]{:S(2)}) %copy-start) | copy-done | bytes 1048600
  28.0 0.8 %copy-done.1 = bf16[4,32,128]{2,1,0:T(8,128)(2,1)S(1)} copy-done((bf16[4,32,128]{2,1,0:T(8,128)(2,1)S(1)}, bf16[4,32,128]{2,1,0:T(8,128)(2,1)}, u32[]{:S(2)}) %copy-start.1) | copy-done | bytes 32792
  28.7 2.1 %ladder.1 = f32[512,256]{1,0:T(8,128)} custom-call(s32[4]{0:T(128)S(1)} %copy-done.2, s32[4]{0:T(128)S(1)} %copy-done.3, bf16[512,1024]{1,0:T(8,128)(2,1)S(1)} %copy-done, bf16[4,32,128]{2,1,0:T(8,128)(2,1)S(1)} %copy-done.1, bf16[4,32,128]{2,1,0:T(8,128)(2,1)S(1)} %collective-permute-done.7.refs_1_, bf16[4,32,128]{2,1,0:T(8,128)(2,1)S(1)} %collective-permute-done.8.refs_2_, ...), custom_call_target="tpu_custom_call" | custom-call | tf_op jit(solution)/shard_map/ladder/pallas_call | solution.py:123
  (23 shorter events, 0.0 us)
Async XLA Ops:
  2.2 7.5 %copy-start.11 = (bf16[48,128]{1,0:T(8,128)(2,1)S(1)}, bf16[48,128]{1,0:T(8,128)(2,1)}, u32[]{:S(2)}) copy-start(bf16[48,128]{1,0:T(8,128)(2,1)} %get-tuple-element.23) | copy-start | bytes 36868
  2.2 6.0 %collective-permute-start = (bf16[48,128]{1,0:T(8,128)(2,1)}, bf16[48,128]{1,0:T(8,128)(2,1)S(1)}, u32[]{:S(2)}, u32[]{:S(2)}) collective-permute-start(bf16[48,128]{1,0:T(8,128)(2,1)} %get-tuple-element.17), channel_id=1, source_target_pairs={{0,4},{4,8},{8,12},{12,16},{16,20},{20,24},{24,28},{28,0},{1,5},{5... | collective-permute-start | bytes 36872 | tf_op jit(solution)/shard_map/ppermute | solution.py:86
  2.7 7.0 %collective-permute-start.1 = (bf16[48,128]{1,0:T(8,128)(2,1)}, bf16[48,128]{1,0:T(8,128)(2,1)S(1)}, u32[]{:S(2)}, u32[]{:S(2)}) collective-permute-start(bf16[48,128]{1,0:T(8,128)(2,1)} %get-tuple-element.18), channel_id=1, source_target_pairs={{0,8},{4,12},{8,16},{12,20},{16,24},{20,28},{24,0},{28,4},{1,9},{5... | collective-permute-start | bytes 36872 | tf_op jit(solution)/shard_map/ppermute | solution.py:86
  5.3 6.8 %collective-permute-start.2 = (bf16[48,128]{1,0:T(8,128)(2,1)}, bf16[48,128]{1,0:T(8,128)(2,1)S(1)}, u32[]{:S(2)}, u32[]{:S(2)}) collective-permute-start(bf16[48,128]{1,0:T(8,128)(2,1)} %get-tuple-element.19), channel_id=1, source_target_pairs={{0,12},{4,16},{8,20},{12,24},{16,28},{20,0},{24,4},{28,8},{1,13},{... | collective-permute-start | bytes 36872 | tf_op jit(solution)/shard_map/ppermute | solution.py:86
  7.6 4.4 %collective-permute-start.3 = (bf16[48,128]{1,0:T(8,128)(2,1)}, bf16[48,128]{1,0:T(8,128)(2,1)S(1)}, u32[]{:S(2)}, u32[]{:S(2)}) collective-permute-start(bf16[48,128]{1,0:T(8,128)(2,1)} %get-tuple-element.20), channel_id=1, source_target_pairs={{0,16},{4,20},{8,24},{12,28},{16,0},{20,4},{24,8},{28,12},{1,17},{... | collective-permute-start | bytes 36872 | tf_op jit(solution)/shard_map/ppermute | solution.py:86
  8.1 3.9 %collective-permute-start.4 = (bf16[48,128]{1,0:T(8,128)(2,1)}, bf16[48,128]{1,0:T(8,128)(2,1)S(1)}, u32[]{:S(2)}, u32[]{:S(2)}) collective-permute-start(bf16[48,128]{1,0:T(8,128)(2,1)} %get-tuple-element.21), channel_id=1, source_target_pairs={{0,20},{4,24},{8,28},{12,0},{16,4},{20,8},{24,12},{28,16},{1,21},{... | collective-permute-start | bytes 36872 | tf_op jit(solution)/shard_map/ppermute | solution.py:86
  8.2 5.2 %copy-start.4 = (bf16[48,128]{1,0:T(8,128)(2,1)}, bf16[48,128]{1,0:T(8,128)(2,1)S(1)}, u32[]{:S(2)}) copy-start(bf16[48,128]{1,0:T(8,128)(2,1)S(1)} %collective-permute-done.refs_1_) | copy-start | bytes 36868
  8.3 3.9 %collective-permute-start.5 = (bf16[48,128]{1,0:T(8,128)(2,1)}, bf16[48,128]{1,0:T(8,128)(2,1)S(1)}, u32[]{:S(2)}, u32[]{:S(2)}) collective-permute-start(bf16[48,128]{1,0:T(8,128)(2,1)} %get-tuple-element.22), channel_id=1, source_target_pairs={{0,24},{4,28},{8,0},{12,4},{16,8},{20,12},{24,16},{28,20},{1,25},{... | collective-permute-start | bytes 36872 | tf_op jit(solution)/shard_map/ppermute | solution.py:86
  9.7 3.8 %copy-start.5 = (bf16[48,128]{1,0:T(8,128)(2,1)}, bf16[48,128]{1,0:T(8,128)(2,1)S(1)}, u32[]{:S(2)}) copy-start(bf16[48,128]{1,0:T(8,128)(2,1)S(1)} %collective-permute-done.1.refs_2_) | copy-start | bytes 36868
  9.7 3.8 %collective-permute-start.6 = (bf16[48,128]{1,0:T(8,128)(2,1)S(1)}, bf16[48,128]{1,0:T(8,128)(2,1)S(1)}, u32[]{:S(2)}, u32[]{:S(2)}) collective-permute-start(bf16[48,128]{1,0:T(8,128)(2,1)S(1)} %copy-done.11), channel_id=1, source_target_pairs={{0,28},{4,0},{8,4},{12,8},{16,12},{20,16},{24,20},{28,24},{1,29},{... | collective-permute-start | bytes 36872 | tf_op jit(solution)/shard_map/ppermute | solution.py:86
  12.0 1.4 %copy-start.6 = (bf16[48,128]{1,0:T(8,128)(2,1)}, bf16[48,128]{1,0:T(8,128)(2,1)S(1)}, u32[]{:S(2)}) copy-start(bf16[48,128]{1,0:T(8,128)(2,1)S(1)} %collective-permute-done.2.refs_3_) | copy-start | bytes 36868
  12.1 1.4 %copy-start.7 = (bf16[48,128]{1,0:T(8,128)(2,1)}, bf16[48,128]{1,0:T(8,128)(2,1)S(1)}, u32[]{:S(2)}) copy-start(bf16[48,128]{1,0:T(8,128)(2,1)S(1)} %collective-permute-done.3.refs_4_) | copy-start | bytes 36868
  12.1 1.4 %copy-start.8 = (bf16[48,128]{1,0:T(8,128)(2,1)}, bf16[48,128]{1,0:T(8,128)(2,1)S(1)}, u32[]{:S(2)}) copy-start(bf16[48,128]{1,0:T(8,128)(2,1)S(1)} %collective-permute-done.4.refs_5_) | copy-start | bytes 36868
  12.2 1.3 %copy-start.9 = (bf16[48,128]{1,0:T(8,128)(2,1)}, bf16[48,128]{1,0:T(8,128)(2,1)S(1)}, u32[]{:S(2)}) copy-start(bf16[48,128]{1,0:T(8,128)(2,1)S(1)} %collective-permute-done.5.refs_6_) | copy-start | bytes 36868
  13.4 0.6 %copy-start.10 = (bf16[48,128]{1,0:T(8,128)(2,1)}, bf16[48,128]{1,0:T(8,128)(2,1)S(1)}, u32[]{:S(2)}) copy-start(bf16[48,128]{1,0:T(8,128)(2,1)S(1)} %collective-permute-done.6.refs_7_) | copy-start | bytes 36868
  16.5 5.8 %collective-permute-start.9 = (bf16[4,32,128]{2,1,0:T(8,128)(2,1)}, bf16[4,32,128]{2,1,0:T(8,128)(2,1)S(1)}, u32[]{:S(2)}, u32[]{:S(2)}) collective-permute-start(bf16[4,32,128]{2,1,0:T(8,128)(2,1)} %get-tuple-element.26.refs_0_), channel_id=1, source_target_pairs={{0,3},{1,0},{2,1},{3,2},{4,7},{5,4},{6,5},{7,6},{8,11},{9,8},{10,9... | collective-permute-start | bytes 98312 | tf_op jit(solution)/shard_map/ppermute | solution.py:86
  20.1 5.0 %collective-permute-start.8 = (bf16[4,32,128]{2,1,0:T(8,128)(2,1)}, bf16[4,32,128]{2,1,0:T(8,128)(2,1)S(1)}, u32[]{:S(2)}, u32[]{:S(2)}) collective-permute-start(bf16[4,32,128]{2,1,0:T(8,128)(2,1)} %get-tuple-element.26.refs_0_), channel_id=1, source_target_pairs={{0,2},{1,3},{2,0},{3,1},{4,6},{5,7},{6,4},{7,5},{8,10},{9,11},{10,... | collective-permute-start | bytes 98312 | tf_op jit(solution)/shard_map/ppermute | solution.py:86
  20.1 5.9 %collective-permute-start.7 = (bf16[4,32,128]{2,1,0:T(8,128)(2,1)}, bf16[4,32,128]{2,1,0:T(8,128)(2,1)S(1)}, u32[]{:S(2)}, u32[]{:S(2)}) collective-permute-start(bf16[4,32,128]{2,1,0:T(8,128)(2,1)} %get-tuple-element.26.refs_0_), channel_id=1, source_target_pairs={{0,1},{1,2},{2,3},{3,0},{4,5},{5,6},{6,7},{7,4},{8,9},{9,10},{10,1... | collective-permute-start | bytes 98312 | tf_op jit(solution)/shard_map/ppermute | solution.py:86
  26.1 0.7 %copy-start.2 = (s32[4]{0:T(128)S(1)}, s32[4]{0:T(128)}, u32[]{:S(2)}) copy-start(s32[4]{0:T(128)} %get-tuple-element.24.column) | copy-start | bytes 52
  26.1 0.7 %copy-start.3 = (s32[4]{0:T(128)S(1)}, s32[4]{0:T(128)}, u32[]{:S(2)}) copy-start(s32[4]{0:T(128)} %get-tuple-element.25.place) | copy-start | bytes 52
  26.8 1.2 %copy-start = (bf16[512,1024]{1,0:T(8,128)(2,1)S(1)}, bf16[512,1024]{1,0:T(8,128)(2,1)}, u32[]{:S(2)}) copy-start(bf16[512,1024]{1,0:T(8,128)(2,1)} %amp_ref.1) | copy-start | bytes 3145732
  28.0 0.8 %copy-start.1 = (bf16[4,32,128]{2,1,0:T(8,128)(2,1)S(1)}, bf16[4,32,128]{2,1,0:T(8,128)(2,1)}, u32[]{:S(2)}) copy-start(bf16[4,32,128]{2,1,0:T(8,128)(2,1)} %get-tuple-element.26.refs_0_) | copy-start | bytes 98308

commit v3 on v1

v3 whole, which is shorter than its diff:
```python
import functools

import jax
import jax.numpy as jnp
from jax import lax
from jax.experimental import pallas as pl
from jax.experimental.pallas import tpu as pltpu
from jax.sharding import PartitionSpec as P

META = 8
GROUP = 4


def pack_kernel(own_count, hbm_in, hbm_counts, hbm_out, hbm_map, hbm_rows, send_ref, *scratch):
    in_tile, counts, out_tile, owner_map, rows, sems = scratch
    pairs = [
        (hbm_out, out_tile),
        (hbm_map, owner_map),
        (hbm_counts, counts),
        (hbm_in, in_tile),
        (hbm_rows, rows),
    ]
    copies = [
        pltpu.make_async_copy(source, target, sems.at[i])
        for i, (source, target) in enumerate(pairs)
    ]
    for copy in copies:
        copy.start()
    slot_count, row_count, width = rows.shape
    wide_count, depth_count = send_ref.shape[:2]
    if slot_count != wide_count:
        send_ref[...] = jnp.zeros_like(send_ref)
    for copy in copies:
        copy.wait()

    def place(h, _):
        spot = owner_map[out_tile[h]]
        owner = lax.div(spot, own_count)
        label = in_tile[h] * own_count + lax.rem(spot, own_count) + 1
        label = jnp.where(h < counts[0], label, 0).astype(jnp.float32)
        block = rows[h].astype(jnp.float32)
        meta = jnp.full((META, width), label, jnp.float32)
        message = jnp.concatenate([block, meta], axis=0).astype(send_ref.dtype)
        for z in range(depth_count):
            send_ref[owner, z] = message
        return 0

    lax.fori_loop(0, slot_count, place, 0, unroll=slot_count <= 8)


def ladder_kernel(rows, own_count, amp_ref, got_ref, out_hbm, out, picked, tiles, column, sems):
    wide_count, depth_count, _, width = got_ref.shape
    padded = got_ref.shape[2] - META
    recv_count = column.shape[0]
    tiles[...] = jnp.zeros_like(tiles)
    for u in range(recv_count):
        column[u] = 0

    def list_live(w, found):
        meta = got_ref[w, 0].astype(jnp.float32)[padded:]
        label = jnp.max(meta).astype(jnp.int32)

        @pl.when((label > 0) & (found < recv_count))
        def _():
            column[found] = lax.div(label - 1, own_count)
            spot = pl.multiple_of(lax.rem(label - 1, own_count) * width, width)
            if rows % 16 == 0:
                tile = got_ref[w][:, :rows]
            else:
                tile = got_ref[w].astype(jnp.float32)[:, :rows]
            tile = tile.reshape(depth_count * rows, width).astype(tiles.dtype)
            at = pl.multiple_of(found * width, width)
            tiles[pl.ds(at, width), pl.ds(spot, width)] = tile

        return found + (label > 0).astype(jnp.int32)

    lax.fori_loop(0, wide_count, list_live, jnp.int32(0), unroll=wide_count <= 8)
    row_count = amp_ref.shape[0]
    chunk_count = sems.shape[0]
    chunk = row_count // chunk_count
    copies = []
    for c in range(chunk_count):
        part = pl.ds(c * chunk, chunk)
        total = None
        for first in range(0, recv_count, GROUP):
            size = min(GROUP, recv_count - first)
            for u in range(size):
                at = pl.multiple_of(column[first + u] * width, width)
                picked[:, u * width : (u + 1) * width] = amp_ref[part, pl.ds(at, width)]
            term = jnp.dot(
                picked[:, : size * width],
                tiles[first * width : (first + size) * width],
                preferred_element_type=jnp.float32,
            )
            total = term if total is None else total + term
        out[part] = total
        copy = pltpu.make_async_copy(out.at[part], out_hbm.at[part], sems.at[c])
        copy.start()
        copies.append(copy)
    for copy in copies:
        copy.wait()


def shards(amplitudes, integrals, in_tile, counts, out_tile, owner_map):
    slot_count, rows, width = integrals.shape
    row_count = amplitudes.shape[0]
    wide_count = lax.axis_size("wide")
    depth_count = lax.axis_size("narrow")
    own_count = owner_map.shape[0] // wide_count
    recv_count = slot_count // 2
    kind = integrals.dtype
    whole = pl.BlockSpec(memory_space=pl.ANY)
    vmem = pl.BlockSpec(memory_space=pltpu.VMEM)
    send = pl.pallas_call(
        functools.partial(pack_kernel, own_count),
        out_shape=jax.ShapeDtypeStruct((wide_count, depth_count, rows + META, width), kind),
        in_specs=[whole] * 5,
        out_specs=vmem,
        scratch_shapes=[
            pltpu.SMEM(in_tile.shape, jnp.int32),
            pltpu.SMEM(counts.shape, jnp.int32),
            pltpu.SMEM(out_tile.shape, jnp.int32),
            pltpu.SMEM(owner_map.shape, jnp.int32),
            pltpu.VMEM(integrals.shape, kind),
            pltpu.SemaphoreType.DMA((5,)),
        ],
        compiler_params=pltpu.CompilerParams(vmem_limit_bytes=40 * 2**20),
        name="pack",
    )(in_tile, counts, out_tile, owner_map, integrals)
    got = lax.all_to_all(
        send.reshape(wide_count * depth_count, rows + META, width),
        ("wide", "narrow"),
        split_axis=0,
        concat_axis=0,
        tiled=True,
    ).reshape(wide_count, depth_count, rows + META, width)
    chunk_count = 4 if row_count % 64 == 0 else 1
    return pl.pallas_call(
        functools.partial(ladder_kernel, rows, own_count),
        out_shape=jax.ShapeDtypeStruct((row_count, own_count * width), jnp.float32),
        in_specs=[vmem, vmem],
        out_specs=whole,
        scratch_shapes=[
            pltpu.VMEM((row_count, own_count * width), jnp.float32),
            pltpu.VMEM((row_count // chunk_count, min(GROUP, recv_count) * width), kind),
            pltpu.VMEM((recv_count * width, own_count * width), kind),
            pltpu.SMEM((recv_count,), jnp.int32),
            pltpu.SemaphoreType.DMA((chunk_count,)),
        ],
        compiler_params=pltpu.CompilerParams(vmem_limit_bytes=32 * 2**20),
        name="ladder",
    )(amplitudes, got)


def solution(mesh):
    return jax.shard_map(
        shards,
        mesh=mesh,
        in_specs=(
            P("narrow", None),
            P("wide", "narrow", None),
            P("wide"),
            P("wide"),
            P("wide"),
            P(),
        ),
        out_specs=P("narrow", "wide"),
        check_vma=False,
    )
```

time: 24.2 us -> 25 us (1.033)
  local copies, waits for them, and re-layouts: 0.01 us -> 2.8 us
  blocking collectives: 19.9 us -> 18.5 us
  Pallas kernels: 3.35 us -> 2.81 us
    unnamed x2 -> x10, local copies, waits for them, and re-layouts: 0.01 us -> 2.8 us
    all_to_all x1, blocking collectives: 19.9 us -> 18.5 us  [shards(): lax.all_to_all(send.reshape(wide_count * depth_count, rows + META, width)...]
    pallas_call x1, Pallas kernels: 1.67 us -> 0.66 us  [shards(): pl.pallas_call(functools.partial(pack_kernel, own_count), out_shape=jax.S...]
    pallas_call x1, Pallas kernels: 1.68 us -> 2.15 us  [shards(): pl.pallas_call(functools.partial(ladder_kernel, rows, own_count), out_sha...]
where the time goes in v3:
time: 25 us; the launch traced here: 24.8 us
  blocking collectives  18.5 us (74%)
  Pallas kernels  2.81 us (11%)
  local copies, waits for them, and re-layouts  2.8 us (11%)
  between operations  0.76 us (3%)
    all_to_all x1, blocking collectives, shards(): lax.all_to_all(send.reshape(wide_count * depth_count, rows + META, width)...  18.5 us
    unnamed x10, local copies, waits for them, and re-layouts  2.8 us
    pallas_call x1, Pallas kernels, shards(): pl.pallas_call(functools.partial(ladder_kernel, rows, own_count), out_sha...  2.15 us
    pallas_call x1, Pallas kernels, shards(): pl.pallas_call(functools.partial(pack_kernel, own_count), out_shape=jax.S...  0.66 us

profile of v3, /device:TPU:1, one launch (start us, length us, event | category | flops | bytes accessed | tf_op | source)
XLA Modules:
  0.0 24.8 jit_solution(11891614600605481596)
XLA Ops:
  0.0 0.0 copy-start
  0.7 0.0 copy-start.1
  0.8 0.8 %copy-done.1 = bf16[8,32,128]{2,1,0:T(8,128)(2,1)S(1)} copy-done((bf16[8,32,128]{2,1,0:T(8,128)(2,1)S(1)}, bf16[8,32,128]{2,1,0:T(8,128)(2,1)}, u32[]{:S(2)}) %copy-start.1) | copy-done | bytes 65560
  1.6 0.0 copy-start.2
  1.6 0.7 %copy-done.2 = s32[8]{0:T(128)S(1)} copy-done((s32[8]{0:T(128)S(1)}, s32[8]{0:T(128)}, u32[]{:S(2)}) %copy-start.2) | copy-done | bytes 56
  2.2 0.0 copy-start.3
  2.2 0.7 %copy-done.3 = s32[8]{0:T(128)S(1)} copy-done((s32[8]{0:T(128)S(1)}, s32[8]{0:T(128)}, u32[]{:S(2)}) %copy-start.3) | copy-done | bytes 56
  2.9 0.0 copy-start.4
  2.9 0.7 %copy-done.4 = s32[16]{0:T(128)S(1)} copy-done((s32[16]{0:T(128)S(1)}, s32[16]{0:T(128)}, u32[]{:S(2)}) %copy-start.4) | copy-done | bytes 88
  3.6 0.7 %pack.1 = bf16[8,4,40,128]{3,2,1,0:T(8,128)(2,1)S(1)} custom-call(s32[8]{0:T(128)S(1)} %copy-done.2, s32[1]{0:T(128)S(6)} %copy.7.hbm_counts, s32[8]{0:T(128)S(1)} %copy-done.3, s32[16]{0:T(128)S(1)} %copy-done.4, bf16[8,32,128]{2,1,0:T(8,128)(2,1)S(1)} %copy-done.1), custom_call_target="tpu_custom_call" | custom-call | tf_op jit(solution)/shard_map/pack/pallas_call | solution.py:114
  4.2 18.5 %all_to_all.5 = bf16[32,40,128]{2,1,0:T(8,128)(2,1)S(1)} all-to-all(bf16[32,40,128]{2,1,0:T(8,128)(2,1)S(1)} %bitcast.2), channel_id=1, replica_groups=mesh['wide'=8,'narrow'=4] {'wide','narrow'}, dimensions={0} | all-to-all | bytes 655360 | tf_op jit(solution)/shard_map/all_to_all | solution.py:130
  22.7 0.0 copy-done
  22.7 2.1 %ladder.1 = f32[512,256]{1,0:T(8,128)} custom-call(bf16[512,1024]{1,0:T(8,128)(2,1)S(1)} %copy-done, bf16[8,4,40,128]{3,2,1,0:T(8,128)(2,1)S(1)} %bitcast.3), custom_call_target="tpu_custom_call" | custom-call | tf_op jit(solution)/shard_map/ladder/pallas_call | solution.py:138
Async XLA Ops:
  0.0 22.7 %copy-start = (bf16[512,1024]{1,0:T(8,128)(2,1)S(1)}, bf16[512,1024]{1,0:T(8,128)(2,1)}, u32[]{:S(2)}) copy-start(bf16[512,1024]{1,0:T(8,128)(2,1)} %amp_ref.1) | copy-start | bytes 3145732
  0.7 0.8 %copy-start.1 = (bf16[8,32,128]{2,1,0:T(8,128)(2,1)S(1)}, bf16[8,32,128]{2,1,0:T(8,128)(2,1)}, u32[]{:S(2)}) copy-start(bf16[8,32,128]{2,1,0:T(8,128)(2,1)} %hbm_rows.1) | copy-start | bytes 196612
  1.6 0.7 %copy-start.2 = (s32[8]{0:T(128)S(1)}, s32[8]{0:T(128)}, u32[]{:S(2)}) copy-start(s32[8]{0:T(128)} %hbm_in.1) | copy-start | bytes 100
  2.2 0.7 %copy-start.3 = (s32[8]{0:T(128)S(1)}, s32[8]{0:T(128)}, u32[]{:S(2)}) copy-start(s32[8]{0:T(128)} %hbm_out.1) | copy-start | bytes 100
  2.9 0.7 %copy-start.4 = (s32[16]{0:T(128)S(1)}, s32[16]{0:T(128)}, u32[]{:S(2)}) copy-start(s32[16]{0:T(128)} %hbm_map.1) | copy-start | bytes 196

commit v4 on v1

v4 whole, which is shorter than its diff:
```python
import functools

import jax
import jax.numpy as jnp
from jax import lax
from jax.experimental import pallas as pl
from jax.experimental.pallas import tpu as pltpu
from jax.sharding import PartitionSpec as P

GROUP = 4


def pack_kernel(
    own_count,
    in_tile,
    out_tile,
    owner_map,
    counts_ref,
    rows_ref,
    amp_hbm,
    send_ref,
    label_ref,
    amp_ref,
    sem,
):
    fetch = pltpu.make_async_copy(amp_hbm, amp_ref, sem)
    fetch.start()
    slot_count = rows_ref.shape[0]
    wide_count, depth_count, _, width = send_ref.shape
    if slot_count != wide_count:
        send_ref[...] = jnp.zeros_like(send_ref)
    count = jnp.broadcast_to(counts_ref[...].reshape(1, 1), (wide_count, width))
    owners = lax.broadcasted_iota(jnp.int32, (wide_count, width), 0)

    def place(h, labels):
        spot = owner_map[out_tile[h]]
        owner = lax.div(spot, own_count)
        label = in_tile[h] * own_count + lax.rem(spot, own_count) + 1
        block = rows_ref[h]
        for z in range(depth_count):
            send_ref[owner, z] = block
        return jnp.where((owners == owner) & (h < count), label, labels)

    labels = jnp.zeros((wide_count, width), jnp.int32)
    labels = lax.fori_loop(0, slot_count, place, labels, unroll=slot_count <= 8)
    label_ref[...] = labels.astype(jnp.float32).astype(label_ref.dtype)
    fetch.wait()


def ladder_kernel(rows, own_count, recv_count, label_ref, amp_ref, got_ref, out_ref, tiles, column, seen):
    wide_count, depth_count, _, width = got_ref.shape
    me = lax.axis_index("wide")
    mine = lax.broadcasted_iota(jnp.int32, (wide_count, width), 0) == me
    tiles[...] = jnp.zeros_like(tiles)
    for u in range(recv_count):
        column[u] = 0

    def read_label(w):
        home = label_ref[pl.ds(pl.multiple_of(w * wide_count, wide_count), wide_count)]
        return jnp.max(jnp.where(mine, home.astype(jnp.float32), 0.0)).astype(jnp.int32)

    def keep(w, label, found):
        live = jnp.minimum(label, 1)
        at = jnp.minimum(found, recv_count)
        code = jnp.maximum(label - 1, 0)
        column[at] = lax.div(code, own_count)
        spot = lax.rem(code, own_count)
        if rows % 16 == 0:
            tile = got_ref[w]
        else:
            tile = got_ref[w].astype(jnp.float32)
        tile = tile.reshape(depth_count * rows, width).astype(tiles.dtype)
        at = pl.multiple_of(at * width, width)
        for q in range(own_count):
            kept = jnp.where((live > 0) & (spot == q), tile, jnp.zeros_like(tile))
            tiles[pl.ds(at, width), q * width : (q + 1) * width] = kept
        return found + live

    if wide_count <= 8:
        labels = [read_label(w) for w in range(wide_count)]
        found = jnp.int32(0)
        for w in range(wide_count):
            found = keep(w, labels[w], found)
    else:

        def note(w, _):
            seen[w] = read_label(w)
            return 0

        lax.fori_loop(0, wide_count, note, 0)
        lax.fori_loop(0, wide_count, lambda w, found: keep(w, seen[w], found), jnp.int32(0))
    total = None
    for first in range(0, recv_count, GROUP):
        last = min(first + GROUP, recv_count)
        spots = [pl.multiple_of(column[u] * width, width) for u in range(first, last)]
        picked = jnp.concatenate([amp_ref[:, pl.ds(spot, width)] for spot in spots], axis=1)
        term = jnp.dot(
            picked, tiles[first * width : last * width], preferred_element_type=jnp.float32
        )
        total = term if total is None else total + term
    out_ref[...] = total


def shards(amplitudes, integrals, in_tile, counts, out_tile, owner_map):
    slot_count, rows, width = integrals.shape
    row_count = amplitudes.shape[0]
    wide_count = lax.axis_size("wide")
    depth_count = lax.axis_size("narrow")
    own_count = owner_map.shape[0] // wide_count
    recv_count = slot_count // 2
    kind = integrals.dtype
    smem = pl.BlockSpec(memory_space=pltpu.SMEM)
    vmem = pl.BlockSpec(memory_space=pltpu.VMEM)
    send, labels, near = pl.pallas_call(
        functools.partial(pack_kernel, own_count),
        out_shape=[
            jax.ShapeDtypeStruct((wide_count, depth_count, rows, width), kind),
            jax.ShapeDtypeStruct((wide_count, width), kind),
            jax.ShapeDtypeStruct(amplitudes.shape, amplitudes.dtype),
        ],
        in_specs=[smem] * 3 + [vmem] * 2 + [pl.BlockSpec(memory_space=pl.ANY)],
        out_specs=[vmem] * 3,
        scratch_shapes=[pltpu.SemaphoreType.DMA],
        name="pack",
    )(in_tile, out_tile, owner_map, counts, integrals, amplitudes)
    labels = lax.all_gather(labels, "wide", axis=0, tiled=True)
    got = lax.all_to_all(
        send.reshape(wide_count * depth_count, rows, width),
        ("wide", "narrow"),
        split_axis=0,
        concat_axis=0,
        tiled=True,
    ).reshape(wide_count, depth_count, rows, width)
    return pl.pallas_call(
        functools.partial(ladder_kernel, rows, own_count, recv_count),
        out_shape=jax.ShapeDtypeStruct((row_count, own_count * width), jnp.float32),
        in_specs=[vmem] * 3,
        out_specs=vmem,
        scratch_shapes=[
            pltpu.VMEM(((recv_count + 1) * width, own_count * width), kind),
            pltpu.SMEM((recv_count + 1,), jnp.int32),
            pltpu.SMEM((wide_count,), jnp.int32),
        ],
        compiler_params=pltpu.CompilerParams(vmem_limit_bytes=32 * 2**20),
        name="ladder",
    )(labels, near, got)


def solution(mesh):
    return jax.shard_map(
        shards,
        mesh=mesh,
        in_specs=(
            P("narrow", None),
            P("wide", "narrow", None),
            P("wide"),
            P("wide"),
            P("wide"),
            P(),
        ),
        out_specs=P("narrow", "wide"),
        check_vma=False,
    )
```

time: 24.2 us -> 24.2 us (level)
  the two profiles are of different devices: /device:TPU:1 before, /device:TPU:0 now
where the time goes in v4:
time: 24.2 us; the launch traced here: 23.9 us
  blocking collectives  9.2 us (38%)
  starting transfers between devices  7.3 us (30%)
  Pallas kernels  4.48 us (19%)
  local copies, waits for them, and re-layouts  1.23 us (5%)
  waiting for transfers between devices  0.99 us (4%)
  between operations  0.69 us (3%)
    all_gather x1, blocking collectives, shards(): labels = lax.all_gather(labels, 'wide', axis=0, tiled=True)  9.2 us
    all_to_all x1, starting transfers between devices, shards(): lax.all_to_all(send.reshape(wide_count * depth_count, rows, width), ('wid...  7.3 us
    pallas_call x1, Pallas kernels, shards(): pl.pallas_call(functools.partial(pack_kernel, own_count), out_shape=[jax....  3.14 us
    pallas_call x1, Pallas kernels, shards(): pl.pallas_call(functools.partial(ladder_kernel, rows, own_count, recv_cou...  1.34 us
    unnamed x4, local copies, waits for them, and re-layouts  1.23 us
    all_to_all x1, waiting for transfers between devices, shards(): lax.all_to_all(send.reshape(wide_count * depth_count, rows, width), ('wid...  0.99 us
  transfers between devices with their start and end apart: 1, of which 1 were waited for; matrix products, arithmetic and copies ran while one was open for 0% of the time, Pallas kernels for 0%

profile of v4, /device:TPU:0, one launch (start us, length us, event | category | flops | bytes accessed | tf_op | source)
XLA Modules:
  0.0 23.9 jit_solution(15058828377847374689)
XLA Ops:
  0.7 3.1 %pack.1 = (bf16[8,4,32,128]{3,2,1,0:T(8,128)(2,1)}, bf16[8,128]{1,0:T(8,128)(2,1)}, bf16[512,1024]{1,0:T(8,128)(2,1)}) custom-call(s32[8]{0:T(128)} %in_tile.1, s32[8]{0:T(128)} %out_tile.1, s32[16]{0:T(128)} %owner_map.1, s32[1]{0:T(128)S(6)} %copy.7.counts_ref, bf16[8,32,128]{2,1,0:T(8,128)(2,1)} %rows_ref.1, bf16[512,1024]{1,0:T(8,128)(2,1)} %amp_hbm.1), custom_call_target="tpu_custom_call" | custom-call | tf_op jit(solution)/shard_map/pack/pallas_call | solution.py:114
  3.8 0.0 copy-start.1
  3.8 7.3 %all-to-all-start = ((bf16[32,32,128]{2,1,0:T(8,128)(2,1)}), bf16[32,32,128]{2,1,0:T(8,128)(2,1)S(1)}, u32[]{:S(2)}, u32[]{:S(2)}) async-start(bf16[32,32,128]{2,1,0:T(8,128)(2,1)} %bitcast.3), calls=%async_computation | async-start | bytes 524288 | tf_op jit(solution)/shard_map/all_to_all | solution.py:127
  11.1 0.0 copy-done.1
  11.1 9.2 %all_gather.3.label_ref = bf16[64,128]{1,0:T(8,128)(2,1)S(1)} all-gather(bf16[8,128]{1,0:T(8,128)(2,1)S(1)} %copy-done.1), channel_id=1, replica_groups=mesh['wide'=8,'narrow'=4] {'wide'}, dimensions={0}, use_global_device_ids=true | all-gather | bytes 18432 | tf_op jit(solution)/shard_map/all_gather | solution.py:126
  20.3 1.0 %all-to-all-done = bf16[32,32,128]{2,1,0:T(8,128)(2,1)S(1)} async-done(((bf16[32,32,128]{2,1,0:T(8,128)(2,1)}), bf16[32,32,128]{2,1,0:T(8,128)(2,1)S(1)}, u32[]{:S(2)}, u32[]{:S(2)}) %all-to-all-start) | async-done | bytes 262176 | tf_op jit(solution)/shard_map/all_to_all | solution.py:127
  21.3 0.0 copy-start
  21.3 1.2 %copy-done = bf16[512,1024]{1,0:T(8,128)(2,1)S(1)} copy-done((bf16[512,1024]{1,0:T(8,128)(2,1)S(1)}, bf16[512,1024]{1,0:T(8,128)(2,1)}, u32[]{:S(2)}) %copy-start) | copy-done | bytes 1048600
  22.5 1.3 %ladder.1 = f32[512,256]{1,0:T(8,128)} custom-call(bf16[64,128]{1,0:T(8,128)(2,1)S(1)} %all_gather.3.label_ref, bf16[512,1024]{1,0:T(8,128)(2,1)S(1)} %copy-done, bf16[8,4,32,128]{3,2,1,0:T(8,128)(2,1)S(1)} %bitcast.2), custom_call_target="tpu_custom_call" | custom-call | tf_op jit(solution)/shard_map/ladder/pallas_call | solution.py:134
Async XLA Ops:
  3.8 7.3 %copy-start.1 = (bf16[8,128]{1,0:T(8,128)(2,1)S(1)}, bf16[8,128]{1,0:T(8,128)(2,1)}, u32[]{:S(2)}) copy-start(bf16[8,128]{1,0:T(8,128)(2,1)} %get-tuple-element.8) | copy-start | bytes 6148
  3.8 17.5 %all-to-all-start = ((bf16[32,32,128]{2,1,0:T(8,128)(2,1)}), bf16[32,32,128]{2,1,0:T(8,128)(2,1)S(1)}, u32[]{:S(2)}, u32[]{:S(2)}) async-start(bf16[32,32,128]{2,1,0:T(8,128)(2,1)} %bitcast.3), calls=%async_computation | async-start | bytes 524288 | tf_op jit(solution)/shard_map/all_to_all | solution.py:127
  21.3 1.2 %copy-start = (bf16[512,1024]{1,0:T(8,128)(2,1)S(1)}, bf16[512,1024]{1,0:T(8,128)(2,1)}, u32[]{:S(2)}) copy-start(bf16[512,1024]{1,0:T(8,128)(2,1)} %get-tuple-element.9.amp_ref) | copy-start | bytes 3145732

commit v5 on v4

v5 whole, which is shorter than its diff:
```python
import functools

import jax
import jax.numpy as jnp
from jax import lax
from jax.experimental import pallas as pl
from jax.experimental.pallas import tpu as pltpu
from jax.sharding import PartitionSpec as P

META = 8
GROUP = 4


def pack_kernel(
    own_count, in_tile, counts, out_tile, owner_map, rows_ref, far_ref, send_ref
):
    slot_count, _, width = rows_ref.shape
    wide_count, near_count = send_ref.shape[:2]
    if slot_count != wide_count:
        send_ref[...] = jnp.zeros_like(send_ref)
    upper = lax.axis_index("narrow") >= near_count

    def place(h, _):
        spot = owner_map[out_tile[h]]
        owner = lax.div(spot, own_count)
        label = in_tile[h] * own_count + lax.rem(spot, own_count) + 1
        label = jnp.where(h < counts[0], label, 0).astype(jnp.float32)
        mine = rows_ref[h].astype(jnp.float32)
        far = far_ref[h].astype(jnp.float32)
        message = [
            jnp.where(upper, far, mine),
            jnp.where(upper, mine, far),
            jnp.full((META, width), label, jnp.float32),
        ]
        message = jnp.concatenate(message, axis=0).astype(send_ref.dtype)
        for z in range(near_count):
            send_ref[owner, z] = message
        return 0

    lax.fori_loop(0, slot_count, place, 0, unroll=slot_count <= 8)


def ladder_kernel(
    rows, own_count, recv_count, amp_hbm, got_ref, out_ref, amp_ref, tiles, column, seen, sem
):
    fetch = pltpu.make_async_copy(amp_hbm, amp_ref, sem)
    fetch.start()
    wide_count, near_count, _, width = got_ref.shape
    tiles[...] = jnp.zeros_like(tiles)
    for u in range(recv_count):
        column[u] = 0

    def read_label(w):
        meta = got_ref[w, 0].astype(jnp.float32)[2 * rows :]
        return jnp.max(meta).astype(jnp.int32)

    def keep(w, label, found):
        live = jnp.minimum(label, 1)
        at = jnp.minimum(found, recv_count)
        code = jnp.maximum(label - 1, 0)
        column[at] = lax.div(code, own_count)
        spot = lax.rem(code, own_count)
        message = got_ref[w]
        if rows % 16 != 0:
            message = message.astype(jnp.float32)
        halves = [message[:, :rows], message[:, rows : 2 * rows]]
        halves = [half.reshape(near_count * rows, width) for half in halves]
        tile = jnp.concatenate(halves, axis=0).astype(tiles.dtype)
        at = pl.multiple_of(at * width, width)
        for q in range(own_count):
            kept = jnp.where((live > 0) & (spot == q), tile, jnp.zeros_like(tile))
            tiles[pl.ds(at, width), q * width : (q + 1) * width] = kept
        return found + live

    if wide_count <= 8:
        labels = [read_label(w) for w in range(wide_count)]
        found = jnp.int32(0)
        for w in range(wide_count):
            found = keep(w, labels[w], found)
    else:

        def note(w, _):
            seen[w] = read_label(w)
            return 0

        lax.fori_loop(0, wide_count, note, 0)
        lax.fori_loop(0, wide_count, lambda w, found: keep(w, seen[w], found), jnp.int32(0))
    fetch.wait()
    total = None
    for first in range(0, recv_count, GROUP):
        last = min(first + GROUP, recv_count)
        spots = [pl.multiple_of(column[u] * width, width) for u in range(first, last)]
        picked = jnp.concatenate([amp_ref[:, pl.ds(spot, width)] for spot in spots], axis=1)
        term = jnp.dot(
            picked, tiles[first * width : last * width], preferred_element_type=jnp.float32
        )
        total = term if total is None else total + term
    out_ref[...] = total


def shards(amplitudes, integrals, in_tile, counts, out_tile, owner_map):
    slot_count, rows, width = integrals.shape
    row_count = amplitudes.shape[0]
    wide_count = lax.axis_size("wide")
    depth_count = lax.axis_size("narrow")
    near_count = depth_count // 2
    own_count = owner_map.shape[0] // wide_count
    recv_count = slot_count // 2
    kind = integrals.dtype
    length = 2 * rows + META
    smem = pl.BlockSpec(memory_space=pltpu.SMEM)
    vmem = pl.BlockSpec(memory_space=pltpu.VMEM)
    across = [(z, (z + near_count) % depth_count) for z in range(depth_count)]
    far = lax.ppermute(integrals, "narrow", across)
    send = pl.pallas_call(
        functools.partial(pack_kernel, own_count),
        out_shape=jax.ShapeDtypeStruct((wide_count, near_count, length, width), kind),
        in_specs=[smem] * 4 + [vmem] * 2,
        out_specs=vmem,
        name="pack",
    )(in_tile, counts, out_tile, owner_map, integrals, far)
    groups = [
        [w * depth_count + half * near_count + z for w in range(wide_count) for z in range(near_count)]
        for half in range(2)
    ]
    got = lax.all_to_all(
        send.reshape(wide_count * near_count, length, width),
        ("wide", "narrow"),
        split_axis=0,
        concat_axis=0,
        tiled=True,
        axis_index_groups=groups,
    ).reshape(wide_count, near_count, length, width)
    return pl.pallas_call(
        functools.partial(ladder_kernel, rows, own_count, recv_count),
        out_shape=jax.ShapeDtypeStruct((row_count, own_count * width), jnp.float32),
        in_specs=[pl.BlockSpec(memory_space=pl.ANY), vmem],
        out_specs=vmem,
        scratch_shapes=[
            pltpu.VMEM(amplitudes.shape, amplitudes.dtype),
            pltpu.VMEM(((recv_count + 1) * width, own_count * width), kind),
            pltpu.SMEM((recv_count + 1,), jnp.int32),
            pltpu.SMEM((wide_count,), jnp.int32),
            pltpu.SemaphoreType.DMA,
        ],
        name="ladder",
    )(amplitudes, got)


def solution(mesh):
    return jax.shard_map(
        shards,
        mesh=mesh,
        in_specs=(
            P("narrow", None),
            P("wide", "narrow", None),
            P("wide"),
            P("wide"),
            P("wide"),
            P(),
        ),
        out_specs=P("narrow", "wide"),
        check_vma=False,
    )
```

time: 24.2 us -> 24.9 us (1.029)
  starting transfers between devices: 7.3 us -> 4.04 us
  waiting for transfers between devices: 0.99 us -> 3.21 us
  blocking collectives: 9.2 us -> 10.9 us
  Pallas kernels: 4.48 us -> 5.13 us
  local copies, waits for them, and re-layouts: 1.23 us -> 0.61 us
    all_to_all x0 -> x1, blocking collectives: none -> 10.9 us  [shards(): lax.all_to_all(send.reshape(wide_count * near_count, length, width), ('wi...]
    all_gather x1 -> x0, blocking collectives: 9.2 us -> none  [shards(): labels = lax.all_gather(labels, 'wide', axis=0, tiled=True)]
    all_to_all x1 -> x0, starting transfers between devices: 7.3 us -> none  [shards(): lax.all_to_all(send.reshape(wide_count * depth_count, rows, width), ('wid...]
    ppermute x0 -> x1, starting transfers between devices: none -> 4.04 us  [shards(): far = lax.ppermute(integrals, 'narrow', across)]
    ppermute x0 -> x1, waiting for transfers between devices: none -> 3.21 us  [shards(): far = lax.ppermute(integrals, 'narrow', across)]
    pallas_call x1, Pallas kernels: 1.34 us -> 3.49 us  [shards(): pl.pallas_call(functools.partial(ladder_kernel, rows, own_count, recv_cou...]
    pallas_call x1, Pallas kernels: 3.14 us -> 1.64 us  [shards(): pl.pallas_call(functools.partial(pack_kernel, own_count), out_shape=jax.S...]
    all_to_all x1 -> x0, waiting for transfers between devices: 0.99 us -> none  [shards(): lax.all_to_all(send.reshape(wide_count * depth_count, rows, width), ('wid...]
where the time goes in v5:
time: 24.9 us; the launch traced here: 24.6 us
  blocking collectives  10.9 us (44%)
  Pallas kernels  5.13 us (21%)
  starting transfers between devices  4.04 us (16%)
  waiting for transfers between devices  3.21 us (13%)
  between operations  0.66 us (3%)
  local copies, waits for them, and re-layouts  0.61 us (2%)
    all_to_all x1, blocking collectives, shards(): lax.all_to_all(send.reshape(wide_count * near_count, length, width), ('wi...  10.9 us
    ppermute x1, starting transfers between devices, shards(): far = lax.ppermute(integrals, 'narrow', across)  4.04 us
    pallas_call x1, Pallas kernels, shards(): pl.pallas_call(functools.partial(ladder_kernel, rows, own_count, recv_cou...  3.49 us
    ppermute x1, waiting for transfers between devices, shards(): far = lax.ppermute(integrals, 'narrow', across)  3.21 us
    pallas_call x1, Pallas kernels, shards(): pl.pallas_call(functools.partial(pack_kernel, own_count), out_shape=jax.S...  1.64 us
    unnamed x2, local copies, waits for them, and re-layouts  0.61 us
  transfers between devices with their start and end apart: 1, of which 1 were waited for; matrix products, arithmetic and copies ran while one was open for 0% of the time, Pallas kernels for 0%

profile of v5, /device:TPU:0, one launch (start us, length us, event | category | flops | bytes accessed | tf_op | source)
XLA Modules:
  0.0 24.6 jit_solution(10135677401041686795)
XLA Ops:
  0.0 4.0 %collective-permute-start = (bf16[8,32,128]{2,1,0:T(8,128)(2,1)}, bf16[8,32,128]{2,1,0:T(8,128)(2,1)S(1)}, u32[]{:S(2)}, u32[]{:S(2)}) collective-permute-start(bf16[8,32,128]{2,1,0:T(8,128)(2,1)} %rows_ref.1), channel_id=1, source_target_pairs={{0,2},{1,3},{2,0},{3,1},{4,6},{5,7},{6,4},{7,5},{8,10},{9,11},{10,... | collective-permute-start | bytes 196616 | tf_op jit(solution)/shard_map/ppermute | solution.py:114
  4.7 3.2 %collective-permute-done.far_ref = bf16[8,32,128]{2,1,0:T(8,128)(2,1)S(1)} collective-permute-done((bf16[8,32,128]{2,1,0:T(8,128)(2,1)}, bf16[8,32,128]{2,1,0:T(8,128)(2,1)S(1)}, u32[]{:S(2)}, u32[]{:S(2)}) %collective-permute-start) | collective-permute-done | bytes 65568 | tf_op jit(solution)/shard_map/ppermute | solution.py:114
  7.9 0.0 copy-start
  7.9 0.6 %copy-done = bf16[8,32,128]{2,1,0:T(8,128)(2,1)} copy-done((bf16[8,32,128]{2,1,0:T(8,128)(2,1)}, bf16[8,32,128]{2,1,0:T(8,128)(2,1)S(1)}, u32[]{:S(2)}) %copy-start) | copy-done | bytes 65560
  8.5 1.6 %pack.1 = bf16[8,2,72,128]{3,2,1,0:T(8,128)(2,1)} custom-call(s32[8]{0:T(128)} %in_tile.1, s32[1]{0:T(128)S(6)} %copy.7.counts, s32[8]{0:T(128)} %out_tile.1, s32[16]{0:T(128)} %owner_map.1, bf16[8,32,128]{2,1,0:T(8,128)(2,1)} %rows_ref.1, bf16[8,32,128]{2,1,0:T(8,128)(2,1)} %copy-done), custom_call_target="tpu_custom_call" | custom-call | tf_op jit(solution)/shard_map/pack/pallas_call | solution.py:115
  10.2 10.9 %all_to_all.5 = bf16[16,72,128]{2,1,0:T(8,128)(2,1)} all-to-all(bf16[16,72,128]{2,1,0:T(8,128)(2,1)} %bitcast.3), channel_id=1, replica_groups={{0,1,4,5,8,9,12,13,16,17,20,21,24,25,28,29},{2,3,6,7,10,11,14,15,18,19,..., dimensions={0} | all-to-all | bytes 589824 | tf_op jit(solution)/shard_map/all_to_all | solution.py:126
  21.1 3.5 %ladder.1 = f32[512,256]{1,0:T(8,128)} custom-call(bf16[512,1024]{1,0:T(8,128)(2,1)} %amp_hbm.1, bf16[8,2,72,128]{3,2,1,0:T(8,128)(2,1)} %bitcast.2), custom_call_target="tpu_custom_call" | custom-call | tf_op jit(solution)/shard_map/ladder/pallas_call | solution.py:134
Async XLA Ops:
  0.0 7.9 %collective-permute-start = (bf16[8,32,128]{2,1,0:T(8,128)(2,1)}, bf16[8,32,128]{2,1,0:T(8,128)(2,1)S(1)}, u32[]{:S(2)}, u32[]{:S(2)}) collective-permute-start(bf16[8,32,128]{2,1,0:T(8,128)(2,1)} %rows_ref.1), channel_id=1, source_target_pairs={{0,2},{1,3},{2,0},{3,1},{4,6},{5,7},{6,4},{7,5},{8,10},{9,11},{10,... | collective-permute-start | bytes 196616 | tf_op jit(solution)/shard_map/ppermute | solution.py:114
  7.9 0.6 %copy-start = (bf16[8,32,128]{2,1,0:T(8,128)(2,1)}, bf16[8,32,128]{2,1,0:T(8,128)(2,1)S(1)}, u32[]{:S(2)}) copy-start(bf16[8,32,128]{2,1,0:T(8,128)(2,1)S(1)} %collective-permute-done.far_ref) | copy-start | bytes 196612

commit v6 on v5

v6 whole, which is shorter than its diff:
```python
import functools

import jax
import jax.numpy as jnp
from jax import lax
from jax.experimental import pallas as pl
from jax.experimental.pallas import tpu as pltpu
from jax.sharding import PartitionSpec as P

PAIR = 2
GROUP = 4
UNROLL = 8


def each(count, body, start):
    if count > UNROLL:
        return lax.fori_loop(0, count, body, start)
    for i in range(count):
        start = body(i, start)
    return start


def message_at(index, length):
    start = index * length
    if not isinstance(index, int):
        start = pl.multiple_of(start, length)
    return start


def pack_kernel(own_count, depth_count, in_tile, counts, out_tile, owner_map, rows_ref, send_ref, slot, code):
    slot_count, rows, width = rows_ref.shape
    wide_count = slot.shape[0]
    length = send_ref.shape[0] // (wide_count * depth_count)
    for owner in range(wide_count):
        slot[owner] = 0
        code[owner] = 0

    def route(h, _):
        spot = owner_map[out_tile[h]]
        owner = lax.div(spot, own_count)
        label = in_tile[h] * own_count + lax.rem(spot, own_count) + 1
        slot[owner] = h
        code[owner] = jnp.where(h < counts[0], label, 0)
        return 0

    each(slot_count, route, 0)

    def write(owner, _):
        block = rows_ref[slot[owner]]
        label = jnp.full((length - rows, width), code[owner].astype(jnp.float32), jnp.float32)
        if length % 16 == 0:
            message = jnp.concatenate([block.astype(jnp.float32), label], axis=0)
            pieces = [(0, message.astype(send_ref.dtype))]
        else:
            pieces = [(0, block), (rows, label.astype(send_ref.dtype))]
        for z in range(depth_count):
            start = message_at(owner * depth_count + z, length)
            for offset, piece in pieces:
                send_ref[pl.ds(start + offset, piece.shape[0])] = piece
        return 0

    each(wide_count, write, 0)


def ladder_kernel(
    rows, depth_count, own_count, recv_count, amp_ref, got_ref, out_ref, tiles, column, seen
):
    wide_count = seen.shape[0]
    width = got_ref.shape[1]
    length = got_ref.shape[0] // (wide_count * depth_count)
    tiles[...] = jnp.zeros_like(tiles)
    for u in range(recv_count):
        column[u] = 0

    def message(w, z):
        start = message_at(w * depth_count + z, length)
        if length % 16 == 0:
            return got_ref[pl.ds(start, length)].astype(jnp.float32)[:rows]
        return got_ref[pl.ds(start, rows)]

    def read_label(w):
        start = message_at(w * depth_count, length)
        if length % 16 == 0:
            label = got_ref[pl.ds(start, length)].astype(jnp.float32)[rows:]
        else:
            label = got_ref[pl.ds(start + rows, length - rows)].astype(jnp.float32)
        return jnp.max(label).astype(jnp.int32)

    def keep(w, label, found):
        live = jnp.minimum(label, 1)
        at = jnp.minimum(found, recv_count)
        place = jnp.maximum(label - 1, 0)
        column[at] = lax.div(place, own_count)
        spot = lax.rem(place, own_count)
        tile = jnp.concatenate([message(w, z) for z in range(depth_count)], axis=0)
        tile = tile.astype(tiles.dtype)
        at = pl.multiple_of(at * width, width)
        for q in range(own_count):
            kept = jnp.where((live > 0) & (spot == q), tile, jnp.zeros_like(tile))
            tiles[pl.ds(at, width), q * width : (q + 1) * width] = kept
        return found + live

    if wide_count <= UNROLL:
        labels = [read_label(w) for w in range(wide_count)]
        found = jnp.int32(0)
        for w in range(wide_count):
            found = keep(w, labels[w], found)
    else:

        def note(w, _):
            seen[w] = read_label(w)
            return 0

        lax.fori_loop(0, wide_count, note, 0)
        lax.fori_loop(0, wide_count, lambda w, found: keep(w, seen[w], found), jnp.int32(0))
    total = None
    for first in range(0, recv_count, GROUP):
        last = min(first + GROUP, recv_count)
        spots = [pl.multiple_of(column[u] * width, width) for u in range(first, last)]
        picked = jnp.concatenate([amp_ref[:, pl.ds(spot, width)] for spot in spots], axis=1)
        term = jnp.dot(
            picked, tiles[first * width : last * width], preferred_element_type=jnp.float32
        )
        total = term if total is None else total + term
    out_ref[...] = total


def shards(amplitudes, integrals, in_tile, counts, out_tile, owner_map):
    slot_count, rows, width = integrals.shape
    row_count = amplitudes.shape[0]
    wide_count = lax.axis_size("wide")
    depth_count = lax.axis_size("narrow")
    own_count = owner_map.shape[0] // wide_count
    recv_count = slot_count // 2
    kind = integrals.dtype
    message_count = wide_count * depth_count
    length = rows + PAIR
    if wide_count > UNROLL or rows % PAIR != 0 or message_count * length % 16 != 0:
        length = -(-length // 16) * 16
    smem = pl.BlockSpec(memory_space=pltpu.SMEM)
    vmem = pl.BlockSpec(memory_space=pltpu.VMEM)
    send = pl.pallas_call(
        functools.partial(pack_kernel, own_count, depth_count),
        out_shape=jax.ShapeDtypeStruct((message_count * length, width), kind),
        in_specs=[smem] * 4 + [vmem],
        out_specs=vmem,
        scratch_shapes=[pltpu.SMEM((wide_count,), jnp.int32)] * 2,
        name="pack",
    )(in_tile, counts, out_tile, owner_map, integrals)
    got = lax.all_to_all(
        send.reshape(message_count, length // PAIR, PAIR, width),
        ("wide", "narrow"),
        split_axis=0,
        concat_axis=0,
        tiled=True,
    ).reshape(message_count * length, width)
    return pl.pallas_call(
        functools.partial(ladder_kernel, rows, depth_count, own_count, recv_count),
        out_shape=jax.ShapeDtypeStruct((row_count, own_count * width), jnp.float32),
        in_specs=[vmem] * 2,
        out_specs=vmem,
        scratch_shapes=[
            pltpu.VMEM(((recv_count + 1) * width, own_count * width), kind),
            pltpu.SMEM((recv_count + 1,), jnp.int32),
            pltpu.SMEM((wide_count,), jnp.int32),
        ],
        compiler_params=pltpu.CompilerParams(vmem_limit_bytes=32 * 2**20),
        name="ladder",
    )(amplitudes, got)


def solution(mesh):
    return jax.shard_map(
        shards,
        mesh=mesh,
        in_specs=(
            P("narrow", None),
            P("wide", "narrow", None),
            P("wide"),
            P("wide"),
            P("wide"),
            P(),
        ),
        out_specs=P("narrow", "wide"),
        check_vma=False,
    )
```

time: 24.9 us -> 22.9 us (0.920)
  blocking collectives: 10.9 us -> 17.7 us
  starting transfers between devices: 4.04 us -> 0 us
  waiting for transfers between devices: 3.21 us -> 0 us
  Pallas kernels: 5.13 us -> 3 us
  local copies, waits for them, and re-layouts: 0.61 us -> 1.22 us
    all_to_all x1, blocking collectives: 10.9 us -> 17.7 us  [shards(): lax.all_to_all(send.reshape(message_count, length // PAIR, PAIR, width),...]
    ppermute x1 -> x0, starting transfers between devices: 4.04 us -> none  [shards(): far = lax.ppermute(integrals, 'narrow', across)]
    ppermute x1 -> x0, waiting for transfers between devices: 3.21 us -> none  [shards(): far = lax.ppermute(integrals, 'narrow', across)]
    pallas_call x2, Pallas kernels: 5.13 us -> 3 us  [the longest x1 1.68 us: shards(): pl.pallas_call(functools.partial(pack_kernel, own_count, depth_count), ou...]
    unnamed x2, local copies, waits for them, and re-layouts: 0.61 us -> 1.22 us
  transfers between devices with their start and end apart: 1 -> 0, of which waited for: 1 -> 0; matrix products, arithmetic and copies ran while one was open for 0% -> 0% of each run, Pallas kernels for 0% -> 0%
where the time goes in v6:
time: 22.9 us; the launch traced here: 22.6 us
  blocking collectives  17.7 us (77%)
  Pallas kernels  3 us (13%)
  local copies, waits for them, and re-layouts  1.22 us (5%)
  between operations  0.65 us (3%)
    all_to_all x1, blocking collectives, shards(): lax.all_to_all(send.reshape(message_count, length // PAIR, PAIR, width),...  17.7 us
    pallas_call x1, Pallas kernels, shards(): pl.pallas_call(functools.partial(pack_kernel, own_count, depth_count), ou...  1.68 us
    pallas_call x1, Pallas kernels, shards(): pl.pallas_call(functools.partial(ladder_kernel, rows, depth_count, own_co...  1.32 us
    unnamed x2, local copies, waits for them, and re-layouts  1.22 us

profile of v6, /device:TPU:0, one launch (start us, length us, event | category | flops | bytes accessed | tf_op | source)
XLA Modules:
  0.0 22.6 jit_solution(5100836471264433789)
XLA Ops:
  0.7 1.7 %pack.1 = bf16[1088,128]{1,0:T(8,128)(2,1)} custom-call(s32[8]{0:T(128)} %in_tile.1, s32[1]{0:T(128)S(6)} %copy.7.counts, s32[8]{0:T(128)} %out_tile.1, s32[16]{0:T(128)} %owner_map.1, bf16[8,32,128]{2,1,0:T(8,128)(2,1)} %rows_ref.1), custom_call_target="tpu_custom_call" | custom-call | tf_op jit(solution)/shard_map/pack/pallas_call | solution.py:142
  2.3 17.7 %all_to_all.5 = bf16[32,17,2,128]{3,2,1,0:T(2,128)(2,1)S(1)} all-to-all(bf16[32,17,2,128]{3,2,1,0:T(2,128)(2,1)} %bitcast.3), channel_id=1, replica_groups=mesh['wide'=8,'narrow'=4] {'wide','narrow'}, dimensions={0} | all-to-all | bytes 557056 | tf_op jit(solution)/shard_map/all_to_all | solution.py:150
  20.1 0.0 copy-start
  20.1 1.2 %copy-done = bf16[512,1024]{1,0:T(8,128)(2,1)S(1)} copy-done((bf16[512,1024]{1,0:T(8,128)(2,1)S(1)}, bf16[512,1024]{1,0:T(8,128)(2,1)}, u32[]{:S(2)}) %copy-start) | copy-done | bytes 1048600
  21.3 1.3 %ladder.1 = f32[512,256]{1,0:T(8,128)} custom-call(bf16[512,1024]{1,0:T(8,128)(2,1)S(1)} %copy-done, bf16[1088,128]{1,0:T(8,128)(2,1)S(1)} %bitcast.2), custom_call_target="tpu_custom_call" | custom-call | tf_op jit(solution)/shard_map/ladder/pallas_call | solution.py:157
Async XLA Ops:
  20.1 1.2 %copy-start = (bf16[512,1024]{1,0:T(8,128)(2,1)S(1)}, bf16[512,1024]{1,0:T(8,128)(2,1)}, u32[]{:S(2)}) copy-start(bf16[512,1024]{1,0:T(8,128)(2,1)} %amp_ref.1) | copy-start | bytes 3145732

commit v7 on v6

--- a/solution.py
+++ b/solution.py
@@ -27,13 +27,23 @@
     return start
 
 
-def pack_kernel(own_count, depth_count, in_tile, counts, out_tile, owner_map, rows_ref, send_ref, slot, code):
+def pack_kernel(own_count, depth_count, *refs):
+    sources, send_ref, targets, (slot, code, sems) = refs[:5], refs[5], refs[6:11], refs[11:]
+    in_tile, counts, out_tile, owner_map, rows_ref = targets
+    copies = [
+        pltpu.make_async_copy(source, target, sems.at[i])
+        for i, (source, target) in enumerate(zip(sources, targets))
+    ]
+    for copy in copies:
+        copy.start()
     slot_count, rows, width = rows_ref.shape
     wide_count = slot.shape[0]
     length = send_ref.shape[0] // (wide_count * depth_count)
     for owner in range(wide_count):
         slot[owner] = 0
         code[owner] = 0
+    for copy in copies:
+        copy.wait()
 
     def route(h, _):
         spot = owner_map[out_tile[h]]
@@ -137,16 +147,26 @@
     length = rows + PAIR
     if wide_count > UNROLL or rows % PAIR != 0 or message_count * length % 16 != 0:
         length = -(-length // 16) * 16
-    smem = pl.BlockSpec(memory_space=pltpu.SMEM)
+    hbm = pl.BlockSpec(memory_space=pltpu.HBM)
     vmem = pl.BlockSpec(memory_space=pltpu.VMEM)
+    given = [in_tile, counts, out_tile, owner_map, integrals]
+    given = [
+        value if value.size == 1 else pltpu.with_memory_space_constraint(value, pltpu.HBM)
+        for value in given
+    ]
     send = pl.pallas_call(
         functools.partial(pack_kernel, own_count, depth_count),
         out_shape=jax.ShapeDtypeStruct((message_count * length, width), kind),
-        in_specs=[smem] * 4 + [vmem],
+        in_specs=[hbm] * len(given),
         out_specs=vmem,
-        scratch_shapes=[pltpu.SMEM((wide_count,), jnp.int32)] * 2,
+        scratch_shapes=[pltpu.SMEM(value.shape, value.dtype) for value in given[:-1]]
+        + [pltpu.VMEM(integrals.shape, kind)]
+        + [pltpu.SMEM((wide_count,), jnp.int32)] * 2
+        + [pltpu.SemaphoreType.DMA((len(given),))],
+        compiler_params=pltpu.CompilerParams(vmem_limit_bytes=32 * 2**20),
+        cost_estimate=pl.CostEstimate(flops=2**30, bytes_accessed=2**20, transcendentals=0),
         name="pack",
-    )(in_tile, counts, out_tile, owner_map, integrals)
+    )(*given)
     got = lax.all_to_all(
         send.reshape(message_count, length // PAIR, PAIR, width),
         ("wide", "narrow"),

time: 22.9 us -> 20.8 us (0.908)
  local copies, waits for them, and re-layouts: 1.22 us -> 0.01 us
  Pallas kernels: 3 us -> 2.36 us
    unnamed x2, local copies, waits for them, and re-layouts: 1.22 us -> 0.01 us
    pallas_call x1, Pallas kernels: 1.68 us -> 1.04 us  [shards(): pl.pallas_call(functools.partial(pack_kernel, own_count, depth_count), ou...]
where the time goes in v7:
time: 20.8 us; the launch traced here: 20.6 us
  blocking collectives  17.5 us (84%)
  Pallas kernels  2.36 us (11%)
  between operations  0.67 us (3%)
    all_to_all x1, blocking collectives, shards(): lax.all_to_all(send.reshape(message_count, length // PAIR, PAIR, width),...  17.5 us
    pallas_call x1, Pallas kernels, shards(): pl.pallas_call(functools.partial(ladder_kernel, rows, depth_count, own_co...  1.32 us
    pallas_call x1, Pallas kernels, shards(): pl.pallas_call(functools.partial(pack_kernel, own_count, depth_count), ou...  1.04 us

profile of v7, /device:TPU:0, one launch (start us, length us, event | category | flops | bytes accessed | tf_op | source)
XLA Modules:
  0.0 20.6 jit_solution(13925004296664708550)
XLA Ops:
  0.7 0.0 copy-start
  0.7 1.0 %pack.1 = bf16[1088,128]{1,0:T(8,128)(2,1)S(1)} custom-call(s32[8]{0:T(128)} %refs_0_.1, s32[1]{0:T(128)S(6)} %copy.7.refs_1_, s32[8]{0:T(128)} %refs_2_.1, s32[16]{0:T(128)} %refs_3_.1, bf16[8,32,128]{2,1,0:T(8,128)(2,1)} %refs_4_.1), custom_call_target="tpu_custom_call" | custom-call | flops 1073741824 | bytes 1048576 | tf_op jit(solution)/shard_map/pack/pallas_call | solution.py:157
  1.7 17.5 %all_to_all.5 = bf16[32,17,2,128]{3,2,1,0:T(2,128)(2,1)S(1)} all-to-all(bf16[32,17,2,128]{3,2,1,0:T(2,128)(2,1)S(1)} %bitcast.3), channel_id=1, replica_groups=mesh['wide'=8,'narrow'=4] {'wide','narrow'}, dimensions={0} | all-to-all | bytes 557056 | tf_op jit(solution)/shard_map/all_to_all | solution.py:170
  19.2 0.0 copy-done
  19.2 1.3 %ladder.1 = f32[512,256]{1,0:T(8,128)} custom-call(bf16[512,1024]{1,0:T(8,128)(2,1)S(1)} %copy-done, bf16[1088,128]{1,0:T(8,128)(2,1)S(1)} %bitcast.2), custom_call_target="tpu_custom_call" | custom-call | tf_op jit(solution)/shard_map/ladder/pallas_call | solution.py:177
Async XLA Ops:
  0.7 18.6 %copy-start = (bf16[512,1024]{1,0:T(8,128)(2,1)S(1)}, bf16[512,1024]{1,0:T(8,128)(2,1)}, u32[]{:S(2)}) copy-start(bf16[512,1024]{1,0:T(8,128)(2,1)} %amp_ref.1) | copy-start | bytes 3145732

commit v8 on v7

--- a/solution.py
+++ b/solution.py
@@ -70,6 +70,12 @@
         return 0
 
     each(wide_count, write, 0)
+
+
+def fetch_kernel(source, target, sem):
+    copy = pltpu.make_async_copy(source, target, sem)
+    copy.start()
+    copy.wait()
 
 
 def ladder_kernel(
@@ -164,7 +170,6 @@
         + [pltpu.SMEM((wide_count,), jnp.int32)] * 2
         + [pltpu.SemaphoreType.DMA((len(given),))],
         compiler_params=pltpu.CompilerParams(vmem_limit_bytes=32 * 2**20),
-        cost_estimate=pl.CostEstimate(flops=2**30, bytes_accessed=2**20, transcendentals=0),
         name="pack",
     )(*given)
     got = lax.all_to_all(
@@ -174,6 +179,16 @@
         concat_axis=0,
         tiled=True,
     ).reshape(message_count * length, width)
+    near = pl.pallas_call(
+        fetch_kernel,
+        out_shape=jax.ShapeDtypeStruct(amplitudes.shape, amplitudes.dtype),
+        in_specs=[hbm],
+        out_specs=vmem,
+        scratch_shapes=[pltpu.SemaphoreType.DMA],
+        compiler_params=pltpu.CompilerParams(vmem_limit_bytes=32 * 2**20),
+        cost_estimate=pl.CostEstimate(flops=2**30, bytes_accessed=2**21, transcendentals=0),
+        name="fetch",
+    )(pltpu.with_memory_space_constraint(amplitudes, pltpu.HBM))
     return pl.pallas_call(
         functools.partial(ladder_kernel, rows, depth_count, own_count, recv_count),
         out_shape=jax.ShapeDtypeStruct((row_count, own_count * width), jnp.float32),
@@ -186,7 +201,7 @@
         ],
         compiler_params=pltpu.CompilerParams(vmem_limit_bytes=32 * 2**20),
         name="ladder",
-    )(amplitudes, got)
+    )(near, got)
 
 
 def solution(mesh):

time: 20.8 us -> 21.7 us (1.043)
  blocking collectives: 17.5 us -> 0 us
  waiting for transfers between devices: 0 us -> 9.18 us
  starting transfers between devices: 0 us -> 7.3 us
  Pallas kernels: 2.36 us -> 4.22 us
    all_to_all x1 -> x0, blocking collectives: 17.5 us -> none  [shards(): lax.all_to_all(send.reshape(message_count, length // PAIR, PAIR, width),...]
    all_to_all x0 -> x1, waiting for transfers between devices: none -> 9.18 us  [shards(): lax.all_to_all(send.reshape(message_count, length // PAIR, PAIR, width),...]
    all_to_all x0 -> x1, starting transfers between devices: none -> 7.3 us  [shards(): lax.all_to_all(send.reshape(message_count, length // PAIR, PAIR, width),...]
    pallas_call x0 -> x1, Pallas kernels: none -> 1.24 us  [shards(): pl.pallas_call(fetch_kernel, out_shape=jax.ShapeDtypeStruct(amplitudes.sh...]
    pallas_call x1, Pallas kernels: 1.04 us -> 1.66 us  [shards(): pl.pallas_call(functools.partial(pack_kernel, own_count, depth_count), ou...]
  transfers between devices with their start and end apart: 0 -> 1, of which waited for: 0 -> 1; matrix products, arithmetic and copies ran while one was open for 0% -> 0% of each run, Pallas kernels for 0% -> 6%
where the time goes in v8:
time: 21.7 us; the launch traced here: 21.4 us
  waiting for transfers between devices  9.18 us (42%)
  starting transfers between devices  7.3 us (34%)
  Pallas kernels  4.22 us (19%)
  between operations  0.68 us (3%)
    all_to_all x1, waiting for transfers between devices, shards(): lax.all_to_all(send.reshape(message_count, length // PAIR, PAIR, width),...  9.18 us
    all_to_all x1, starting transfers between devices, shards(): lax.all_to_all(send.reshape(message_count, length // PAIR, PAIR, width),...  7.3 us
    pallas_call x1, Pallas kernels, shards(): pl.pallas_call(functools.partial(pack_kernel, own_count, depth_count), ou...  1.66 us
    pallas_call x1, Pallas kernels, shards(): pl.pallas_call(functools.partial(ladder_kernel, rows, depth_count, own_co...  1.32 us
    pallas_call x1, Pallas kernels, shards(): pl.pallas_call(fetch_kernel, out_shape=jax.ShapeDtypeStruct(amplitudes.sh...  1.24 us
  transfers between devices with their start and end apart: 1, of which 1 were waited for; matrix products, arithmetic and copies ran while one was open for 0% of the time, Pallas kernels for 6%

profile of v8, /device:TPU:0, one launch (start us, length us, event | category | flops | bytes accessed | tf_op | source)
XLA Modules:
  0.0 21.4 jit_solution(16871174013037488452)
XLA Ops:
  0.7 1.7 %pack.1 = bf16[1088,128]{1,0:T(8,128)(2,1)} custom-call(s32[8]{0:T(128)} %refs_0_.1, s32[1]{0:T(128)S(6)} %copy.7.refs_1_, s32[8]{0:T(128)} %refs_2_.1, s32[16]{0:T(128)} %refs_3_.1, bf16[8,32,128]{2,1,0:T(8,128)(2,1)} %refs_4_.1), custom_call_target="tpu_custom_call" | custom-call | tf_op jit(solution)/shard_map/pack/pallas_call | solution.py:163
  2.3 7.3 %all-to-all-start = ((bf16[32,17,2,128]{3,2,1,0:T(2,128)(2,1)}), bf16[32,17,2,128]{3,2,1,0:T(2,128)(2,1)S(1)}, u32[]{:S(2)}, u32[]{:S(2)}) async-start(bf16[32,17,2,128]{3,2,1,0:T(2,128)(2,1)} %bitcast), calls=%async_computation | async-start | bytes 557056 | tf_op jit(solution)/shard_map/all_to_all | solution.py:175
  9.6 1.2 %fetch.1.amp_ref = bf16[512,1024]{1,0:T(8,128)(2,1)S(1)} custom-call(bf16[512,1024]{1,0:T(8,128)(2,1)} %source.1), custom_call_target="tpu_custom_call" | custom-call | flops 1073741824 | bytes 2097152 | tf_op jit(solution)/shard_map/fetch/pallas_call | solution.py:182
  10.9 9.2 %all-to-all-done = bf16[32,17,2,128]{3,2,1,0:T(2,128)(2,1)S(1)} async-done(((bf16[32,17,2,128]{3,2,1,0:T(2,128)(2,1)}), bf16[32,17,2,128]{3,2,1,0:T(2,128)(2,1)S(1)}, u32[]{:S(2)}, u32[]{:S(2)}) %all-to-all-start) | async-done | bytes 278560 | tf_op jit(solution)/shard_map/all_to_all | solution.py:175
  20.1 1.3 %ladder.1 = f32[512,256]{1,0:T(8,128)} custom-call(bf16[512,1024]{1,0:T(8,128)(2,1)S(1)} %fetch.1.amp_ref, bf16[1088,128]{1,0:T(8,128)(2,1)S(1)} %bitcast.2), custom_call_target="tpu_custom_call" | custom-call | tf_op jit(solution)/shard_map/ladder/pallas_call | solution.py:192
Async XLA Ops:
  2.3 17.7 %all-to-all-start = ((bf16[32,17,2,128]{3,2,1,0:T(2,128)(2,1)}), bf16[32,17,2,128]{3,2,1,0:T(2,128)(2,1)S(1)}, u32[]{:S(2)}, u32[]{:S(2)}) async-start(bf16[32,17,2,128]{3,2,1,0:T(2,128)(2,1)} %bitcast), calls=%async_computation | async-start | bytes 557056 | tf_op jit(solution)/shard_map/all_to_all | solution.py:175

commit v9 on v7

--- a/solution.py
+++ b/solution.py
@@ -20,8 +20,8 @@
     return start
 
 
-def message_at(index, length):
-    start = index * length
+def message_at(index, count, length):
+    start = (count - 1 - index) * length
     if not isinstance(index, int):
         start = pl.multiple_of(start, length)
     return start
@@ -64,7 +64,7 @@
         else:
             pieces = [(0, block), (rows, label.astype(send_ref.dtype))]
         for z in range(depth_count):
-            start = message_at(owner * depth_count + z, length)
+            start = message_at(owner * depth_count + z, wide_count * depth_count, length)
             for offset, piece in pieces:
                 send_ref[pl.ds(start + offset, piece.shape[0])] = piece
         return 0
@@ -83,13 +83,13 @@
         column[u] = 0
 
     def message(w, z):
-        start = message_at(w * depth_count + z, length)
+        start = message_at(w * depth_count + z, wide_count * depth_count, length)
         if length % 16 == 0:
             return got_ref[pl.ds(start, length)].astype(jnp.float32)[:rows]
         return got_ref[pl.ds(start, rows)]
 
     def read_label(w):
-        start = message_at(w * depth_count, length)
+        start = message_at(w * depth_count, wide_count * depth_count, length)
         if length % 16 == 0:
             label = got_ref[pl.ds(start, length)].astype(jnp.float32)[rows:]
         else:
@@ -173,6 +173,7 @@
         split_axis=0,
         concat_axis=0,
         tiled=True,
+        axis_index_groups=[list(reversed(range(message_count)))],
     ).reshape(message_count * length, width)
     return pl.pallas_call(
         functools.partial(ladder_kernel, rows, depth_count, own_count, recv_count),

time: 20.8 us -> 21.8 us (1.048)
  blocking collectives: 17.5 us -> 18.6 us
    all_to_all x1, blocking collectives: 17.5 us -> 18.6 us  [shards(): lax.all_to_all(send.reshape(message_count, length // PAIR, PAIR, width),...]
where the time goes in v9:
time: 21.8 us; the launch traced here: 21.6 us
  blocking collectives  18.6 us (85%)
  Pallas kernels  2.36 us (11%)
  between operations  0.67 us (3%)
    all_to_all x1, blocking collectives, shards(): lax.all_to_all(send.reshape(message_count, length // PAIR, PAIR, width),...  18.6 us
    pallas_call x1, Pallas kernels, shards(): pl.pallas_call(functools.partial(ladder_kernel, rows, depth_count, own_co...  1.32 us
    pallas_call x1, Pallas kernels, shards(): pl.pallas_call(functools.partial(pack_kernel, own_count, depth_count), ou...  1.04 us

profile of v9, /device:TPU:0, one launch (start us, length us, event | category | flops | bytes accessed | tf_op | source)
XLA Modules:
  0.0 21.6 jit_solution(13020002043490677576)
XLA Ops:
  0.7 0.0 copy-start
  0.7 1.0 %pack.1 = bf16[1088,128]{1,0:T(8,128)(2,1)S(1)} custom-call(s32[8]{0:T(128)} %refs_0_.1, s32[1]{0:T(128)S(6)} %copy.7.refs_1_, s32[8]{0:T(128)} %refs_2_.1, s32[16]{0:T(128)} %refs_3_.1, bf16[8,32,128]{2,1,0:T(8,128)(2,1)} %refs_4_.1), custom_call_target="tpu_custom_call" | custom-call | flops 1073741824 | bytes 1048576 | tf_op jit(solution)/shard_map/pack/pallas_call | solution.py:157
  1.7 18.6 %all_to_all.5 = bf16[32,17,2,128]{3,2,1,0:T(2,128)(2,1)S(1)} all-to-all(bf16[32,17,2,128]{3,2,1,0:T(2,128)(2,1)S(1)} %bitcast.3), channel_id=1, replica_groups={{31,30,29,28,27,26,25,24,23,22,21,20,19,18,17,16,15,14,13,12,11,10,9,8,..., dimensions={0} | all-to-all | bytes 557056 | tf_op jit(solution)/shard_map/all_to_all | solution.py:170
  20.3 0.0 copy-done
  20.3 1.3 %ladder.1 = f32[512,256]{1,0:T(8,128)} custom-call(bf16[512,1024]{1,0:T(8,128)(2,1)S(1)} %copy-done, bf16[1088,128]{1,0:T(8,128)(2,1)S(1)} %bitcast.2), custom_call_target="tpu_custom_call" | custom-call | tf_op jit(solution)/shard_map/ladder/pallas_call | solution.py:178
Async XLA Ops:
  0.7 19.6 %copy-start = (bf16[512,1024]{1,0:T(8,128)(2,1)S(1)}, bf16[512,1024]{1,0:T(8,128)(2,1)}, u32[]{:S(2)}) copy-start(bf16[512,1024]{1,0:T(8,128)(2,1)} %amp_ref.1) | copy-start | bytes 3145732

commit v10 on v7

--- a/solution.py
+++ b/solution.py
@@ -64,7 +64,7 @@
         else:
             pieces = [(0, block), (rows, label.astype(send_ref.dtype))]
         for z in range(depth_count):
-            start = message_at(owner * depth_count + z, length)
+            start = message_at(z * wide_count + owner, length)
             for offset, piece in pieces:
                 send_ref[pl.ds(start + offset, piece.shape[0])] = piece
         return 0
@@ -83,13 +83,13 @@
         column[u] = 0
 
     def message(w, z):
-        start = message_at(w * depth_count + z, length)
+        start = message_at(z * wide_count + w, length)
         if length % 16 == 0:
             return got_ref[pl.ds(start, length)].astype(jnp.float32)[:rows]
         return got_ref[pl.ds(start, rows)]
 
     def read_label(w):
-        start = message_at(w * depth_count, length)
+        start = message_at(w, length)
         if length % 16 == 0:
             label = got_ref[pl.ds(start, length)].astype(jnp.float32)[rows:]
         else:
@@ -169,7 +169,7 @@
     )(*given)
     got = lax.all_to_all(
         send.reshape(message_count, length // PAIR, PAIR, width),
-        ("wide", "narrow"),
+        ("narrow", "wide"),
         split_axis=0,
         concat_axis=0,
         tiled=True,

time: 20.8 us -> 21.4 us (1.029)
  blocking collectives: 17.5 us -> 18.2 us
    all_to_all x1, blocking collectives: 17.5 us -> 18.2 us  [shards(): lax.all_to_all(send.reshape(message_count, length // PAIR, PAIR, width),...]
where the time goes in v10:
time: 21.4 us; the launch traced here: 21.2 us
  blocking collectives  18.2 us (85%)
  Pallas kernels  2.35 us (11%)
  between operations  0.67 us (3%)
    all_to_all x1, blocking collectives, shards(): lax.all_to_all(send.reshape(message_count, length // PAIR, PAIR, width),...  18.2 us
    pallas_call x1, Pallas kernels, shards(): pl.pallas_call(functools.partial(ladder_kernel, rows, depth_count, own_co...  1.32 us
    pallas_call x1, Pallas kernels, shards(): pl.pallas_call(functools.partial(pack_kernel, own_count, depth_count), ou...  1.03 us

profile of v10, /device:TPU:0, one launch (start us, length us, event | category | flops | bytes accessed | tf_op | source)
XLA Modules:
  0.0 21.2 jit_solution(4596689496981952403)
XLA Ops:
  0.7 0.0 copy-start
  0.7 1.0 %pack.1 = bf16[1088,128]{1,0:T(8,128)(2,1)S(1)} custom-call(s32[8]{0:T(128)} %refs_0_.1, s32[1]{0:T(128)S(6)} %copy.7.refs_1_, s32[8]{0:T(128)} %refs_2_.1, s32[16]{0:T(128)} %refs_3_.1, bf16[8,32,128]{2,1,0:T(8,128)(2,1)} %refs_4_.1), custom_call_target="tpu_custom_call" | custom-call | flops 1073741824 | bytes 1048576 | tf_op jit(solution)/shard_map/pack/pallas_call | solution.py:157
  1.7 18.2 %all_to_all.5 = bf16[32,17,2,128]{3,2,1,0:T(2,128)(2,1)S(1)} all-to-all(bf16[32,17,2,128]{3,2,1,0:T(2,128)(2,1)S(1)} %bitcast.3), channel_id=1, replica_groups=mesh['wide'=8,'narrow'=4] {'narrow','wide'}, dimensions={0} | all-to-all | bytes 557056 | tf_op jit(solution)/shard_map/all_to_all | solution.py:170
  19.9 0.0 copy-done
  19.9 1.3 %ladder.1 = f32[512,256]{1,0:T(8,128)} custom-call(bf16[512,1024]{1,0:T(8,128)(2,1)S(1)} %copy-done, bf16[1088,128]{1,0:T(8,128)(2,1)S(1)} %bitcast.2), custom_call_target="tpu_custom_call" | custom-call | tf_op jit(solution)/shard_map/ladder/pallas_call | solution.py:177
Async XLA Ops:
  0.7 19.2 %copy-start = (bf16[512,1024]{1,0:T(8,128)(2,1)S(1)}, bf16[512,1024]{1,0:T(8,128)(2,1)}, u32[]{:S(2)}) copy-start(bf16[512,1024]{1,0:T(8,128)(2,1)} %amp_ref.1) | copy-start | bytes 3145732

commit v11 on v7

v11 whole, which is shorter than its diff:
```python
import functools

import jax
import jax.numpy as jnp
from jax import lax
from jax.experimental import pallas as pl
from jax.experimental.pallas import tpu as pltpu
from jax.sharding import PartitionSpec as P

PAIR = 2
GROUP = 4
UNROLL = 8


def each(count, body, start):
    if count > UNROLL:
        return lax.fori_loop(0, count, body, start)
    for i in range(count):
        start = body(i, start)
    return start


def message_at(index, length):
    start = index * length
    if not isinstance(index, int):
        start = pl.multiple_of(start, length)
    return start


def route_kernel(own_count, wide_count, *refs):
    sources, (order_ref, label_ref, near_ref), targets, sems = refs[:5], refs[5:8], refs[8:12], refs[12]
    in_tile, counts, out_tile, owner_map = targets
    copies = [
        pltpu.make_async_copy(source, target, sems.at[i])
        for i, (source, target) in enumerate(zip(sources, (*targets, near_ref)))
    ]
    for copy in copies:
        copy.start()
    for copy in copies[:4]:
        copy.wait()
    slot_count, rows, width = near_ref.shape
    column = lax.broadcasted_iota(jnp.int32, (1, slot_count * rows), 1)
    owners = lax.broadcasted_iota(jnp.int32, (wide_count, width), 0)

    def route(h, carry):
        owner_of, labels = carry
        spot = owner_map[out_tile[h]]
        owner = lax.div(spot, own_count)
        label = in_tile[h] * own_count + lax.rem(spot, own_count) + 1
        label = jnp.where(h < counts[0], label, 0)
        owner_of = jnp.where(lax.div(column, rows) == h, owner, owner_of)
        return owner_of, jnp.where(owners == owner, label, labels)

    start = (jnp.zeros_like(column), jnp.zeros((wide_count, width), jnp.int32))
    owner_of, labels = each(slot_count, route, start)
    label_ref[...] = labels.astype(jnp.float32).astype(label_ref.dtype)
    row = lax.broadcasted_iota(jnp.int32, (wide_count * rows, 1), 0)
    hit = row == owner_of * rows + lax.rem(column, rows)
    order_ref[...] = hit.astype(jnp.float32).astype(order_ref.dtype)
    copies[4].wait()


def pack_kernel(wide_count, near_count, order_ref, label_ref, near_ref, far_ref, send_ref, both, ordered):
    slot_count, rows, width = near_ref.shape
    length = send_ref.shape[0] // (wide_count * near_count)
    for side, ref in enumerate((near_ref, far_ref)):
        block = ref[...]
        if rows % 16 != 0:
            block = block.astype(jnp.float32)
        block = block.reshape(slot_count * rows, width).astype(both.dtype)
        both[:, side * width : (side + 1) * width] = block
    ordered[...] = jnp.dot(order_ref[...], both[...], preferred_element_type=jnp.float32)
    labels = label_ref[...].astype(jnp.float32)
    ids = lax.broadcasted_iota(jnp.int32, labels.shape, 0)

    def write(owner, _):
        spot = owner * rows
        if not isinstance(owner, int):
            spot = pl.multiple_of(spot, rows)
        near = ordered[pl.ds(spot, rows), :width]
        far = ordered[pl.ds(spot, rows), width:]
        label = jnp.sum(jnp.where(ids == owner, labels, 0.0), axis=0, keepdims=True)
        label = jnp.broadcast_to(label, (length - 2 * rows, width))
        if length % 16 == 0:
            pieces = [(0, jnp.concatenate([near, far, label], axis=0))]
        else:
            pieces = [(0, near), (rows, far), (2 * rows, label)]
        for z in range(near_count):
            start = message_at(owner * near_count + z, length)
            for offset, piece in pieces:
                send_ref[pl.ds(start + offset, piece.shape[0])] = piece.astype(send_ref.dtype)
        return 0

    each(wide_count, write, 0)


def ladder_kernel(
    rows, near_count, own_count, recv_count, amp_ref, got_ref, out_ref, tiles, column, seen
):
    wide_count = seen.shape[0]
    width = got_ref.shape[1]
    length = got_ref.shape[0] // (wide_count * near_count)
    upper = lax.axis_index("narrow") >= near_count
    tiles[...] = jnp.zeros_like(tiles)
    for u in range(recv_count):
        column[u] = 0

    def message(w, z):
        start = message_at(w * near_count + z, length)
        if length % 16 == 0:
            block = got_ref[pl.ds(start, length)].astype(jnp.float32)
            return block[:rows], block[rows : 2 * rows]
        return got_ref[pl.ds(start, rows)], got_ref[pl.ds(start + rows, rows)]

    def read_label(w):
        start = message_at(w * near_count, length)
        if length % 16 == 0:
            label = got_ref[pl.ds(start, length)].astype(jnp.float32)[2 * rows :]
        else:
            label = got_ref[pl.ds(start + 2 * rows, length - 2 * rows)].astype(jnp.float32)
        return jnp.max(label).astype(jnp.int32)

    def keep(w, label, found):
        live = jnp.minimum(label, 1)
        at = jnp.minimum(found, recv_count)
        place = jnp.maximum(label - 1, 0)
        column[at] = lax.div(place, own_count)
        spot = lax.rem(place, own_count)
        parts = [message(w, z) for z in range(near_count)]
        near = jnp.concatenate([part[0] for part in parts], axis=0).astype(tiles.dtype)
        far = jnp.concatenate([part[1] for part in parts], axis=0).astype(tiles.dtype)
        halves = [jnp.where(upper, far, near), jnp.where(upper, near, far)]
        tile = jnp.concatenate(halves, axis=0)
        at = pl.multiple_of(at * width, width)
        for q in range(own_count):
            kept = jnp.where((live > 0) & (spot == q), tile, jnp.zeros_like(tile))
            tiles[pl.ds(at, width), q * width : (q + 1) * width] = kept
        return found + live

    if wide_count <= UNROLL:
        labels = [read_label(w) for w in range(wide_count)]
        found = jnp.int32(0)
        for w in range(wide_count):
            found = keep(w, labels[w], found)
    else:

        def note(w, _):
            seen[w] = read_label(w)
            return 0

        lax.fori_loop(0, wide_count, note, 0)
        lax.fori_loop(0, wide_count, lambda w, found: keep(w, seen[w], found), jnp.int32(0))
    total = None
    for first in range(0, recv_count, GROUP):
        last = min(first + GROUP, recv_count)
        spots = [pl.multiple_of(column[u] * width, width) for u in range(first, last)]
        picked = jnp.concatenate([amp_ref[:, pl.ds(spot, width)] for spot in spots], axis=1)
        term = jnp.dot(
            picked, tiles[first * width : last * width], preferred_element_type=jnp.float32
        )
        total = term if total is None else total + term
    out_ref[...] = total


def shards(amplitudes, integrals, in_tile, counts, out_tile, owner_map):
    slot_count, rows, width = integrals.shape
    row_count = amplitudes.shape[0]
    wide_count = lax.axis_size("wide")
    depth_count = lax.axis_size("narrow")
    own_count = owner_map.shape[0] // wide_count
    recv_count = slot_count // 2
    near_count = depth_count // 2
    kind = integrals.dtype
    message_count = wide_count * near_count
    length = 2 * rows + PAIR
    if wide_count > UNROLL or length % PAIR != 0 or message_count * length % 16 != 0:
        length = -(-length // 16) * 16
    hbm = pl.BlockSpec(memory_space=pltpu.HBM)
    vmem = pl.BlockSpec(memory_space=pltpu.VMEM)
    limit = pltpu.CompilerParams(vmem_limit_bytes=32 * 2**20)
    across = [(z, (z + near_count) % depth_count) for z in range(depth_count)]
    far = lax.ppermute(integrals, "narrow", across)
    given = [in_tile, counts, out_tile, owner_map, integrals]
    given = [
        value if value.size == 1 else pltpu.with_memory_space_constraint(value, pltpu.HBM)
        for value in given
    ]
    ordered, sent = wide_count * rows, slot_count * rows
    order, labels, near = pl.pallas_call(
        functools.partial(route_kernel, own_count, wide_count),
        out_shape=[
            jax.ShapeDtypeStruct((ordered, sent), kind),
            jax.ShapeDtypeStruct((wide_count, width), kind),
            jax.ShapeDtypeStruct(integrals.shape, kind),
        ],
        in_specs=[hbm] * len(given),
        out_specs=[vmem] * 3,
        scratch_shapes=[pltpu.SMEM(value.shape, value.dtype) for value in given[:-1]]
        + [pltpu.SemaphoreType.DMA((len(given),))],
        compiler_params=limit,
        cost_estimate=pl.CostEstimate(flops=2**30, bytes_accessed=2**20, transcendentals=0),
        name="route",
    )(*given)
    send = pl.pallas_call(
        functools.partial(pack_kernel, wide_count, near_count),
        out_shape=jax.ShapeDtypeStruct((message_count * length, width), kind),
        in_specs=[vmem] * 4,
        out_specs=vmem,
        scratch_shapes=[
            pltpu.VMEM((sent, 2 * width), kind),
            pltpu.VMEM((ordered, 2 * width), jnp.float32),
        ],
        compiler_params=limit,
        name="pack",
    )(order, labels, near, far)
    groups = [
        [w * depth_count + half * near_count + z for w in range(wide_count) for z in range(near_count)]
        for half in range(2)
    ]
    got = lax.all_to_all(
        send.reshape(message_count, length // PAIR, PAIR, width),
        ("wide", "narrow"),
        split_axis=0,
        concat_axis=0,
        tiled=True,
        axis_index_groups=groups,
    ).reshape(message_count * length, width)
    return pl.pallas_call(
        functools.partial(ladder_kernel, rows, near_count, own_count, recv_count),
        out_shape=jax.ShapeDtypeStruct((row_count, own_count * width), jnp.float32),
        in_specs=[vmem] * 2,
        out_specs=vmem,
        scratch_shapes=[
            pltpu.VMEM(((recv_count + 1) * width, own_count * width), kind),
            pltpu.SMEM((recv_count + 1,), jnp.int32),
            pltpu.SMEM((wide_count,), jnp.int32),
        ],
        compiler_params=limit,
        name="ladder",
    )(amplitudes, got)


def solution(mesh):
    return jax.shard_map(
        shards,
        mesh=mesh,
        in_specs=(
            P("narrow", None),
            P("wide", "narrow", None),
            P("wide"),
            P("wide"),
            P("wide"),
            P(),
        ),
        out_specs=P("narrow", "wide"),
        check_vma=False,
    )
```

time: 20.8 us -> 20.1 us (0.966)
  blocking collectives: 17.5 us -> 10.4 us
  starting transfers between devices: 0 us -> 4.04 us
  waiting for transfers between devices: 0 us -> 2.3 us
    all_to_all x1, blocking collectives: 17.5 us -> 10.4 us  [shards(): lax.all_to_all(send.reshape(message_count, length // PAIR, PAIR, width),...]
    ppermute x0 -> x1, starting transfers between devices: none -> 4.04 us  [shards(): far = lax.ppermute(integrals, 'narrow', across)]
    ppermute x0 -> x1, waiting for transfers between devices: none -> 2.3 us  [shards(): far = lax.ppermute(integrals, 'narrow', across)]
    pallas_call x2 -> x3, Pallas kernels: 2.36 us -> 2.43 us  [the longest x1 1.32 us: shards(): pl.pallas_call(functools.partial(ladder_kernel, rows, near_count, own_cou...]
  transfers between devices with their start and end apart: 0 -> 1, of which waited for: 0 -> 1; matrix products, arithmetic and copies ran while one was open for 0% -> 0% of each run, Pallas kernels for 0% -> 4%
where the time goes in v11:
time: 20.1 us; the launch traced here: 19.9 us
  blocking collectives  10.4 us (52%)
  starting transfers between devices  4.04 us (20%)
  Pallas kernels  2.43 us (12%)
  waiting for transfers between devices  2.3 us (11%)
  between operations  0.68 us (3%)
    all_to_all x1, blocking collectives, shards(): lax.all_to_all(send.reshape(message_count, length // PAIR, PAIR, width),...  10.4 us
    ppermute x1, starting transfers between devices, shards(): far = lax.ppermute(integrals, 'narrow', across)  4.04 us
    ppermute x1, waiting for transfers between devices, shards(): far = lax.ppermute(integrals, 'narrow', across)  2.3 us
    pallas_call x1, Pallas kernels, shards(): pl.pallas_call(functools.partial(ladder_kernel, rows, near_count, own_cou...  1.32 us
    pallas_call x1, Pallas kernels, shards(): pl.pallas_call(functools.partial(route_kernel, own_count, wide_count), ou...  0.89 us
  transfers between devices with their start and end apart: 1, of which 1 were waited for; matrix products, arithmetic and copies ran while one was open for 0% of the time, Pallas kernels for 4%

profile of v11, /device:TPU:0, one launch (start us, length us, event | category | flops | bytes accessed | tf_op | source)
XLA Modules:
  0.0 19.9 jit_solution(2319027254335666285)
XLA Ops:
  0.0 4.0 %collective-permute-start = (bf16[8,32,128]{2,1,0:T(8,128)(2,1)}, bf16[8,32,128]{2,1,0:T(8,128)(2,1)S(1)}, u32[]{:S(2)}, u32[]{:S(2)}) collective-permute-start(bf16[8,32,128]{2,1,0:T(8,128)(2,1)} %refs_4_.1), channel_id=1, source_target_pairs={{0,2},{1,3},{2,0},{3,1},{4,6},{5,7},{6,4},{7,5},{8,10},{9,11},{10,... | collective-permute-start | bytes 196616 | tf_op jit(solution)/shard_map/ppermute | solution.py:182
  4.7 0.9 %route.1 = (bf16[256,256]{1,0:T(8,128)(2,1)S(1)}, bf16[8,128]{1,0:T(8,128)(2,1)S(1)}, bf16[8,32,128]{2,1,0:T(8,128)(2,1)S(1)}) custom-call(s32[8]{0:T(128)} %refs_0_.1, s32[1]{0:T(128)S(6)} %copy.7.refs_1_, s32[8]{0:T(128)} %refs_2_.1, s32[16]{0:T(128)} %refs_3_.1, bf16[8,32,128]{2,1,0:T(8,128)(2,1)} %refs_4_.1), custom_call_target="tpu_custom_call" | custom-call | flops 1073741824 | bytes 1048576 | tf_op jit(solution)/shard_map/route/pallas_call | solution.py:189
  5.6 0.0 copy-start
  5.6 2.3 %collective-permute-done.far_ref = bf16[8,32,128]{2,1,0:T(8,128)(2,1)S(1)} collective-permute-done((bf16[8,32,128]{2,1,0:T(8,128)(2,1)}, bf16[8,32,128]{2,1,0:T(8,128)(2,1)S(1)}, u32[]{:S(2)}, u32[]{:S(2)}) %collective-permute-start) | collective-permute-done | bytes 65568 | tf_op jit(solution)/shard_map/ppermute | solution.py:182
  7.9 0.2 %pack.1 = bf16[1056,128]{1,0:T(8,128)(2,1)S(1)} custom-call(bf16[256,256]{1,0:T(8,128)(2,1)S(1)} %get-tuple-element.8.order_ref, bf16[8,128]{1,0:T(8,128)(2,1)S(1)} %get-tuple-element.9.label_ref, bf16[8,32,128]{2,1,0:T(8,128)(2,1)S(1)} %get-tuple-element.10.near_ref, bf16[8,32,128]{2,1,0:T(8,128)(2,1)S(1)} %collective-permute-done.far_ref), custom_call_target="tpu_custom_call" | custom-call | tf_op jit(solution)/shard_map/pack/pallas_call | solution.py:204
  8.1 10.4 %all_to_all.5 = bf16[16,33,2,128]{3,2,1,0:T(2,128)(2,1)S(1)} all-to-all(bf16[16,33,2,128]{3,2,1,0:T(2,128)(2,1)S(1)} %bitcast.3), channel_id=1, replica_groups={{0,1,4,5,8,9,12,13,16,17,20,21,24,25,28,29},{2,3,6,7,10,11,14,15,18,19,..., dimensions={0} | all-to-all | bytes 540672 | tf_op jit(solution)/shard_map/all_to_all | solution.py:220
  18.5 0.0 copy-done
  18.5 1.3 %ladder.1 = f32[512,256]{1,0:T(8,128)} custom-call(bf16[512,1024]{1,0:T(8,128)(2,1)S(1)} %copy-done, bf16[1056,128]{1,0:T(8,128)(2,1)S(1)} %bitcast.2), custom_call_target="tpu_custom_call" | custom-call | tf_op jit(solution)/shard_map/ladder/pallas_call | solution.py:228
Async XLA Ops:
  0.0 7.9 %collective-permute-start = (bf16[8,32,128]{2,1,0:T(8,128)(2,1)}, bf16[8,32,128]{2,1,0:T(8,128)(2,1)S(1)}, u32[]{:S(2)}, u32[]{:S(2)}) collective-permute-start(bf16[8,32,128]{2,1,0:T(8,128)(2,1)} %refs_4_.1), channel_id=1, source_target_pairs={{0,2},{1,3},{2,0},{3,1},{4,6},{5,7},{6,4},{7,5},{8,10},{9,11},{10,... | collective-permute-start | bytes 196616 | tf_op jit(solution)/shard_map/ppermute | solution.py:182
  5.6 12.9 %copy-start = (bf16[512,1024]{1,0:T(8,128)(2,1)S(1)}, bf16[512,1024]{1,0:T(8,128)(2,1)}, u32[]{:S(2)}) copy-start(bf16[512,1024]{1,0:T(8,128)(2,1)} %amp_ref.1) | copy-start | bytes 3145732

commit v12 on v11

--- a/solution.py
+++ b/solution.py
@@ -9,6 +9,7 @@
 
 PAIR = 2
 GROUP = 4
+PARTS = 2
 UNROLL = 8
 
 
@@ -95,7 +96,7 @@
 
 
 def ladder_kernel(
-    rows, near_count, own_count, recv_count, amp_ref, got_ref, out_ref, tiles, column, seen
+    rows, near_count, own_count, recv_count, amp_ref, got_ref, out_hbm, out_ref, tiles, column, seen, sems
 ):
     wide_count = seen.shape[0]
     width = got_ref.shape[1]
@@ -150,16 +151,27 @@
 
         lax.fori_loop(0, wide_count, note, 0)
         lax.fori_loop(0, wide_count, lambda w, found: keep(w, seen[w], found), jnp.int32(0))
-    total = None
-    for first in range(0, recv_count, GROUP):
-        last = min(first + GROUP, recv_count)
-        spots = [pl.multiple_of(column[u] * width, width) for u in range(first, last)]
-        picked = jnp.concatenate([amp_ref[:, pl.ds(spot, width)] for spot in spots], axis=1)
-        term = jnp.dot(
-            picked, tiles[first * width : last * width], preferred_element_type=jnp.float32
-        )
-        total = term if total is None else total + term
-    out_ref[...] = total
+    row_count = amp_ref.shape[0]
+    chunk = row_count // PARTS
+    copies = []
+    for part in range(PARTS):
+        at = slice(part * chunk, (part + 1) * chunk)
+        total = None
+        for first in range(0, recv_count, GROUP):
+            last = min(first + GROUP, recv_count)
+            spots = [pl.multiple_of(column[u] * width, width) for u in range(first, last)]
+            picked = [amp_ref[at, pl.ds(spot, width)] for spot in spots]
+            term = jnp.dot(
+                jnp.concatenate(picked, axis=1),
+                tiles[first * width : last * width],
+                preferred_element_type=jnp.float32,
+            )
+            total = term if total is None else total + term
+        out_ref[at] = total
+        copies.append(pltpu.make_async_copy(out_ref.at[at], out_hbm.at[at], sems.at[part]))
+        copies[-1].start()
+    for copy in copies:
+        copy.wait()
 
 
 def shards(amplitudes, integrals, in_tile, counts, out_tile, owner_map):
@@ -229,11 +241,13 @@
         functools.partial(ladder_kernel, rows, near_count, own_count, recv_count),
         out_shape=jax.ShapeDtypeStruct((row_count, own_count * width), jnp.float32),
         in_specs=[vmem] * 2,
-        out_specs=vmem,
+        out_specs=hbm,
         scratch_shapes=[
+            pltpu.VMEM((row_count, own_count * width), jnp.float32),
             pltpu.VMEM(((recv_count + 1) * width, own_count * width), kind),
             pltpu.SMEM((recv_count + 1,), jnp.int32),
             pltpu.SMEM((wide_count,), jnp.int32),
+            pltpu.SemaphoreType.DMA((PARTS,)),
         ],
         compiler_params=limit,
         name="ladder",

time: 20.1 us -> 20.1 us (level)
  no operation moved by 1% of the time
where the time goes in v12:
time: 20.1 us; the launch traced here: 19.9 us
  blocking collectives  10.4 us (52%)
  starting transfers between devices  4.04 us (20%)
  Pallas kernels  2.45 us (12%)
  waiting for transfers between devices  2.3 us (11%)
  between operations  0.68 us (3%)
    all_to_all x1, blocking collectives, shards(): lax.all_to_all(send.reshape(message_count, length // PAIR, PAIR, width),...  10.4 us
    ppermute x1, starting transfers between devices, shards(): far = lax.ppermute(integrals, 'narrow', across)  4.04 us
    ppermute x1, waiting for transfers between devices, shards(): far = lax.ppermute(integrals, 'narrow', across)  2.3 us
    pallas_call x1, Pallas kernels, shards(): pl.pallas_call(functools.partial(ladder_kernel, rows, near_count, own_cou...  1.34 us
    pallas_call x1, Pallas kernels, shards(): pl.pallas_call(functools.partial(route_kernel, own_count, wide_count), ou...  0.89 us
  transfers between devices with their start and end apart: 1, of which 1 were waited for; matrix products, arithmetic and copies ran while one was open for 0% of the time, Pallas kernels for 4%

profile of v12, /device:TPU:0, one launch (start us, length us, event | category | flops | bytes accessed | tf_op | source)
XLA Modules:
  0.0 19.9 jit_solution(13169342556001702917)
XLA Ops:
  0.0 4.0 %collective-permute-start = (bf16[8,32,128]{2,1,0:T(8,128)(2,1)}, bf16[8,32,128]{2,1,0:T(8,128)(2,1)S(1)}, u32[]{:S(2)}, u32[]{:S(2)}) collective-permute-start(bf16[8,32,128]{2,1,0:T(8,128)(2,1)} %refs_4_.1), channel_id=1, source_target_pairs={{0,2},{1,3},{2,0},{3,1},{4,6},{5,7},{6,4},{7,5},{8,10},{9,11},{10,... | collective-permute-start | bytes 196616 | tf_op jit(solution)/shard_map/ppermute | solution.py:194
  4.7 0.9 %route.1 = (bf16[256,256]{1,0:T(8,128)(2,1)S(1)}, bf16[8,128]{1,0:T(8,128)(2,1)S(1)}, bf16[8,32,128]{2,1,0:T(8,128)(2,1)S(1)}) custom-call(s32[8]{0:T(128)} %refs_0_.1, s32[1]{0:T(128)S(6)} %copy.7.refs_1_, s32[8]{0:T(128)} %refs_2_.1, s32[16]{0:T(128)} %refs_3_.1, bf16[8,32,128]{2,1,0:T(8,128)(2,1)} %refs_4_.1), custom_call_target="tpu_custom_call" | custom-call | flops 1073741824 | bytes 1048576 | tf_op jit(solution)/shard_map/route/pallas_call | solution.py:201
  5.6 0.0 copy-start
  5.6 2.3 %collective-permute-done.far_ref = bf16[8,32,128]{2,1,0:T(8,128)(2,1)S(1)} collective-permute-done((bf16[8,32,128]{2,1,0:T(8,128)(2,1)}, bf16[8,32,128]{2,1,0:T(8,128)(2,1)S(1)}, u32[]{:S(2)}, u32[]{:S(2)}) %collective-permute-start) | collective-permute-done | bytes 65568 | tf_op jit(solution)/shard_map/ppermute | solution.py:194
  7.9 0.2 %pack.1 = bf16[1056,128]{1,0:T(8,128)(2,1)S(1)} custom-call(bf16[256,256]{1,0:T(8,128)(2,1)S(1)} %get-tuple-element.8.order_ref, bf16[8,128]{1,0:T(8,128)(2,1)S(1)} %get-tuple-element.9.label_ref, bf16[8,32,128]{2,1,0:T(8,128)(2,1)S(1)} %get-tuple-element.10.near_ref, bf16[8,32,128]{2,1,0:T(8,128)(2,1)S(1)} %collective-permute-done.far_ref), custom_call_target="tpu_custom_call" | custom-call | tf_op jit(solution)/shard_map/pack/pallas_call | solution.py:216
  8.1 10.4 %all_to_all.5 = bf16[16,33,2,128]{3,2,1,0:T(2,128)(2,1)S(1)} all-to-all(bf16[16,33,2,128]{3,2,1,0:T(2,128)(2,1)S(1)} %bitcast.3), channel_id=1, replica_groups={{0,1,4,5,8,9,12,13,16,17,20,21,24,25,28,29},{2,3,6,7,10,11,14,15,18,19,..., dimensions={0} | all-to-all | bytes 540672 | tf_op jit(solution)/shard_map/all_to_all | solution.py:232
  18.5 0.0 copy-done
  18.5 1.3 %ladder.1 = f32[512,256]{1,0:T(8,128)} custom-call(bf16[512,1024]{1,0:T(8,128)(2,1)S(1)} %copy-done, bf16[1056,128]{1,0:T(8,128)(2,1)S(1)} %bitcast.2), custom_call_target="tpu_custom_call" | custom-call | tf_op jit(solution)/shard_map/ladder/pallas_call | solution.py:240
Async XLA Ops:
  0.0 7.9 %collective-permute-start = (bf16[8,32,128]{2,1,0:T(8,128)(2,1)}, bf16[8,32,128]{2,1,0:T(8,128)(2,1)S(1)}, u32[]{:S(2)}, u32[]{:S(2)}) collective-permute-start(bf16[8,32,128]{2,1,0:T(8,128)(2,1)} %refs_4_.1), channel_id=1, source_target_pairs={{0,2},{1,3},{2,0},{3,1},{4,6},{5,7},{6,4},{7,5},{8,10},{9,11},{10,... | collective-permute-start | bytes 196616 | tf_op jit(solution)/shard_map/ppermute | solution.py:194
  5.6 12.9 %copy-start = (bf16[512,1024]{1,0:T(8,128)(2,1)S(1)}, bf16[512,1024]{1,0:T(8,128)(2,1)}, u32[]{:S(2)}) copy-start(bf16[512,1024]{1,0:T(8,128)(2,1)} %amp_ref.1) | copy-start | bytes 3145732

commit v13 on v12

--- a/solution.py
+++ b/solution.py
@@ -10,6 +10,7 @@
 PAIR = 2
 GROUP = 4
 PARTS = 2
+PIECES = 4
 UNROLL = 8
 
 
@@ -87,7 +88,7 @@
         else:
             pieces = [(0, near), (rows, far), (2 * rows, label)]
         for z in range(near_count):
-            start = message_at(owner * near_count + z, length)
+            start = message_at(z * wide_count + owner, length)
             for offset, piece in pieces:
                 send_ref[pl.ds(start + offset, piece.shape[0])] = piece.astype(send_ref.dtype)
         return 0
@@ -107,14 +108,14 @@
         column[u] = 0
 
     def message(w, z):
-        start = message_at(w * near_count + z, length)
+        start = message_at(z * wide_count + w, length)
         if length % 16 == 0:
             block = got_ref[pl.ds(start, length)].astype(jnp.float32)
             return block[:rows], block[rows : 2 * rows]
         return got_ref[pl.ds(start, rows)], got_ref[pl.ds(start + rows, rows)]
 
     def read_label(w):
-        start = message_at(w * near_count, length)
+        start = message_at(w, length)
         if length % 16 == 0:
             label = got_ref[pl.ds(start, length)].astype(jnp.float32)[2 * rows :]
         else:
@@ -168,8 +169,13 @@
             )
             total = term if total is None else total + term
         out_ref[at] = total
-        copies.append(pltpu.make_async_copy(out_ref.at[at], out_hbm.at[at], sems.at[part]))
-        copies[-1].start()
+        for piece in range(PIECES):
+            size = chunk // PIECES
+            rows_at = pl.ds(part * chunk + piece * size, size)
+            sem = sems.at[part * PIECES + piece]
+            copy = pltpu.make_async_copy(out_ref.at[rows_at], out_hbm.at[rows_at], sem)
+            copy.start()
+            copies.append(copy)
     for copy in copies:
         copy.wait()
 
@@ -226,7 +232,7 @@
         name="pack",
     )(order, labels, near, far)
     groups = [
-        [w * depth_count + half * near_count + z for w in range(wide_count) for z in range(near_count)]
+        [w * depth_count + half * near_count + z for z in range(near_count) for w in range(wide_count)]
         for half in range(2)
     ]
     got = lax.all_to_all(
@@ -247,7 +253,7 @@
             pltpu.VMEM(((recv_count + 1) * width, own_count * width), kind),
             pltpu.SMEM((recv_count + 1,), jnp.int32),
             pltpu.SMEM((wide_count,), jnp.int32),
-            pltpu.SemaphoreType.DMA((PARTS,)),
+            pltpu.SemaphoreType.DMA((PARTS * PIECES,)),
         ],
         compiler_params=limit,
         name="ladder",

time: 20.1 us -> 21.4 us (1.065)
  blocking collectives: 10.4 us -> 11.7 us
    all_to_all x1, blocking collectives: 10.4 us -> 11.7 us  [shards(): lax.all_to_all(send.reshape(message_count, length // PAIR, PAIR, width),...]
where the time goes in v13:
time: 21.4 us; the launch traced here: 21.2 us
  blocking collectives  11.7 us (55%)
  starting transfers between devices  4.04 us (19%)
  Pallas kernels  2.48 us (12%)
  waiting for transfers between devices  2.3 us (11%)
  between operations  0.68 us (3%)
    all_to_all x1, blocking collectives, shards(): lax.all_to_all(send.reshape(message_count, length // PAIR, PAIR, width),...  11.7 us
    ppermute x1, starting transfers between devices, shards(): far = lax.ppermute(integrals, 'narrow', across)  4.04 us
    ppermute x1, waiting for transfers between devices, shards(): far = lax.ppermute(integrals, 'narrow', across)  2.3 us
    pallas_call x1, Pallas kernels, shards(): pl.pallas_call(functools.partial(ladder_kernel, rows, near_count, own_cou...  1.38 us
    pallas_call x1, Pallas kernels, shards(): pl.pallas_call(functools.partial(route_kernel, own_count, wide_count), ou...  0.89 us
  transfers between devices with their start and end apart: 1, of which 1 were waited for; matrix products, arithmetic and copies ran while one was open for 0% of the time, Pallas kernels for 4%

profile of v13, /device:TPU:0, one launch (start us, length us, event | category | flops | bytes accessed | tf_op | source)
XLA Modules:
  0.0 21.2 jit_solution(13843878582615905565)
XLA Ops:
  0.0 4.0 %collective-permute-start = (bf16[8,32,128]{2,1,0:T(8,128)(2,1)}, bf16[8,32,128]{2,1,0:T(8,128)(2,1)S(1)}, u32[]{:S(2)}, u32[]{:S(2)}) collective-permute-start(bf16[8,32,128]{2,1,0:T(8,128)(2,1)} %refs_4_.1), channel_id=1, source_target_pairs={{0,2},{1,3},{2,0},{3,1},{4,6},{5,7},{6,4},{7,5},{8,10},{9,11},{10,... | collective-permute-start | bytes 196616 | tf_op jit(solution)/shard_map/ppermute | solution.py:200
  4.7 0.9 %route.1 = (bf16[256,256]{1,0:T(8,128)(2,1)S(1)}, bf16[8,128]{1,0:T(8,128)(2,1)S(1)}, bf16[8,32,128]{2,1,0:T(8,128)(2,1)S(1)}) custom-call(s32[8]{0:T(128)} %refs_0_.1, s32[1]{0:T(128)S(6)} %copy.7.refs_1_, s32[8]{0:T(128)} %refs_2_.1, s32[16]{0:T(128)} %refs_3_.1, bf16[8,32,128]{2,1,0:T(8,128)(2,1)} %refs_4_.1), custom_call_target="tpu_custom_call" | custom-call | flops 1073741824 | bytes 1048576 | tf_op jit(solution)/shard_map/route/pallas_call | solution.py:207
  5.6 0.0 copy-start
  5.6 2.3 %collective-permute-done.far_ref = bf16[8,32,128]{2,1,0:T(8,128)(2,1)S(1)} collective-permute-done((bf16[8,32,128]{2,1,0:T(8,128)(2,1)}, bf16[8,32,128]{2,1,0:T(8,128)(2,1)S(1)}, u32[]{:S(2)}, u32[]{:S(2)}) %collective-permute-start) | collective-permute-done | bytes 65568 | tf_op jit(solution)/shard_map/ppermute | solution.py:200
  7.9 0.2 pack.1
  8.1 11.7 %all_to_all.5 = bf16[16,33,2,128]{3,2,1,0:T(2,128)(2,1)S(1)} all-to-all(bf16[16,33,2,128]{3,2,1,0:T(2,128)(2,1)S(1)} %bitcast.3), channel_id=1, replica_groups={{0,4,8,12,16,20,24,28,1,5,9,13,17,21,25,29},{2,6,10,14,18,22,26,30,3,7,..., dimensions={0} | all-to-all | bytes 540672 | tf_op jit(solution)/shard_map/all_to_all | solution.py:238
  19.8 0.0 copy-done
  19.8 1.4 %ladder.1 = f32[512,256]{1,0:T(8,128)} custom-call(bf16[512,1024]{1,0:T(8,128)(2,1)S(1)} %copy-done, bf16[1056,128]{1,0:T(8,128)(2,1)S(1)} %bitcast.2), custom_call_target="tpu_custom_call" | custom-call | tf_op jit(solution)/shard_map/ladder/pallas_call | solution.py:246
Async XLA Ops:
  0.0 7.9 %collective-permute-start = (bf16[8,32,128]{2,1,0:T(8,128)(2,1)}, bf16[8,32,128]{2,1,0:T(8,128)(2,1)S(1)}, u32[]{:S(2)}, u32[]{:S(2)}) collective-permute-start(bf16[8,32,128]{2,1,0:T(8,128)(2,1)} %refs_4_.1), channel_id=1, source_target_pairs={{0,2},{1,3},{2,0},{3,1},{4,6},{5,7},{6,4},{7,5},{8,10},{9,11},{10,... | collective-permute-start | bytes 196616 | tf_op jit(solution)/shard_map/ppermute | solution.py:200
  5.6 14.2 %copy-start = (bf16[512,1024]{1,0:T(8,128)(2,1)S(1)}, bf16[512,1024]{1,0:T(8,128)(2,1)}, u32[]{:S(2)}) copy-start(bf16[512,1024]{1,0:T(8,128)(2,1)} %amp_ref.1) | copy-start | bytes 3145732

commit v14 on v11

--- a/solution.py
+++ b/solution.py
@@ -10,6 +10,7 @@
 PAIR = 2
 GROUP = 4
 UNROLL = 8
+CORES = 2
 
 
 def each(count, body, start):
@@ -20,9 +21,11 @@
     return start
 
 
-def message_at(index, length):
+def message_at(w, z, wide_count, near_count, length):
+    core, chip = w % CORES, w // CORES
+    index = (core * (wide_count // CORES) + chip) * near_count + z
     start = index * length
-    if not isinstance(index, int):
+    if not isinstance(w, int):
         start = pl.multiple_of(start, length)
     return start
 
@@ -86,7 +89,7 @@
         else:
             pieces = [(0, near), (rows, far), (2 * rows, label)]
         for z in range(near_count):
-            start = message_at(owner * near_count + z, length)
+            start = message_at(owner, z, wide_count, near_count, length)
             for offset, piece in pieces:
                 send_ref[pl.ds(start + offset, piece.shape[0])] = piece.astype(send_ref.dtype)
         return 0
@@ -106,14 +109,14 @@
         column[u] = 0
 
     def message(w, z):
-        start = message_at(w * near_count + z, length)
+        start = message_at(w, z, wide_count, near_count, length)
         if length % 16 == 0:
             block = got_ref[pl.ds(start, length)].astype(jnp.float32)
             return block[:rows], block[rows : 2 * rows]
         return got_ref[pl.ds(start, rows)], got_ref[pl.ds(start + rows, rows)]
 
     def read_label(w):
-        start = message_at(w * near_count, length)
+        start = message_at(w, 0, wide_count, near_count, length)
         if length % 16 == 0:
             label = got_ref[pl.ds(start, length)].astype(jnp.float32)[2 * rows :]
         else:
@@ -214,7 +217,12 @@
         name="pack",
     )(order, labels, near, far)
     groups = [
-        [w * depth_count + half * near_count + z for w in range(wide_count) for z in range(near_count)]
+        [
+            (chip * CORES + core) * depth_count + half * near_count + z
+            for core in range(CORES)
+            for chip in range(wide_count // CORES)
+            for z in range(near_count)
+        ]
         for half in range(2)
     ]
     got = lax.all_to_all(

time: 20.1 us -> 20.7 us (1.030)
  blocking collectives: 10.4 us -> 11 us
    all_to_all x1, blocking collectives: 10.4 us -> 11 us  [shards(): lax.all_to_all(send.reshape(message_count, length // PAIR, PAIR, width),...]
where the time goes in v14:
time: 20.7 us; the launch traced here: 20.5 us
  blocking collectives  11 us (53%)
  starting transfers between devices  4.04 us (20%)
  Pallas kernels  2.43 us (12%)
  waiting for transfers between devices  2.3 us (11%)
  between operations  0.68 us (3%)
    all_to_all x1, blocking collectives, shards(): lax.all_to_all(send.reshape(message_count, length // PAIR, PAIR, width),...  11 us
    ppermute x1, starting transfers between devices, shards(): far = lax.ppermute(integrals, 'narrow', across)  4.04 us
    ppermute x1, waiting for transfers between devices, shards(): far = lax.ppermute(integrals, 'narrow', across)  2.3 us
    pallas_call x1, Pallas kernels, shards(): pl.pallas_call(functools.partial(ladder_kernel, rows, near_count, own_cou...  1.32 us
    pallas_call x1, Pallas kernels, shards(): pl.pallas_call(functools.partial(route_kernel, own_count, wide_count), ou...  0.89 us
  transfers between devices with their start and end apart: 1, of which 1 were waited for; matrix products, arithmetic and copies ran while one was open for 0% of the time, Pallas kernels for 4%

profile of v14, /device:TPU:0, one launch (start us, length us, event | category | flops | bytes accessed | tf_op | source)
XLA Modules:
  0.0 20.5 jit_solution(6561937842733994341)
XLA Ops:
  0.0 4.0 %collective-permute-start = (bf16[8,32,128]{2,1,0:T(8,128)(2,1)}, bf16[8,32,128]{2,1,0:T(8,128)(2,1)S(1)}, u32[]{:S(2)}, u32[]{:S(2)}) collective-permute-start(bf16[8,32,128]{2,1,0:T(8,128)(2,1)} %refs_4_.1), channel_id=1, source_target_pairs={{0,2},{1,3},{2,0},{3,1},{4,6},{5,7},{6,4},{7,5},{8,10},{9,11},{10,... | collective-permute-start | bytes 196616 | tf_op jit(solution)/shard_map/ppermute | solution.py:185
  4.7 0.9 %route.1 = (bf16[256,256]{1,0:T(8,128)(2,1)S(1)}, bf16[8,128]{1,0:T(8,128)(2,1)S(1)}, bf16[8,32,128]{2,1,0:T(8,128)(2,1)S(1)}) custom-call(s32[8]{0:T(128)} %refs_0_.1, s32[1]{0:T(128)S(6)} %copy.7.refs_1_, s32[8]{0:T(128)} %refs_2_.1, s32[16]{0:T(128)} %refs_3_.1, bf16[8,32,128]{2,1,0:T(8,128)(2,1)} %refs_4_.1), custom_call_target="tpu_custom_call" | custom-call | flops 1073741824 | bytes 1048576 | tf_op jit(solution)/shard_map/route/pallas_call | solution.py:192
  5.6 0.0 copy-start
  5.6 2.3 %collective-permute-done.far_ref = bf16[8,32,128]{2,1,0:T(8,128)(2,1)S(1)} collective-permute-done((bf16[8,32,128]{2,1,0:T(8,128)(2,1)}, bf16[8,32,128]{2,1,0:T(8,128)(2,1)S(1)}, u32[]{:S(2)}, u32[]{:S(2)}) %collective-permute-start) | collective-permute-done | bytes 65568 | tf_op jit(solution)/shard_map/ppermute | solution.py:185
  7.9 0.2 %pack.1 = bf16[1056,128]{1,0:T(8,128)(2,1)S(1)} custom-call(bf16[256,256]{1,0:T(8,128)(2,1)S(1)} %get-tuple-element.8.order_ref, bf16[8,128]{1,0:T(8,128)(2,1)S(1)} %get-tuple-element.9.label_ref, bf16[8,32,128]{2,1,0:T(8,128)(2,1)S(1)} %get-tuple-element.10.near_ref, bf16[8,32,128]{2,1,0:T(8,128)(2,1)S(1)} %collective-permute-done.far_ref), custom_call_target="tpu_custom_call" | custom-call | tf_op jit(solution)/shard_map/pack/pallas_call | solution.py:207
  8.1 11.0 %all_to_all.5 = bf16[16,33,2,128]{3,2,1,0:T(2,128)(2,1)S(1)} all-to-all(bf16[16,33,2,128]{3,2,1,0:T(2,128)(2,1)S(1)} %bitcast.3), channel_id=1, replica_groups={{0,1,8,9,16,17,24,25,4,5,12,13,20,21,28,29},{2,3,10,11,18,19,26,27,6,7,..., dimensions={0} | all-to-all | bytes 540672 | tf_op jit(solution)/shard_map/all_to_all | solution.py:228
  19.2 0.0 copy-done
  19.2 1.3 %ladder.1 = f32[512,256]{1,0:T(8,128)} custom-call(bf16[512,1024]{1,0:T(8,128)(2,1)S(1)} %copy-done, bf16[1056,128]{1,0:T(8,128)(2,1)S(1)} %bitcast.2), custom_call_target="tpu_custom_call" | custom-call | tf_op jit(solution)/shard_map/ladder/pallas_call | solution.py:236
Async XLA Ops:
  0.0 7.9 %collective-permute-start = (bf16[8,32,128]{2,1,0:T(8,128)(2,1)}, bf16[8,32,128]{2,1,0:T(8,128)(2,1)S(1)}, u32[]{:S(2)}, u32[]{:S(2)}) collective-permute-start(bf16[8,32,128]{2,1,0:T(8,128)(2,1)} %refs_4_.1), channel_id=1, source_target_pairs={{0,2},{1,3},{2,0},{3,1},{4,6},{5,7},{6,4},{7,5},{8,10},{9,11},{10,... | collective-permute-start | bytes 196616 | tf_op jit(solution)/shard_map/ppermute | solution.py:185
  5.6 13.6 %copy-start = (bf16[512,1024]{1,0:T(8,128)(2,1)S(1)}, bf16[512,1024]{1,0:T(8,128)(2,1)}, u32[]{:S(2)}) copy-start(bf16[512,1024]{1,0:T(8,128)(2,1)} %amp_ref.1) | copy-start | bytes 3145732

commit v15 on v14

--- a/solution.py
+++ b/solution.py
@@ -10,7 +10,6 @@
 PAIR = 2
 GROUP = 4
 UNROLL = 8
-CORES = 2
 
 
 def each(count, body, start):
@@ -22,9 +21,8 @@
 
 
 def message_at(w, z, wide_count, near_count, length):
-    core, chip = w % CORES, w // CORES
-    index = (core * (wide_count // CORES) + chip) * near_count + z
-    start = index * length
+    place = (w + wide_count // 2) % wide_count
+    start = (place * near_count + z) * length
     if not isinstance(w, int):
         start = pl.multiple_of(start, length)
     return start
@@ -218,9 +216,8 @@
     )(order, labels, near, far)
     groups = [
         [
-            (chip * CORES + core) * depth_count + half * near_count + z
-            for core in range(CORES)
-            for chip in range(wide_count // CORES)
+            (place - wide_count // 2) % wide_count * depth_count + half * near_count + z
+            for place in range(wide_count)
             for z in range(near_count)
         ]
         for half in range(2)

time: 20.7 us -> 20.1 us (0.971)
  blocking collectives: 11 us -> 10.4 us
    all_to_all x1, blocking collectives: 11 us -> 10.4 us  [shards(): lax.all_to_all(send.reshape(message_count, length // PAIR, PAIR, width),...]
where the time goes in v15:
time: 20.1 us; the launch traced here: 19.9 us
  blocking collectives  10.4 us (52%)
  starting transfers between devices  4.04 us (20%)
  Pallas kernels  2.43 us (12%)
  waiting for transfers between devices  2.3 us (11%)
  between operations  0.68 us (3%)
    all_to_all x1, blocking collectives, shards(): lax.all_to_all(send.reshape(message_count, length // PAIR, PAIR, width),...  10.4 us
    ppermute x1, starting transfers between devices, shards(): far = lax.ppermute(integrals, 'narrow', across)  4.04 us
    ppermute x1, waiting for transfers between devices, shards(): far = lax.ppermute(integrals, 'narrow', across)  2.3 us
    pallas_call x1, Pallas kernels, shards(): pl.pallas_call(functools.partial(ladder_kernel, rows, near_count, own_cou...  1.32 us
    pallas_call x1, Pallas kernels, shards(): pl.pallas_call(functools.partial(route_kernel, own_count, wide_count), ou...  0.89 us
  transfers between devices with their start and end apart: 1, of which 1 were waited for; matrix products, arithmetic and copies ran while one was open for 0% of the time, Pallas kernels for 4%

profile of v15, /device:TPU:0, one launch (start us, length us, event | category | flops | bytes accessed | tf_op | source)
XLA Modules:
  0.0 19.9 jit_solution(4634305708542621567)
XLA Ops:
  0.0 4.0 %collective-permute-start = (bf16[8,32,128]{2,1,0:T(8,128)(2,1)}, bf16[8,32,128]{2,1,0:T(8,128)(2,1)S(1)}, u32[]{:S(2)}, u32[]{:S(2)}) collective-permute-start(bf16[8,32,128]{2,1,0:T(8,128)(2,1)} %refs_4_.1), channel_id=1, source_target_pairs={{0,2},{1,3},{2,0},{3,1},{4,6},{5,7},{6,4},{7,5},{8,10},{9,11},{10,... | collective-permute-start | bytes 196616 | tf_op jit(solution)/shard_map/ppermute | solution.py:183
  4.7 0.9 %route.1 = (bf16[256,256]{1,0:T(8,128)(2,1)S(1)}, bf16[8,128]{1,0:T(8,128)(2,1)S(1)}, bf16[8,32,128]{2,1,0:T(8,128)(2,1)S(1)}) custom-call(s32[8]{0:T(128)} %refs_0_.1, s32[1]{0:T(128)S(6)} %copy.7.refs_1_, s32[8]{0:T(128)} %refs_2_.1, s32[16]{0:T(128)} %refs_3_.1, bf16[8,32,128]{2,1,0:T(8,128)(2,1)} %refs_4_.1), custom_call_target="tpu_custom_call" | custom-call | flops 1073741824 | bytes 1048576 | tf_op jit(solution)/shard_map/route/pallas_call | solution.py:190
  5.6 0.0 copy-start
  5.6 2.3 %collective-permute-done.far_ref = bf16[8,32,128]{2,1,0:T(8,128)(2,1)S(1)} collective-permute-done((bf16[8,32,128]{2,1,0:T(8,128)(2,1)}, bf16[8,32,128]{2,1,0:T(8,128)(2,1)S(1)}, u32[]{:S(2)}, u32[]{:S(2)}) %collective-permute-start) | collective-permute-done | bytes 65568 | tf_op jit(solution)/shard_map/ppermute | solution.py:183
  7.9 0.2 %pack.1 = bf16[1056,128]{1,0:T(8,128)(2,1)S(1)} custom-call(bf16[256,256]{1,0:T(8,128)(2,1)S(1)} %get-tuple-element.8.order_ref, bf16[8,128]{1,0:T(8,128)(2,1)S(1)} %get-tuple-element.9.label_ref, bf16[8,32,128]{2,1,0:T(8,128)(2,1)S(1)} %get-tuple-element.10.near_ref, bf16[8,32,128]{2,1,0:T(8,128)(2,1)S(1)} %collective-permute-done.far_ref), custom_call_target="tpu_custom_call" | custom-call | tf_op jit(solution)/shard_map/pack/pallas_call | solution.py:205
  8.1 10.4 %all_to_all.5 = bf16[16,33,2,128]{3,2,1,0:T(2,128)(2,1)S(1)} all-to-all(bf16[16,33,2,128]{3,2,1,0:T(2,128)(2,1)S(1)} %bitcast.3), channel_id=1, replica_groups={{16,17,20,21,24,25,28,29,0,1,4,5,8,9,12,13},{18,19,22,23,26,27,30,31,2,..., dimensions={0} | all-to-all | bytes 540672 | tf_op jit(solution)/shard_map/all_to_all | solution.py:225
  18.5 0.0 copy-done
  18.5 1.3 %ladder.1 = f32[512,256]{1,0:T(8,128)} custom-call(bf16[512,1024]{1,0:T(8,128)(2,1)S(1)} %copy-done, bf16[1056,128]{1,0:T(8,128)(2,1)S(1)} %bitcast.2), custom_call_target="tpu_custom_call" | custom-call | tf_op jit(solution)/shard_map/ladder/pallas_call | solution.py:233
Async XLA Ops:
  0.0 7.9 %collective-permute-start = (bf16[8,32,128]{2,1,0:T(8,128)(2,1)}, bf16[8,32,128]{2,1,0:T(8,128)(2,1)S(1)}, u32[]{:S(2)}, u32[]{:S(2)}) collective-permute-start(bf16[8,32,128]{2,1,0:T(8,128)(2,1)} %refs_4_.1), channel_id=1, source_target_pairs={{0,2},{1,3},{2,0},{3,1},{4,6},{5,7},{6,4},{7,5},{8,10},{9,11},{10,... | collective-permute-start | bytes 196616 | tf_op jit(solution)/shard_map/ppermute | solution.py:183
  5.6 12.9 %copy-start = (bf16[512,1024]{1,0:T(8,128)(2,1)S(1)}, bf16[512,1024]{1,0:T(8,128)(2,1)}, u32[]{:S(2)}) copy-start(bf16[512,1024]{1,0:T(8,128)(2,1)} %amp_ref.1) | copy-start | bytes 3145732

commit v16 on v15

--- a/solution.py
+++ b/solution.py
@@ -10,6 +10,7 @@
 PAIR = 2
 GROUP = 4
 UNROLL = 8
+SHIFT = 2
 
 
 def each(count, body, start):
@@ -21,7 +22,7 @@
 
 
 def message_at(w, z, wide_count, near_count, length):
-    place = (w + wide_count // 2) % wide_count
+    place = (w + wide_count - SHIFT) % wide_count
     start = (place * near_count + z) * length
     if not isinstance(w, int):
         start = pl.multiple_of(start, length)
@@ -216,7 +217,7 @@
     )(order, labels, near, far)
     groups = [
         [
-            (place - wide_count // 2) % wide_count * depth_count + half * near_count + z
+            (place + SHIFT) % wide_count * depth_count + half * near_count + z
             for place in range(wide_count)
             for z in range(near_count)
         ]

time: 20.1 us -> 19.5 us (0.970)
  blocking collectives: 10.4 us -> 9.87 us
    all_to_all x1, blocking collectives: 10.4 us -> 9.87 us  [shards(): lax.all_to_all(send.reshape(message_count, length // PAIR, PAIR, width),...]
  transfers between devices with their start and end apart: 1 -> 1, of which waited for: 1 -> 1; matrix products, arithmetic and copies ran while one was open for 0% -> 0% of each run, Pallas kernels for 4% -> 5%
where the time goes in v16:
time: 19.5 us; the launch traced here: 19.3 us
  blocking collectives  9.87 us (51%)
  starting transfers between devices  4.04 us (21%)
  Pallas kernels  2.44 us (13%)
  waiting for transfers between devices  2.3 us (12%)
  between operations  0.68 us (3%)
    all_to_all x1, blocking collectives, shards(): lax.all_to_all(send.reshape(message_count, length // PAIR, PAIR, width),...  9.87 us
    ppermute x1, starting transfers between devices, shards(): far = lax.ppermute(integrals, 'narrow', across)  4.04 us
    ppermute x1, waiting for transfers between devices, shards(): far = lax.ppermute(integrals, 'narrow', across)  2.3 us
    pallas_call x1, Pallas kernels, shards(): pl.pallas_call(functools.partial(ladder_kernel, rows, near_count, own_cou...  1.32 us
    pallas_call x1, Pallas kernels, shards(): pl.pallas_call(functools.partial(route_kernel, own_count, wide_count), ou...  0.89 us
  transfers between devices with their start and end apart: 1, of which 1 were waited for; matrix products, arithmetic and copies ran while one was open for 0% of the time, Pallas kernels for 5%

profile of v16, /device:TPU:0, one launch (start us, length us, event | category | flops | bytes accessed | tf_op | source)
XLA Modules:
  0.0 19.3 jit_solution(5501897176777424372)
XLA Ops:
  0.0 4.0 %collective-permute-start = (bf16[8,32,128]{2,1,0:T(8,128)(2,1)}, bf16[8,32,128]{2,1,0:T(8,128)(2,1)S(1)}, u32[]{:S(2)}, u32[]{:S(2)}) collective-permute-start(bf16[8,32,128]{2,1,0:T(8,128)(2,1)} %refs_4_.1), channel_id=1, source_target_pairs={{0,2},{1,3},{2,0},{3,1},{4,6},{5,7},{6,4},{7,5},{8,10},{9,11},{10,... | collective-permute-start | bytes 196616 | tf_op jit(solution)/shard_map/ppermute | solution.py:184
  4.7 0.9 %route.1 = (bf16[256,256]{1,0:T(8,128)(2,1)S(1)}, bf16[8,128]{1,0:T(8,128)(2,1)S(1)}, bf16[8,32,128]{2,1,0:T(8,128)(2,1)S(1)}) custom-call(s32[8]{0:T(128)} %refs_0_.1, s32[1]{0:T(128)S(6)} %copy.7.refs_1_, s32[8]{0:T(128)} %refs_2_.1, s32[16]{0:T(128)} %refs_3_.1, bf16[8,32,128]{2,1,0:T(8,128)(2,1)} %refs_4_.1), custom_call_target="tpu_custom_call" | custom-call | flops 1073741824 | bytes 1048576 | tf_op jit(solution)/shard_map/route/pallas_call | solution.py:191
  5.6 0.0 copy-start
  5.6 2.3 %collective-permute-done.far_ref = bf16[8,32,128]{2,1,0:T(8,128)(2,1)S(1)} collective-permute-done((bf16[8,32,128]{2,1,0:T(8,128)(2,1)}, bf16[8,32,128]{2,1,0:T(8,128)(2,1)S(1)}, u32[]{:S(2)}, u32[]{:S(2)}) %collective-permute-start) | collective-permute-done | bytes 65568 | tf_op jit(solution)/shard_map/ppermute | solution.py:184
  7.9 0.2 %pack.1 = bf16[1056,128]{1,0:T(8,128)(2,1)S(1)} custom-call(bf16[256,256]{1,0:T(8,128)(2,1)S(1)} %get-tuple-element.8.order_ref, bf16[8,128]{1,0:T(8,128)(2,1)S(1)} %get-tuple-element.9.label_ref, bf16[8,32,128]{2,1,0:T(8,128)(2,1)S(1)} %get-tuple-element.10.near_ref, bf16[8,32,128]{2,1,0:T(8,128)(2,1)S(1)} %collective-permute-done.far_ref), custom_call_target="tpu_custom_call" | custom-call | tf_op jit(solution)/shard_map/pack/pallas_call | solution.py:206
  8.1 9.9 %all_to_all.5 = bf16[16,33,2,128]{3,2,1,0:T(2,128)(2,1)S(1)} all-to-all(bf16[16,33,2,128]{3,2,1,0:T(2,128)(2,1)S(1)} %bitcast.3), channel_id=1, replica_groups={{8,9,12,13,16,17,20,21,24,25,28,29,0,1,4,5},{10,11,14,15,18,19,22,23,26..., dimensions={0} | all-to-all | bytes 540672 | tf_op jit(solution)/shard_map/all_to_all | solution.py:226
  18.0 0.0 copy-done
  18.0 1.3 %ladder.1 = f32[512,256]{1,0:T(8,128)} custom-call(bf16[512,1024]{1,0:T(8,128)(2,1)S(1)} %copy-done, bf16[1056,128]{1,0:T(8,128)(2,1)S(1)} %bitcast.2), custom_call_target="tpu_custom_call" | custom-call | tf_op jit(solution)/shard_map/ladder/pallas_call | solution.py:234
Async XLA Ops:
  0.0 7.9 %collective-permute-start = (bf16[8,32,128]{2,1,0:T(8,128)(2,1)}, bf16[8,32,128]{2,1,0:T(8,128)(2,1)S(1)}, u32[]{:S(2)}, u32[]{:S(2)}) collective-permute-start(bf16[8,32,128]{2,1,0:T(8,128)(2,1)} %refs_4_.1), channel_id=1, source_target_pairs={{0,2},{1,3},{2,0},{3,1},{4,6},{5,7},{6,4},{7,5},{8,10},{9,11},{10,... | collective-permute-start | bytes 196616 | tf_op jit(solution)/shard_map/ppermute | solution.py:184
  5.6 12.4 %copy-start = (bf16[512,1024]{1,0:T(8,128)(2,1)S(1)}, bf16[512,1024]{1,0:T(8,128)(2,1)}, u32[]{:S(2)}) copy-start(bf16[512,1024]{1,0:T(8,128)(2,1)} %amp_ref.1) | copy-start | bytes 3145732

commit v17 on v14

--- a/solution.py
+++ b/solution.py
@@ -22,9 +22,8 @@
 
 
 def message_at(w, z, wide_count, near_count, length):
-    core, chip = w % CORES, w // CORES
-    index = (core * (wide_count // CORES) + chip) * near_count + z
-    start = index * length
+    place = (wide_count // CORES - 1 - w // CORES) * CORES + w % CORES
+    start = (place * near_count + z) * length
     if not isinstance(w, int):
         start = pl.multiple_of(start, length)
     return start
@@ -219,8 +218,8 @@
     groups = [
         [
             (chip * CORES + core) * depth_count + half * near_count + z
+            for chip in reversed(range(wide_count // CORES))
             for core in range(CORES)
-            for chip in range(wide_count // CORES)
             for z in range(near_count)
         ]
         for half in range(2)

time: 20.7 us -> 20.4 us (0.986)
  blocking collectives: 11 us -> 10.7 us
    all_to_all x1, blocking collectives: 11 us -> 10.7 us  [shards(): lax.all_to_all(send.reshape(message_count, length // PAIR, PAIR, width),...]
where the time goes in v17:
time: 20.4 us; the launch traced here: 20.2 us
  blocking collectives  10.7 us (52%)
  starting transfers between devices  4.04 us (20%)
  Pallas kernels  2.43 us (12%)
  waiting for transfers between devices  2.3 us (11%)
  between operations  0.68 us (3%)
    all_to_all x1, blocking collectives, shards(): lax.all_to_all(send.reshape(message_count, length // PAIR, PAIR, width),...  10.7 us
    ppermute x1, starting transfers between devices, shards(): far = lax.ppermute(integrals, 'narrow', across)  4.04 us
    ppermute x1, waiting for transfers between devices, shards(): far = lax.ppermute(integrals, 'narrow', across)  2.3 us
    pallas_call x1, Pallas kernels, shards(): pl.pallas_call(functools.partial(ladder_kernel, rows, near_count, own_cou...  1.32 us
    pallas_call x1, Pallas kernels, shards(): pl.pallas_call(functools.partial(route_kernel, own_count, wide_count), ou...  0.89 us
  transfers between devices with their start and end apart: 1, of which 1 were waited for; matrix products, arithmetic and copies ran while one was open for 0% of the time, Pallas kernels for 4%

profile of v17, /device:TPU:0, one launch (start us, length us, event | category | flops | bytes accessed | tf_op | source)
XLA Modules:
  0.0 20.2 jit_solution(246536127130546034)
XLA Ops:
  0.0 4.0 %collective-permute-start = (bf16[8,32,128]{2,1,0:T(8,128)(2,1)}, bf16[8,32,128]{2,1,0:T(8,128)(2,1)S(1)}, u32[]{:S(2)}, u32[]{:S(2)}) collective-permute-start(bf16[8,32,128]{2,1,0:T(8,128)(2,1)} %refs_4_.1), channel_id=1, source_target_pairs={{0,2},{1,3},{2,0},{3,1},{4,6},{5,7},{6,4},{7,5},{8,10},{9,11},{10,... | collective-permute-start | bytes 196616 | tf_op jit(solution)/shard_map/ppermute | solution.py:184
  4.7 0.9 %route.1 = (bf16[256,256]{1,0:T(8,128)(2,1)S(1)}, bf16[8,128]{1,0:T(8,128)(2,1)S(1)}, bf16[8,32,128]{2,1,0:T(8,128)(2,1)S(1)}) custom-call(s32[8]{0:T(128)} %refs_0_.1, s32[1]{0:T(128)S(6)} %copy.7.refs_1_, s32[8]{0:T(128)} %refs_2_.1, s32[16]{0:T(128)} %refs_3_.1, bf16[8,32,128]{2,1,0:T(8,128)(2,1)} %refs_4_.1), custom_call_target="tpu_custom_call" | custom-call | flops 1073741824 | bytes 1048576 | tf_op jit(solution)/shard_map/route/pallas_call | solution.py:191
  5.6 0.0 copy-start
  5.6 2.3 %collective-permute-done.far_ref = bf16[8,32,128]{2,1,0:T(8,128)(2,1)S(1)} collective-permute-done((bf16[8,32,128]{2,1,0:T(8,128)(2,1)}, bf16[8,32,128]{2,1,0:T(8,128)(2,1)S(1)}, u32[]{:S(2)}, u32[]{:S(2)}) %collective-permute-start) | collective-permute-done | bytes 65568 | tf_op jit(solution)/shard_map/ppermute | solution.py:184
  7.9 0.2 %pack.1 = bf16[1056,128]{1,0:T(8,128)(2,1)S(1)} custom-call(bf16[256,256]{1,0:T(8,128)(2,1)S(1)} %get-tuple-element.8.order_ref, bf16[8,128]{1,0:T(8,128)(2,1)S(1)} %get-tuple-element.9.label_ref, bf16[8,32,128]{2,1,0:T(8,128)(2,1)S(1)} %get-tuple-element.10.near_ref, bf16[8,32,128]{2,1,0:T(8,128)(2,1)S(1)} %collective-permute-done.far_ref), custom_call_target="tpu_custom_call" | custom-call | tf_op jit(solution)/shard_map/pack/pallas_call | solution.py:206
  8.1 10.7 %all_to_all.5 = bf16[16,33,2,128]{3,2,1,0:T(2,128)(2,1)S(1)} all-to-all(bf16[16,33,2,128]{3,2,1,0:T(2,128)(2,1)S(1)} %bitcast.3), channel_id=1, replica_groups={{24,25,28,29,16,17,20,21,8,9,12,13,0,1,4,5},{26,27,30,31,18,19,22,23,10..., dimensions={0} | all-to-all | bytes 540672 | tf_op jit(solution)/shard_map/all_to_all | solution.py:227
  18.8 0.0 copy-done
  18.8 1.3 %ladder.1 = f32[512,256]{1,0:T(8,128)} custom-call(bf16[512,1024]{1,0:T(8,128)(2,1)S(1)} %copy-done, bf16[1056,128]{1,0:T(8,128)(2,1)S(1)} %bitcast.2), custom_call_target="tpu_custom_call" | custom-call | tf_op jit(solution)/shard_map/ladder/pallas_call | solution.py:235
Async XLA Ops:
  0.0 7.9 %collective-permute-start = (bf16[8,32,128]{2,1,0:T(8,128)(2,1)}, bf16[8,32,128]{2,1,0:T(8,128)(2,1)S(1)}, u32[]{:S(2)}, u32[]{:S(2)}) collective-permute-start(bf16[8,32,128]{2,1,0:T(8,128)(2,1)} %refs_4_.1), channel_id=1, source_target_pairs={{0,2},{1,3},{2,0},{3,1},{4,6},{5,7},{6,4},{7,5},{8,10},{9,11},{10,... | collective-permute-start | bytes 196616 | tf_op jit(solution)/shard_map/ppermute | solution.py:184
  5.6 13.3 %copy-start = (bf16[512,1024]{1,0:T(8,128)(2,1)S(1)}, bf16[512,1024]{1,0:T(8,128)(2,1)}, u32[]{:S(2)}) copy-start(bf16[512,1024]{1,0:T(8,128)(2,1)} %amp_ref.1) | copy-start | bytes 3145732

commit v18 on v17

--- a/solution.py
+++ b/solution.py
@@ -21,8 +21,20 @@
     return start
 
 
+def chip_order(wide_count):
+    chip_count = wide_count // CORES
+    if wide_count > UNROLL:
+        return list(range(chip_count))
+    bits = (chip_count - 1).bit_length()
+    flipped = [int(format(chip, "b").zfill(bits)[::-1], 2) for chip in range(2**bits)]
+    return [chip for chip in flipped[1:] if chip < chip_count] + [0]
+
+
 def message_at(w, z, wide_count, near_count, length):
-    place = (wide_count // CORES - 1 - w // CORES) * CORES + w % CORES
+    if isinstance(w, int):
+        place = chip_order(wide_count).index(w // CORES) * CORES + w % CORES
+    else:
+        place = w
     start = (place * near_count + z) * length
     if not isinstance(w, int):
         start = pl.multiple_of(start, length)
@@ -103,9 +115,6 @@
     width = got_ref.shape[1]
     length = got_ref.shape[0] // (wide_count * near_count)
     upper = lax.axis_index("narrow") >= near_count
-    tiles[...] = jnp.zeros_like(tiles)
-    for u in range(recv_count):
-        column[u] = 0
 
     def message(w, z):
         start = message_at(w, z, wide_count, near_count, length)
@@ -122,17 +131,20 @@
             label = got_ref[pl.ds(start + 2 * rows, length - 2 * rows)].astype(jnp.float32)
         return jnp.max(label).astype(jnp.int32)
 
+    def whole_tile(w):
+        parts = [message(w, z) for z in range(near_count)]
+        near = jnp.concatenate([part[0] for part in parts], axis=0).astype(tiles.dtype)
+        far = jnp.concatenate([part[1] for part in parts], axis=0).astype(tiles.dtype)
+        halves = [jnp.where(upper, far, near), jnp.where(upper, near, far)]
+        return jnp.concatenate(halves, axis=0)
+
     def keep(w, label, found):
         live = jnp.minimum(label, 1)
         at = jnp.minimum(found, recv_count)
         place = jnp.maximum(label - 1, 0)
         column[at] = lax.div(place, own_count)
         spot = lax.rem(place, own_count)
-        parts = [message(w, z) for z in range(near_count)]
-        near = jnp.concatenate([part[0] for part in parts], axis=0).astype(tiles.dtype)
-        far = jnp.concatenate([part[1] for part in parts], axis=0).astype(tiles.dtype)
-        halves = [jnp.where(upper, far, near), jnp.where(upper, near, far)]
-        tile = jnp.concatenate(halves, axis=0)
+        tile = whole_tile(w)
         at = pl.multiple_of(at * width, width)
         for q in range(own_count):
             kept = jnp.where((live > 0) & (spot == q), tile, jnp.zeros_like(tile))
@@ -140,11 +152,23 @@
         return found + live
 
     if wide_count <= UNROLL:
-        labels = [read_label(w) for w in range(wide_count)]
-        found = jnp.int32(0)
+        used = wide_count
         for w in range(wide_count):
-            found = keep(w, labels[w], found)
+            start = message_at(w, 0, wide_count, near_count, length) + 2 * rows
+            label = got_ref[pl.ds(start, length - 2 * rows)].astype(jnp.float32)[:1]
+            column[w] = lax.div(jnp.maximum(read_label(w) - 1, 0), own_count)
+            code = label.astype(jnp.int32) - 1
+            tile = whole_tile(w)
+            for q in range(own_count):
+                kept = (code >= 0) & (lax.rem(code, own_count) == q)
+                factor = jnp.where(kept, 1.0, 0.0).astype(tiles.dtype)
+                at = slice(w * width, (w + 1) * width)
+                tiles[at, q * width : (q + 1) * width] = tile * factor
     else:
+        used = recv_count
+        tiles[...] = jnp.zeros_like(tiles)
+        for u in range(recv_count):
+            column[u] = 0
 
         def note(w, _):
             seen[w] = read_label(w)
@@ -153,8 +177,8 @@
         lax.fori_loop(0, wide_count, note, 0)
         lax.fori_loop(0, wide_count, lambda w, found: keep(w, seen[w], found), jnp.int32(0))
     total = None
-    for first in range(0, recv_count, GROUP):
-        last = min(first + GROUP, recv_count)
+    for first in range(0, used, GROUP):
+        last = min(first + GROUP, used)
         spots = [pl.multiple_of(column[u] * width, width) for u in range(first, last)]
         picked = jnp.concatenate([amp_ref[:, pl.ds(spot, width)] for spot in spots], axis=1)
         term = jnp.dot(
@@ -172,6 +196,7 @@
     own_count = owner_map.shape[0] // wide_count
     recv_count = slot_count // 2
     near_count = depth_count // 2
+    held = max(recv_count + 1, min(wide_count, UNROLL))
     kind = integrals.dtype
     message_count = wide_count * near_count
     length = 2 * rows + PAIR
@@ -218,7 +243,7 @@
     groups = [
         [
             (chip * CORES + core) * depth_count + half * near_count + z
-            for chip in reversed(range(wide_count // CORES))
+            for chip in chip_order(wide_count)
             for core in range(CORES)
             for z in range(near_count)
         ]
@@ -238,8 +263,8 @@
         in_specs=[vmem] * 2,
         out_specs=vmem,
         scratch_shapes=[
-            pltpu.VMEM(((recv_count + 1) * width, own_count * width), kind),
-            pltpu.SMEM((recv_count + 1,), jnp.int32),
+            pltpu.VMEM((held * width, own_count * width), kind),
+            pltpu.SMEM((held,), jnp.int32),
             pltpu.SMEM((wide_count,), jnp.int32),
         ],
         compiler_params=limit,

time: 20.4 us -> 19.6 us (0.961)
  blocking collectives: 10.7 us -> 9.87 us
    all_to_all x1, blocking collectives: 10.7 us -> 9.87 us  [shards(): lax.all_to_all(send.reshape(message_count, length // PAIR, PAIR, width),...]
  transfers between devices with their start and end apart: 1 -> 1, of which waited for: 1 -> 1; matrix products, arithmetic and copies ran while one was open for 0% -> 0% of each run, Pallas kernels for 4% -> 5%
where the time goes in v18:
time: 19.6 us; the launch traced here: 19.4 us
  blocking collectives  9.87 us (50%)
  starting transfers between devices  4.04 us (21%)
  Pallas kernels  2.48 us (13%)
  waiting for transfers between devices  2.3 us (12%)
  between operations  0.68 us (3%)
    all_to_all x1, blocking collectives, shards(): lax.all_to_all(send.reshape(message_count, length // PAIR, PAIR, width),...  9.87 us
    ppermute x1, starting transfers between devices, shards(): far = lax.ppermute(integrals, 'narrow', across)  4.04 us
    ppermute x1, waiting for transfers between devices, shards(): far = lax.ppermute(integrals, 'narrow', across)  2.3 us
    pallas_call x1, Pallas kernels, shards(): pl.pallas_call(functools.partial(ladder_kernel, rows, near_count, own_cou...  1.37 us
    pallas_call x1, Pallas kernels, shards(): pl.pallas_call(functools.partial(route_kernel, own_count, wide_count), ou...  0.89 us
  transfers between devices with their start and end apart: 1, of which 1 were waited for; matrix products, arithmetic and copies ran while one was open for 0% of the time, Pallas kernels for 5%

profile of v18, /device:TPU:0, one launch (start us, length us, event | category | flops | bytes accessed | tf_op | source)
XLA Modules:
  0.0 19.4 jit_solution(3601804299674203672)
XLA Ops:
  0.0 4.0 %collective-permute-start = (bf16[8,32,128]{2,1,0:T(8,128)(2,1)}, bf16[8,32,128]{2,1,0:T(8,128)(2,1)S(1)}, u32[]{:S(2)}, u32[]{:S(2)}) collective-permute-start(bf16[8,32,128]{2,1,0:T(8,128)(2,1)} %refs_4_.1), channel_id=1, source_target_pairs={{0,2},{1,3},{2,0},{3,1},{4,6},{5,7},{6,4},{7,5},{8,10},{9,11},{10,... | collective-permute-start | bytes 196616 | tf_op jit(solution)/shard_map/ppermute | solution.py:209
  4.7 0.9 %route.1 = (bf16[256,256]{1,0:T(8,128)(2,1)S(1)}, bf16[8,128]{1,0:T(8,128)(2,1)S(1)}, bf16[8,32,128]{2,1,0:T(8,128)(2,1)S(1)}) custom-call(s32[8]{0:T(128)} %refs_0_.1, s32[1]{0:T(128)S(6)} %copy.7.refs_1_, s32[8]{0:T(128)} %refs_2_.1, s32[16]{0:T(128)} %refs_3_.1, bf16[8,32,128]{2,1,0:T(8,128)(2,1)} %refs_4_.1), custom_call_target="tpu_custom_call" | custom-call | flops 1073741824 | bytes 1048576 | tf_op jit(solution)/shard_map/route/pallas_call | solution.py:216
  5.6 0.0 copy-start
  5.6 2.3 %collective-permute-done.far_ref = bf16[8,32,128]{2,1,0:T(8,128)(2,1)S(1)} collective-permute-done((bf16[8,32,128]{2,1,0:T(8,128)(2,1)}, bf16[8,32,128]{2,1,0:T(8,128)(2,1)S(1)}, u32[]{:S(2)}, u32[]{:S(2)}) %collective-permute-start) | collective-permute-done | bytes 65568 | tf_op jit(solution)/shard_map/ppermute | solution.py:209
  7.9 0.2 %pack.1 = bf16[1056,128]{1,0:T(8,128)(2,1)S(1)} custom-call(bf16[256,256]{1,0:T(8,128)(2,1)S(1)} %get-tuple-element.8.order_ref, bf16[8,128]{1,0:T(8,128)(2,1)S(1)} %get-tuple-element.9.label_ref, bf16[8,32,128]{2,1,0:T(8,128)(2,1)S(1)} %get-tuple-element.10.near_ref, bf16[8,32,128]{2,1,0:T(8,128)(2,1)S(1)} %collective-permute-done.far_ref), custom_call_target="tpu_custom_call" | custom-call | tf_op jit(solution)/shard_map/pack/pallas_call | solution.py:231
  8.1 9.9 %all_to_all.5 = bf16[16,33,2,128]{3,2,1,0:T(2,128)(2,1)S(1)} all-to-all(bf16[16,33,2,128]{3,2,1,0:T(2,128)(2,1)S(1)} %bitcast.3), channel_id=1, replica_groups={{16,17,20,21,8,9,12,13,24,25,28,29,0,1,4,5},{18,19,22,23,10,11,14,15,26..., dimensions={0} | all-to-all | bytes 540672 | tf_op jit(solution)/shard_map/all_to_all | solution.py:252
  18.0 0.0 copy-done
  18.0 1.4 %ladder.1 = f32[512,256]{1,0:T(8,128)} custom-call(bf16[512,1024]{1,0:T(8,128)(2,1)S(1)} %copy-done, bf16[1056,128]{1,0:T(8,128)(2,1)S(1)} %bitcast.2), custom_call_target="tpu_custom_call" | custom-call | tf_op jit(solution)/shard_map/ladder/pallas_call | solution.py:260
Async XLA Ops:
  0.0 7.9 %collective-permute-start = (bf16[8,32,128]{2,1,0:T(8,128)(2,1)}, bf16[8,32,128]{2,1,0:T(8,128)(2,1)S(1)}, u32[]{:S(2)}, u32[]{:S(2)}) collective-permute-start(bf16[8,32,128]{2,1,0:T(8,128)(2,1)} %refs_4_.1), channel_id=1, source_target_pairs={{0,2},{1,3},{2,0},{3,1},{4,6},{5,7},{6,4},{7,5},{8,10},{9,11},{10,... | collective-permute-start | bytes 196616 | tf_op jit(solution)/shard_map/ppermute | solution.py:209
  5.6 12.4 %copy-start = (bf16[512,1024]{1,0:T(8,128)(2,1)S(1)}, bf16[512,1024]{1,0:T(8,128)(2,1)}, u32[]{:S(2)}) copy-start(bf16[512,1024]{1,0:T(8,128)(2,1)} %amp_ref.1) | copy-start | bytes 3145732

commit v19 on v17

--- a/solution.py
+++ b/solution.py
@@ -21,12 +21,26 @@
     return start
 
 
+def chip_order(wide_count):
+    chip_count = wide_count // CORES
+    if wide_count > UNROLL:
+        return list(range(chip_count))
+    bits = (chip_count - 1).bit_length()
+    flipped = [int(format(chip, "b").zfill(bits)[::-1], 2) for chip in range(2**bits)]
+    return [chip for chip in flipped[1:] if chip < chip_count] + [0]
+
+
+def group_places(wide_count, near_count):
+    depths = list(reversed(range(near_count)))
+    cores = range(CORES)
+    return [(chip * CORES + core, z) for chip in chip_order(wide_count) for z in depths for core in cores]
+
+
 def message_at(w, z, wide_count, near_count, length):
-    place = (wide_count // CORES - 1 - w // CORES) * CORES + w % CORES
-    start = (place * near_count + z) * length
-    if not isinstance(w, int):
-        start = pl.multiple_of(start, length)
-    return start
+    if isinstance(w, int):
+        return group_places(wide_count, near_count).index((w, z)) * length
+    place = (w // CORES * near_count + near_count - 1 - z) * CORES + w % CORES
+    return pl.multiple_of(place * length, length)
 
 
 def route_kernel(own_count, wide_count, *refs):
@@ -215,14 +229,9 @@
         compiler_params=limit,
         name="pack",
     )(order, labels, near, far)
+    places = group_places(wide_count, near_count)
     groups = [
-        [
-            (chip * CORES + core) * depth_count + half * near_count + z
-            for chip in reversed(range(wide_count // CORES))
-            for core in range(CORES)
-            for z in range(near_count)
-        ]
-        for half in range(2)
+        [w * depth_count + half * near_count + z for w, z in places] for half in range(2)
     ]
     got = lax.all_to_all(
         send.reshape(message_count, length // PAIR, PAIR, width),

time: 20.4 us -> 19.6 us (0.961)
  blocking collectives: 10.7 us -> 9.92 us
    all_to_all x1, blocking collectives: 10.7 us -> 9.92 us  [shards(): lax.all_to_all(send.reshape(message_count, length // PAIR, PAIR, width),...]
  transfers between devices with their start and end apart: 1 -> 1, of which waited for: 1 -> 1; matrix products, arithmetic and copies ran while one was open for 0% -> 0% of each run, Pallas kernels for 4% -> 5%
where the time goes in v19:
time: 19.6 us; the launch traced here: 19.4 us
  blocking collectives  9.92 us (51%)
  starting transfers between devices  4.04 us (21%)
  Pallas kernels  2.43 us (12%)
  waiting for transfers between devices  2.3 us (12%)
  between operations  0.68 us (3%)
    all_to_all x1, blocking collectives, shards(): lax.all_to_all(send.reshape(message_count, length // PAIR, PAIR, width),...  9.92 us
    ppermute x1, starting transfers between devices, shards(): far = lax.ppermute(integrals, 'narrow', across)  4.04 us
    ppermute x1, waiting for transfers between devices, shards(): far = lax.ppermute(integrals, 'narrow', across)  2.3 us
    pallas_call x1, Pallas kernels, shards(): pl.pallas_call(functools.partial(ladder_kernel, rows, near_count, own_cou...  1.32 us
    pallas_call x1, Pallas kernels, shards(): pl.pallas_call(functools.partial(route_kernel, own_count, wide_count), ou...  0.89 us
  transfers between devices with their start and end apart: 1, of which 1 were waited for; matrix products, arithmetic and copies ran while one was open for 0% of the time, Pallas kernels for 5%

profile of v19, /device:TPU:0, one launch (start us, length us, event | category | flops | bytes accessed | tf_op | source)
XLA Modules:
  0.0 19.4 jit_solution(5806862345899405849)
XLA Ops:
  0.0 4.0 %collective-permute-start = (bf16[8,32,128]{2,1,0:T(8,128)(2,1)}, bf16[8,32,128]{2,1,0:T(8,128)(2,1)S(1)}, u32[]{:S(2)}, u32[]{:S(2)}) collective-permute-start(bf16[8,32,128]{2,1,0:T(8,128)(2,1)} %refs_4_.1), channel_id=1, source_target_pairs={{0,2},{1,3},{2,0},{3,1},{4,6},{5,7},{6,4},{7,5},{8,10},{9,11},{10,... | collective-permute-start | bytes 196616 | tf_op jit(solution)/shard_map/ppermute | solution.py:198
  4.7 0.9 %route.1 = (bf16[256,256]{1,0:T(8,128)(2,1)S(1)}, bf16[8,128]{1,0:T(8,128)(2,1)S(1)}, bf16[8,32,128]{2,1,0:T(8,128)(2,1)S(1)}) custom-call(s32[8]{0:T(128)} %refs_0_.1, s32[1]{0:T(128)S(6)} %copy.7.refs_1_, s32[8]{0:T(128)} %refs_2_.1, s32[16]{0:T(128)} %refs_3_.1, bf16[8,32,128]{2,1,0:T(8,128)(2,1)} %refs_4_.1), custom_call_target="tpu_custom_call" | custom-call | flops 1073741824 | bytes 1048576 | tf_op jit(solution)/shard_map/route/pallas_call | solution.py:205
  5.6 0.0 copy-start
  5.6 2.3 %collective-permute-done.far_ref = bf16[8,32,128]{2,1,0:T(8,128)(2,1)S(1)} collective-permute-done((bf16[8,32,128]{2,1,0:T(8,128)(2,1)}, bf16[8,32,128]{2,1,0:T(8,128)(2,1)S(1)}, u32[]{:S(2)}, u32[]{:S(2)}) %collective-permute-start) | collective-permute-done | bytes 65568 | tf_op jit(solution)/shard_map/ppermute | solution.py:198
  7.9 0.2 %pack.1 = bf16[1056,128]{1,0:T(8,128)(2,1)S(1)} custom-call(bf16[256,256]{1,0:T(8,128)(2,1)S(1)} %get-tuple-element.8.order_ref, bf16[8,128]{1,0:T(8,128)(2,1)S(1)} %get-tuple-element.9.label_ref, bf16[8,32,128]{2,1,0:T(8,128)(2,1)S(1)} %get-tuple-element.10.near_ref, bf16[8,32,128]{2,1,0:T(8,128)(2,1)S(1)} %collective-permute-done.far_ref), custom_call_target="tpu_custom_call" | custom-call | tf_op jit(solution)/shard_map/pack/pallas_call | solution.py:220
  8.1 9.9 %all_to_all.5 = bf16[16,33,2,128]{3,2,1,0:T(2,128)(2,1)S(1)} all-to-all(bf16[16,33,2,128]{3,2,1,0:T(2,128)(2,1)S(1)} %bitcast.3), channel_id=1, replica_groups={{17,21,16,20,9,13,8,12,25,29,24,28,1,5,0,4},{19,23,18,22,11,15,10,14,27..., dimensions={0} | all-to-all | bytes 540672 | tf_op jit(solution)/shard_map/all_to_all | solution.py:236
  18.1 0.0 copy-done
  18.1 1.3 %ladder.1 = f32[512,256]{1,0:T(8,128)} custom-call(bf16[512,1024]{1,0:T(8,128)(2,1)S(1)} %copy-done, bf16[1056,128]{1,0:T(8,128)(2,1)S(1)} %bitcast.2), custom_call_target="tpu_custom_call" | custom-call | tf_op jit(solution)/shard_map/ladder/pallas_call | solution.py:244
Async XLA Ops:
  0.0 7.9 %collective-permute-start = (bf16[8,32,128]{2,1,0:T(8,128)(2,1)}, bf16[8,32,128]{2,1,0:T(8,128)(2,1)S(1)}, u32[]{:S(2)}, u32[]{:S(2)}) collective-permute-start(bf16[8,32,128]{2,1,0:T(8,128)(2,1)} %refs_4_.1), channel_id=1, source_target_pairs={{0,2},{1,3},{2,0},{3,1},{4,6},{5,7},{6,4},{7,5},{8,10},{9,11},{10,... | collective-permute-start | bytes 196616 | tf_op jit(solution)/shard_map/ppermute | solution.py:198
  5.6 12.5 %copy-start = (bf16[512,1024]{1,0:T(8,128)(2,1)S(1)}, bf16[512,1024]{1,0:T(8,128)(2,1)}, u32[]{:S(2)}) copy-start(bf16[512,1024]{1,0:T(8,128)(2,1)} %amp_ref.1) | copy-start | bytes 3145732

commit v20 on v19

--- a/solution.py
+++ b/solution.py
@@ -33,7 +33,13 @@
 def group_places(wide_count, near_count):
     depths = list(reversed(range(near_count)))
     cores = range(CORES)
-    return [(chip * CORES + core, z) for chip in chip_order(wide_count) for z in depths for core in cores]
+    places = []
+    for chip in chip_order(wide_count):
+        if chip == 0 and wide_count <= UNROLL:
+            places += [(core, z) for core in cores for z in range(near_count)]
+        else:
+            places += [(chip * CORES + core, z) for z in depths for core in cores]
+    return places
 
 
 def message_at(w, z, wide_count, near_count, length):
@@ -108,6 +114,12 @@
         return 0
 
     each(wide_count, write, 0)
+
+
+def fetch_kernel(source, target, sem):
+    copy = pltpu.make_async_copy(source, target, sem)
+    copy.start()
+    copy.wait()
 
 
 def ladder_kernel(
@@ -214,7 +226,6 @@
         scratch_shapes=[pltpu.SMEM(value.shape, value.dtype) for value in given[:-1]]
         + [pltpu.SemaphoreType.DMA((len(given),))],
         compiler_params=limit,
-        cost_estimate=pl.CostEstimate(flops=2**30, bytes_accessed=2**20, transcendentals=0),
         name="route",
     )(*given)
     send = pl.pallas_call(
@@ -241,6 +252,16 @@
         tiled=True,
         axis_index_groups=groups,
     ).reshape(message_count * length, width)
+    near = pl.pallas_call(
+        fetch_kernel,
+        out_shape=jax.ShapeDtypeStruct(amplitudes.shape, amplitudes.dtype),
+        in_specs=[hbm],
+        out_specs=vmem,
+        scratch_shapes=[pltpu.SemaphoreType.DMA],
+        compiler_params=limit,
+        cost_estimate=pl.CostEstimate(flops=2**30, bytes_accessed=2**21, transcendentals=0),
+        name="fetch",
+    )(pltpu.with_memory_space_constraint(amplitudes, pltpu.HBM))
     return pl.pallas_call(
         functools.partial(ladder_kernel, rows, near_count, own_count, recv_count),
         out_shape=jax.ShapeDtypeStruct((row_count, own_count * width), jnp.float32),
@@ -253,7 +274,7 @@
         ],
         compiler_params=limit,
         name="ladder",
-    )(amplitudes, got)
+    )(near, got)
 
 
 def solution(mesh):

time: 19.6 us -> 21.4 us (1.092)
  blocking collectives: 9.92 us -> 0 us
  starting transfers between devices: 4.04 us -> 9.45 us
  waiting for transfers between devices: 2.3 us -> 6.63 us
  Pallas kernels: 2.43 us -> 4.37 us
    all_to_all x1 -> x0, blocking collectives: 9.92 us -> none  [shards(): lax.all_to_all(send.reshape(message_count, length // PAIR, PAIR, width),...]
    all_to_all x0 -> x1, starting transfers between devices: none -> 5.41 us  [shards(): lax.all_to_all(send.reshape(message_count, length // PAIR, PAIR, width),...]
    all_to_all x0 -> x1, waiting for transfers between devices: none -> 4.32 us  [shards(): lax.all_to_all(send.reshape(message_count, length // PAIR, PAIR, width),...]
    pallas_call x0 -> x1, Pallas kernels: none -> 1.23 us  [shards(): pl.pallas_call(fetch_kernel, out_shape=jax.ShapeDtypeStruct(amplitudes.sh...]
    pallas_call x1, Pallas kernels: 0.22 us -> 0.93 us  [shards(): pl.pallas_call(functools.partial(pack_kernel, wide_count, near_count), ou...]
  transfers between devices with their start and end apart: 1 -> 2, of which waited for: 1 -> 2; matrix products, arithmetic and copies ran while one was open for 0% -> 0% of each run, Pallas kernels for 5% -> 10%
where the time goes in v20:
time: 21.4 us; the launch traced here: 21.1 us
  starting transfers between devices  9.45 us (44%)
  waiting for transfers between devices  6.63 us (31%)
  Pallas kernels  4.37 us (20%)
  between operations  0.67 us (3%)
    all_to_all x1, starting transfers between devices, shards(): lax.all_to_all(send.reshape(message_count, length // PAIR, PAIR, width),...  5.41 us
    all_to_all x1, waiting for transfers between devices, shards(): lax.all_to_all(send.reshape(message_count, length // PAIR, PAIR, width),...  4.32 us
    ppermute x1, starting transfers between devices, shards(): far = lax.ppermute(integrals, 'narrow', across)  4.04 us
    ppermute x1, waiting for transfers between devices, shards(): far = lax.ppermute(integrals, 'narrow', across)  2.31 us
    pallas_call x1, Pallas kernels, shards(): pl.pallas_call(functools.partial(ladder_kernel, rows, near_count, own_cou...  1.32 us
    pallas_call x1, Pallas kernels, shards(): pl.pallas_call(fetch_kernel, out_shape=jax.ShapeDtypeStruct(amplitudes.sh...  1.23 us
    pallas_call x1, Pallas kernels, shards(): pl.pallas_call(functools.partial(pack_kernel, wide_count, near_count), ou...  0.93 us
    pallas_call x1, Pallas kernels, shards(): pl.pallas_call(functools.partial(route_kernel, own_count, wide_count), ou...  0.89 us
  transfers between devices with their start and end apart: 2, of which 2 were waited for; matrix products, arithmetic and copies ran while one was open for 0% of the time, Pallas kernels for 10%

profile of v20, /device:TPU:0, one launch (start us, length us, event | category | flops | bytes accessed | tf_op | source)
XLA Modules:
  0.0 21.1 jit_solution(6056873299527860419)
XLA Ops:
  0.0 4.0 %collective-permute-start = (bf16[8,32,128]{2,1,0:T(8,128)(2,1)}, bf16[8,32,128]{2,1,0:T(8,128)(2,1)S(1)}, u32[]{:S(2)}, u32[]{:S(2)}) collective-permute-start(bf16[8,32,128]{2,1,0:T(8,128)(2,1)} %refs_4_.1), channel_id=1, source_target_pairs={{0,2},{1,3},{2,0},{3,1},{4,6},{5,7},{6,4},{7,5},{8,10},{9,11},{10,... | collective-permute-start | bytes 196616 | tf_op jit(solution)/shard_map/ppermute | solution.py:210
  4.7 0.9 %route.1 = (bf16[256,256]{1,0:T(8,128)(2,1)S(1)}, bf16[8,128]{1,0:T(8,128)(2,1)S(1)}, bf16[8,32,128]{2,1,0:T(8,128)(2,1)S(1)}) custom-call(s32[8]{0:T(128)} %refs_0_.1, s32[1]{0:T(128)S(6)} %copy.7.refs_1_, s32[8]{0:T(128)} %refs_2_.1, s32[16]{0:T(128)} %refs_3_.1, bf16[8,32,128]{2,1,0:T(8,128)(2,1)} %refs_4_.1), custom_call_target="tpu_custom_call" | custom-call | tf_op jit(solution)/shard_map/route/pallas_call | solution.py:217
  5.6 2.3 %collective-permute-done.far_ref = bf16[8,32,128]{2,1,0:T(8,128)(2,1)S(1)} collective-permute-done((bf16[8,32,128]{2,1,0:T(8,128)(2,1)}, bf16[8,32,128]{2,1,0:T(8,128)(2,1)S(1)}, u32[]{:S(2)}, u32[]{:S(2)}) %collective-permute-start) | collective-permute-done | bytes 65568 | tf_op jit(solution)/shard_map/ppermute | solution.py:210
  7.9 0.9 %pack.1 = bf16[1056,128]{1,0:T(8,128)(2,1)} custom-call(bf16[256,256]{1,0:T(8,128)(2,1)S(1)} %get-tuple-element.8.order_ref, bf16[8,128]{1,0:T(8,128)(2,1)S(1)} %get-tuple-element.9.label_ref, bf16[8,32,128]{2,1,0:T(8,128)(2,1)S(1)} %get-tuple-element.10.near_ref, bf16[8,32,128]{2,1,0:T(8,128)(2,1)S(1)} %collective-permute-done.far_ref), custom_call_target="tpu_custom_call" | custom-call | tf_op jit(solution)/shard_map/pack/pallas_call | solution.py:231
  8.8 5.4 %all-to-all-start = ((bf16[16,33,2,128]{3,2,1,0:T(2,128)(2,1)}), bf16[16,33,2,128]{3,2,1,0:T(2,128)(2,1)S(1)}, u32[]{:S(2)}, u32[]{:S(2)}) async-start(bf16[16,33,2,128]{3,2,1,0:T(2,128)(2,1)} %bitcast), calls=%async_computation | async-start | bytes 540672 | tf_op jit(solution)/shard_map/all_to_all | solution.py:247
  14.2 1.2 %fetch.1.amp_ref = bf16[512,1024]{1,0:T(8,128)(2,1)S(1)} custom-call(bf16[512,1024]{1,0:T(8,128)(2,1)} %source.1), custom_call_target="tpu_custom_call" | custom-call | flops 1073741824 | bytes 2097152 | tf_op jit(solution)/shard_map/fetch/pallas_call | solution.py:255
  15.5 4.3 %all-to-all-done = bf16[16,33,2,128]{3,2,1,0:T(2,128)(2,1)S(1)} async-done(((bf16[16,33,2,128]{3,2,1,0:T(2,128)(2,1)}), bf16[16,33,2,128]{3,2,1,0:T(2,128)(2,1)S(1)}, u32[]{:S(2)}, u32[]{:S(2)}) %all-to-all-start) | async-done | bytes 270368 | tf_op jit(solution)/shard_map/all_to_all | solution.py:247
  19.8 1.3 %ladder.1 = f32[512,256]{1,0:T(8,128)} custom-call(bf16[512,1024]{1,0:T(8,128)(2,1)S(1)} %fetch.1.amp_ref, bf16[1056,128]{1,0:T(8,128)(2,1)S(1)} %bitcast.2), custom_call_target="tpu_custom_call" | custom-call | tf_op jit(solution)/shard_map/ladder/pallas_call | solution.py:265
Async XLA Ops:
  0.0 7.9 %collective-permute-start = (bf16[8,32,128]{2,1,0:T(8,128)(2,1)}, bf16[8,32,128]{2,1,0:T(8,128)(2,1)S(1)}, u32[]{:S(2)}, u32[]{:S(2)}) collective-permute-start(bf16[8,32,128]{2,1,0:T(8,128)(2,1)} %refs_4_.1), channel_id=1, source_target_pairs={{0,2},{1,3},{2,0},{3,1},{4,6},{5,7},{6,4},{7,5},{8,10},{9,11},{10,... | collective-permute-start | bytes 196616 | tf_op jit(solution)/shard_map/ppermute | solution.py:210
  8.8 11.0 %all-to-all-start = ((bf16[16,33,2,128]{3,2,1,0:T(2,128)(2,1)}), bf16[16,33,2,128]{3,2,1,0:T(2,128)(2,1)S(1)}, u32[]{:S(2)}, u32[]{:S(2)}) async-start(bf16[16,33,2,128]{3,2,1,0:T(2,128)(2,1)} %bitcast), calls=%async_computation | async-start | bytes 540672 | tf_op jit(solution)/shard_map/all_to_all | solution.py:247

commit v21 on v19

--- a/solution.py
+++ b/solution.py
@@ -33,7 +33,13 @@
 def group_places(wide_count, near_count):
     depths = list(reversed(range(near_count)))
     cores = range(CORES)
-    return [(chip * CORES + core, z) for chip in chip_order(wide_count) for z in depths for core in cores]
+    places = []
+    for chip in chip_order(wide_count):
+        if chip == 0 and wide_count <= UNROLL:
+            places += [(core, z) for core in cores for z in range(near_count)]
+        else:
+            places += [(chip * CORES + core, z) for z in depths for core in cores]
+    return places
 
 
 def message_at(w, z, wide_count, near_count, length):

time: 19.6 us -> 20.4 us (1.041)
  blocking collectives: 9.92 us -> 10.8 us
    all_to_all x1, blocking collectives: 9.92 us -> 10.8 us  [shards(): lax.all_to_all(send.reshape(message_count, length // PAIR, PAIR, width),...]
  transfers between devices with their start and end apart: 1 -> 1, of which waited for: 1 -> 1; matrix products, arithmetic and copies ran while one was open for 0% -> 0% of each run, Pallas kernels for 5% -> 4%
where the time goes in v21:
time: 20.4 us; the launch traced here: 20.2 us
  blocking collectives  10.8 us (53%)
  starting transfers between devices  4.04 us (20%)
  Pallas kernels  2.43 us (12%)
  waiting for transfers between devices  2.3 us (11%)
  between operations  0.68 us (3%)
    all_to_all x1, blocking collectives, shards(): lax.all_to_all(send.reshape(message_count, length // PAIR, PAIR, width),...  10.8 us
    ppermute x1, starting transfers between devices, shards(): far = lax.ppermute(integrals, 'narrow', across)  4.04 us
    ppermute x1, waiting for transfers between devices, shards(): far = lax.ppermute(integrals, 'narrow', across)  2.3 us
    pallas_call x1, Pallas kernels, shards(): pl.pallas_call(functools.partial(ladder_kernel, rows, near_count, own_cou...  1.32 us
    pallas_call x1, Pallas kernels, shards(): pl.pallas_call(functools.partial(route_kernel, own_count, wide_count), ou...  0.89 us
  transfers between devices with their start and end apart: 1, of which 1 were waited for; matrix products, arithmetic and copies ran while one was open for 0% of the time, Pallas kernels for 4%

profile of v21, /device:TPU:0, one launch (start us, length us, event | category | flops | bytes accessed | tf_op | source)
XLA Modules:
  0.0 20.2 jit_solution(11207948879847383927)
XLA Ops:
  0.0 4.0 %collective-permute-start = (bf16[8,32,128]{2,1,0:T(8,128)(2,1)}, bf16[8,32,128]{2,1,0:T(8,128)(2,1)S(1)}, u32[]{:S(2)}, u32[]{:S(2)}) collective-permute-start(bf16[8,32,128]{2,1,0:T(8,128)(2,1)} %refs_4_.1), channel_id=1, source_target_pairs={{0,2},{1,3},{2,0},{3,1},{4,6},{5,7},{6,4},{7,5},{8,10},{9,11},{10,... | collective-permute-start | bytes 196616 | tf_op jit(solution)/shard_map/ppermute | solution.py:204
  4.7 0.9 %route.1 = (bf16[256,256]{1,0:T(8,128)(2,1)S(1)}, bf16[8,128]{1,0:T(8,128)(2,1)S(1)}, bf16[8,32,128]{2,1,0:T(8,128)(2,1)S(1)}) custom-call(s32[8]{0:T(128)} %refs_0_.1, s32[1]{0:T(128)S(6)} %copy.7.refs_1_, s32[8]{0:T(128)} %refs_2_.1, s32[16]{0:T(128)} %refs_3_.1, bf16[8,32,128]{2,1,0:T(8,128)(2,1)} %refs_4_.1), custom_call_target="tpu_custom_call" | custom-call | flops 1073741824 | bytes 1048576 | tf_op jit(solution)/shard_map/route/pallas_call | solution.py:211
  5.6 0.0 copy-start
  5.6 2.3 %collective-permute-done.far_ref = bf16[8,32,128]{2,1,0:T(8,128)(2,1)S(1)} collective-permute-done((bf16[8,32,128]{2,1,0:T(8,128)(2,1)}, bf16[8,32,128]{2,1,0:T(8,128)(2,1)S(1)}, u32[]{:S(2)}, u32[]{:S(2)}) %collective-permute-start) | collective-permute-done | bytes 65568 | tf_op jit(solution)/shard_map/ppermute | solution.py:204
  7.9 0.2 %pack.1 = bf16[1056,128]{1,0:T(8,128)(2,1)S(1)} custom-call(bf16[256,256]{1,0:T(8,128)(2,1)S(1)} %get-tuple-element.8.order_ref, bf16[8,128]{1,0:T(8,128)(2,1)S(1)} %get-tuple-element.9.label_ref, bf16[8,32,128]{2,1,0:T(8,128)(2,1)S(1)} %get-tuple-element.10.near_ref, bf16[8,32,128]{2,1,0:T(8,128)(2,1)S(1)} %collective-permute-done.far_ref), custom_call_target="tpu_custom_call" | custom-call | tf_op jit(solution)/shard_map/pack/pallas_call | solution.py:226
  8.1 10.8 %all_to_all.5 = bf16[16,33,2,128]{3,2,1,0:T(2,128)(2,1)S(1)} all-to-all(bf16[16,33,2,128]{3,2,1,0:T(2,128)(2,1)S(1)} %bitcast.3), channel_id=1, replica_groups={{17,21,16,20,9,13,8,12,25,29,24,28,0,1,4,5},{19,23,18,22,11,15,10,14,27..., dimensions={0} | all-to-all | bytes 540672 | tf_op jit(solution)/shard_map/all_to_all | solution.py:242
  18.9 0.0 copy-done
  18.9 1.3 %ladder.1 = f32[512,256]{1,0:T(8,128)} custom-call(bf16[512,1024]{1,0:T(8,128)(2,1)S(1)} %copy-done, bf16[1056,128]{1,0:T(8,128)(2,1)S(1)} %bitcast.2), custom_call_target="tpu_custom_call" | custom-call | tf_op jit(solution)/shard_map/ladder/pallas_call | solution.py:250
Async XLA Ops:
  0.0 7.9 %collective-permute-start = (bf16[8,32,128]{2,1,0:T(8,128)(2,1)}, bf16[8,32,128]{2,1,0:T(8,128)(2,1)S(1)}, u32[]{:S(2)}, u32[]{:S(2)}) collective-permute-start(bf16[8,32,128]{2,1,0:T(8,128)(2,1)} %refs_4_.1), channel_id=1, source_target_pairs={{0,2},{1,3},{2,0},{3,1},{4,6},{5,7},{6,4},{7,5},{8,10},{9,11},{10,... | collective-permute-start | bytes 196616 | tf_op jit(solution)/shard_map/ppermute | solution.py:204
  5.6 13.3 %copy-start = (bf16[512,1024]{1,0:T(8,128)(2,1)S(1)}, bf16[512,1024]{1,0:T(8,128)(2,1)}, u32[]{:S(2)}) copy-start(bf16[512,1024]{1,0:T(8,128)(2,1)} %amp_ref.1) | copy-start | bytes 3145732

commit v22 on v21

--- a/solution.py
+++ b/solution.py
@@ -36,7 +36,7 @@
     places = []
     for chip in chip_order(wide_count):
         if chip == 0 and wide_count <= UNROLL:
-            places += [(core, z) for core in cores for z in range(near_count)]
+            places += [(core, z) for core in reversed(cores) for z in depths]
         else:
             places += [(chip * CORES + core, z) for z in depths for core in cores]
     return places

time: 20.4 us -> 20.1 us (0.985)
  blocking collectives: 10.8 us -> 10.4 us
    all_to_all x1, blocking collectives: 10.8 us -> 10.4 us  [shards(): lax.all_to_all(send.reshape(message_count, length // PAIR, PAIR, width),...]
where the time goes in v22:
time: 20.1 us; the launch traced here: 19.9 us
  blocking collectives  10.4 us (52%)
  starting transfers between devices  4.04 us (20%)
  Pallas kernels  2.43 us (12%)
  waiting for transfers between devices  2.3 us (11%)
  between operations  0.68 us (3%)
    all_to_all x1, blocking collectives, shards(): lax.all_to_all(send.reshape(message_count, length // PAIR, PAIR, width),...  10.4 us
    ppermute x1, starting transfers between devices, shards(): far = lax.ppermute(integrals, 'narrow', across)  4.04 us
    ppermute x1, waiting for transfers between devices, shards(): far = lax.ppermute(integrals, 'narrow', across)  2.3 us
    pallas_call x1, Pallas kernels, shards(): pl.pallas_call(functools.partial(ladder_kernel, rows, near_count, own_cou...  1.32 us
    pallas_call x1, Pallas kernels, shards(): pl.pallas_call(functools.partial(route_kernel, own_count, wide_count), ou...  0.89 us
  transfers between devices with their start and end apart: 1, of which 1 were waited for; matrix products, arithmetic and copies ran while one was open for 0% of the time, Pallas kernels for 4%

profile of v22, /device:TPU:0, one launch (start us, length us, event | category | flops | bytes accessed | tf_op | source)
XLA Modules:
  0.0 19.9 jit_solution(10440624946833215817)
XLA Ops:
  0.0 4.0 %collective-permute-start = (bf16[8,32,128]{2,1,0:T(8,128)(2,1)}, bf16[8,32,128]{2,1,0:T(8,128)(2,1)S(1)}, u32[]{:S(2)}, u32[]{:S(2)}) collective-permute-start(bf16[8,32,128]{2,1,0:T(8,128)(2,1)} %refs_4_.1), channel_id=1, source_target_pairs={{0,2},{1,3},{2,0},{3,1},{4,6},{5,7},{6,4},{7,5},{8,10},{9,11},{10,... | collective-permute-start | bytes 196616 | tf_op jit(solution)/shard_map/ppermute | solution.py:204
  4.7 0.9 %route.1 = (bf16[256,256]{1,0:T(8,128)(2,1)S(1)}, bf16[8,128]{1,0:T(8,128)(2,1)S(1)}, bf16[8,32,128]{2,1,0:T(8,128)(2,1)S(1)}) custom-call(s32[8]{0:T(128)} %refs_0_.1, s32[1]{0:T(128)S(6)} %copy.7.refs_1_, s32[8]{0:T(128)} %refs_2_.1, s32[16]{0:T(128)} %refs_3_.1, bf16[8,32,128]{2,1,0:T(8,128)(2,1)} %refs_4_.1), custom_call_target="tpu_custom_call" | custom-call | flops 1073741824 | bytes 1048576 | tf_op jit(solution)/shard_map/route/pallas_call | solution.py:211
  5.6 0.0 copy-start
  5.6 2.3 %collective-permute-done.far_ref = bf16[8,32,128]{2,1,0:T(8,128)(2,1)S(1)} collective-permute-done((bf16[8,32,128]{2,1,0:T(8,128)(2,1)}, bf16[8,32,128]{2,1,0:T(8,128)(2,1)S(1)}, u32[]{:S(2)}, u32[]{:S(2)}) %collective-permute-start) | collective-permute-done | bytes 65568 | tf_op jit(solution)/shard_map/ppermute | solution.py:204
  7.9 0.2 %pack.1 = bf16[1056,128]{1,0:T(8,128)(2,1)S(1)} custom-call(bf16[256,256]{1,0:T(8,128)(2,1)S(1)} %get-tuple-element.8.order_ref, bf16[8,128]{1,0:T(8,128)(2,1)S(1)} %get-tuple-element.9.label_ref, bf16[8,32,128]{2,1,0:T(8,128)(2,1)S(1)} %get-tuple-element.10.near_ref, bf16[8,32,128]{2,1,0:T(8,128)(2,1)S(1)} %collective-permute-done.far_ref), custom_call_target="tpu_custom_call" | custom-call | tf_op jit(solution)/shard_map/pack/pallas_call | solution.py:226
  8.1 10.4 %all_to_all.5 = bf16[16,33,2,128]{3,2,1,0:T(2,128)(2,1)S(1)} all-to-all(bf16[16,33,2,128]{3,2,1,0:T(2,128)(2,1)S(1)} %bitcast.3), channel_id=1, replica_groups={{17,21,16,20,9,13,8,12,25,29,24,28,5,4,1,0},{19,23,18,22,11,15,10,14,27..., dimensions={0} | all-to-all | bytes 540672 | tf_op jit(solution)/shard_map/all_to_all | solution.py:242
  18.6 0.0 copy-done
  18.6 1.3 %ladder.1 = f32[512,256]{1,0:T(8,128)} custom-call(bf16[512,1024]{1,0:T(8,128)(2,1)S(1)} %copy-done, bf16[1056,128]{1,0:T(8,128)(2,1)S(1)} %bitcast.2), custom_call_target="tpu_custom_call" | custom-call | tf_op jit(solution)/shard_map/ladder/pallas_call | solution.py:250
Async XLA Ops:
  0.0 7.9 %collective-permute-start = (bf16[8,32,128]{2,1,0:T(8,128)(2,1)}, bf16[8,32,128]{2,1,0:T(8,128)(2,1)S(1)}, u32[]{:S(2)}, u32[]{:S(2)}) collective-permute-start(bf16[8,32,128]{2,1,0:T(8,128)(2,1)} %refs_4_.1), channel_id=1, source_target_pairs={{0,2},{1,3},{2,0},{3,1},{4,6},{5,7},{6,4},{7,5},{8,10},{9,11},{10,... | collective-permute-start | bytes 196616 | tf_op jit(solution)/shard_map/ppermute | solution.py:204
  5.6 13.0 %copy-start = (bf16[512,1024]{1,0:T(8,128)(2,1)S(1)}, bf16[512,1024]{1,0:T(8,128)(2,1)}, u32[]{:S(2)}) copy-start(bf16[512,1024]{1,0:T(8,128)(2,1)} %amp_ref.1) | copy-start | bytes 3145732

commit v23 on v19

--- a/solution.py
+++ b/solution.py
@@ -33,13 +33,13 @@
 def group_places(wide_count, near_count):
     depths = list(reversed(range(near_count)))
     cores = range(CORES)
-    return [(chip * CORES + core, z) for chip in chip_order(wide_count) for z in depths for core in cores]
+    return [(chip * CORES + core, z) for chip in chip_order(wide_count) for core in cores for z in depths]
 
 
 def message_at(w, z, wide_count, near_count, length):
     if isinstance(w, int):
         return group_places(wide_count, near_count).index((w, z)) * length
-    place = (w // CORES * near_count + near_count - 1 - z) * CORES + w % CORES
+    place = w * near_count + near_count - 1 - z
     return pl.multiple_of(place * length, length)
 
 

time: 19.6 us -> 20.1 us (1.026)
  blocking collectives: 9.92 us -> 10.5 us
    all_to_all x1, blocking collectives: 9.92 us -> 10.5 us  [shards(): lax.all_to_all(send.reshape(message_count, length // PAIR, PAIR, width),...]
  transfers between devices with their start and end apart: 1 -> 1, of which waited for: 1 -> 1; matrix products, arithmetic and copies ran while one was open for 0% -> 0% of each run, Pallas kernels for 5% -> 4%
where the time goes in v23:
time: 20.1 us; the launch traced here: 19.9 us
  blocking collectives  10.5 us (52%)
  starting transfers between devices  4.04 us (20%)
  Pallas kernels  2.43 us (12%)
  waiting for transfers between devices  2.3 us (11%)
  between operations  0.68 us (3%)
    all_to_all x1, blocking collectives, shards(): lax.all_to_all(send.reshape(message_count, length // PAIR, PAIR, width),...  10.5 us
    ppermute x1, starting transfers between devices, shards(): far = lax.ppermute(integrals, 'narrow', across)  4.04 us
    ppermute x1, waiting for transfers between devices, shards(): far = lax.ppermute(integrals, 'narrow', across)  2.3 us
    pallas_call x1, Pallas kernels, shards(): pl.pallas_call(functools.partial(ladder_kernel, rows, near_count, own_cou...  1.32 us
    pallas_call x1, Pallas kernels, shards(): pl.pallas_call(functools.partial(route_kernel, own_count, wide_count), ou...  0.89 us
  transfers between devices with their start and end apart: 1, of which 1 were waited for; matrix products, arithmetic and copies ran while one was open for 0% of the time, Pallas kernels for 4%

profile of v23, /device:TPU:0, one launch (start us, length us, event | category | flops | bytes accessed | tf_op | source)
XLA Modules:
  0.0 19.9 jit_solution(13968739365687385141)
XLA Ops:
  0.0 4.0 %collective-permute-start = (bf16[8,32,128]{2,1,0:T(8,128)(2,1)}, bf16[8,32,128]{2,1,0:T(8,128)(2,1)S(1)}, u32[]{:S(2)}, u32[]{:S(2)}) collective-permute-start(bf16[8,32,128]{2,1,0:T(8,128)(2,1)} %refs_4_.1), channel_id=1, source_target_pairs={{0,2},{1,3},{2,0},{3,1},{4,6},{5,7},{6,4},{7,5},{8,10},{9,11},{10,... | collective-permute-start | bytes 196616 | tf_op jit(solution)/shard_map/ppermute | solution.py:198
  4.7 0.9 %route.1 = (bf16[256,256]{1,0:T(8,128)(2,1)S(1)}, bf16[8,128]{1,0:T(8,128)(2,1)S(1)}, bf16[8,32,128]{2,1,0:T(8,128)(2,1)S(1)}) custom-call(s32[8]{0:T(128)} %refs_0_.1, s32[1]{0:T(128)S(6)} %copy.7.refs_1_, s32[8]{0:T(128)} %refs_2_.1, s32[16]{0:T(128)} %refs_3_.1, bf16[8,32,128]{2,1,0:T(8,128)(2,1)} %refs_4_.1), custom_call_target="tpu_custom_call" | custom-call | flops 1073741824 | bytes 1048576 | tf_op jit(solution)/shard_map/route/pallas_call | solution.py:205
  5.6 0.0 copy-start
  5.6 2.3 %collective-permute-done.far_ref = bf16[8,32,128]{2,1,0:T(8,128)(2,1)S(1)} collective-permute-done((bf16[8,32,128]{2,1,0:T(8,128)(2,1)}, bf16[8,32,128]{2,1,0:T(8,128)(2,1)S(1)}, u32[]{:S(2)}, u32[]{:S(2)}) %collective-permute-start) | collective-permute-done | bytes 65568 | tf_op jit(solution)/shard_map/ppermute | solution.py:198
  7.9 0.2 %pack.1 = bf16[1056,128]{1,0:T(8,128)(2,1)S(1)} custom-call(bf16[256,256]{1,0:T(8,128)(2,1)S(1)} %get-tuple-element.8.order_ref, bf16[8,128]{1,0:T(8,128)(2,1)S(1)} %get-tuple-element.9.label_ref, bf16[8,32,128]{2,1,0:T(8,128)(2,1)S(1)} %get-tuple-element.10.near_ref, bf16[8,32,128]{2,1,0:T(8,128)(2,1)S(1)} %collective-permute-done.far_ref), custom_call_target="tpu_custom_call" | custom-call | tf_op jit(solution)/shard_map/pack/pallas_call | solution.py:220
  8.1 10.5 %all_to_all.5 = bf16[16,33,2,128]{3,2,1,0:T(2,128)(2,1)S(1)} all-to-all(bf16[16,33,2,128]{3,2,1,0:T(2,128)(2,1)S(1)} %bitcast.3), channel_id=1, replica_groups={{17,16,21,20,9,8,13,12,25,24,29,28,1,0,5,4},{19,18,23,22,11,10,15,14,27..., dimensions={0} | all-to-all | bytes 540672 | tf_op jit(solution)/shard_map/all_to_all | solution.py:236
  18.6 0.0 copy-done
  18.6 1.3 %ladder.1 = f32[512,256]{1,0:T(8,128)} custom-call(bf16[512,1024]{1,0:T(8,128)(2,1)S(1)} %copy-done, bf16[1056,128]{1,0:T(8,128)(2,1)S(1)} %bitcast.2), custom_call_target="tpu_custom_call" | custom-call | tf_op jit(solution)/shard_map/ladder/pallas_call | solution.py:244
Async XLA Ops:
  0.0 7.9 %collective-permute-start = (bf16[8,32,128]{2,1,0:T(8,128)(2,1)}, bf16[8,32,128]{2,1,0:T(8,128)(2,1)S(1)}, u32[]{:S(2)}, u32[]{:S(2)}) collective-permute-start(bf16[8,32,128]{2,1,0:T(8,128)(2,1)} %refs_4_.1), channel_id=1, source_target_pairs={{0,2},{1,3},{2,0},{3,1},{4,6},{5,7},{6,4},{7,5},{8,10},{9,11},{10,... | collective-permute-start | bytes 196616 | tf_op jit(solution)/shard_map/ppermute | solution.py:198
  5.6 13.0 %copy-start = (bf16[512,1024]{1,0:T(8,128)(2,1)S(1)}, bf16[512,1024]{1,0:T(8,128)(2,1)}, u32[]{:S(2)}) copy-start(bf16[512,1024]{1,0:T(8,128)(2,1)} %amp_ref.1) | copy-start | bytes 3145732

commit v24 on v23

--- a/solution.py
+++ b/solution.py
@@ -31,15 +31,15 @@
 
 
 def group_places(wide_count, near_count):
-    depths = list(reversed(range(near_count)))
     cores = range(CORES)
+    depths = range(near_count)
     return [(chip * CORES + core, z) for chip in chip_order(wide_count) for core in cores for z in depths]
 
 
 def message_at(w, z, wide_count, near_count, length):
     if isinstance(w, int):
         return group_places(wide_count, near_count).index((w, z)) * length
-    place = w * near_count + near_count - 1 - z
+    place = w * near_count + z
     return pl.multiple_of(place * length, length)
 
 

time: 20.1 us -> 19.5 us (0.970)
  blocking collectives: 10.5 us -> 9.87 us
    all_to_all x1, blocking collectives: 10.5 us -> 9.87 us  [shards(): lax.all_to_all(send.reshape(message_count, length // PAIR, PAIR, width),...]
  transfers between devices with their start and end apart: 1 -> 1, of which waited for: 1 -> 1; matrix products, arithmetic and copies ran while one was open for 0% -> 0% of each run, Pallas kernels for 4% -> 5%
where the time goes in v24:
time: 19.5 us; the launch traced here: 19.3 us
  blocking collectives  9.87 us (51%)
  starting transfers between devices  4.04 us (21%)
  Pallas kernels  2.43 us (12%)
  waiting for transfers between devices  2.3 us (12%)
  between operations  0.68 us (3%)
    all_to_all x1, blocking collectives, shards(): lax.all_to_all(send.reshape(message_count, length // PAIR, PAIR, width),...  9.87 us
    ppermute x1, starting transfers between devices, shards(): far = lax.ppermute(integrals, 'narrow', across)  4.04 us
    ppermute x1, waiting for transfers between devices, shards(): far = lax.ppermute(integrals, 'narrow', across)  2.3 us
    pallas_call x1, Pallas kernels, shards(): pl.pallas_call(functools.partial(ladder_kernel, rows, near_count, own_cou...  1.32 us
    pallas_call x1, Pallas kernels, shards(): pl.pallas_call(functools.partial(route_kernel, own_count, wide_count), ou...  0.89 us
  transfers between devices with their start and end apart: 1, of which 1 were waited for; matrix products, arithmetic and copies ran while one was open for 0% of the time, Pallas kernels for 5%

profile of v24, /device:TPU:0, one launch (start us, length us, event | category | flops | bytes accessed | tf_op | source)
XLA Modules:
  0.0 19.3 jit_solution(12166461289168133650)
XLA Ops:
  0.0 4.0 %collective-permute-start = (bf16[8,32,128]{2,1,0:T(8,128)(2,1)}, bf16[8,32,128]{2,1,0:T(8,128)(2,1)S(1)}, u32[]{:S(2)}, u32[]{:S(2)}) collective-permute-start(bf16[8,32,128]{2,1,0:T(8,128)(2,1)} %refs_4_.1), channel_id=1, source_target_pairs={{0,2},{1,3},{2,0},{3,1},{4,6},{5,7},{6,4},{7,5},{8,10},{9,11},{10,... | collective-permute-start | bytes 196616 | tf_op jit(solution)/shard_map/ppermute | solution.py:198
  4.7 0.9 %route.1 = (bf16[256,256]{1,0:T(8,128)(2,1)S(1)}, bf16[8,128]{1,0:T(8,128)(2,1)S(1)}, bf16[8,32,128]{2,1,0:T(8,128)(2,1)S(1)}) custom-call(s32[8]{0:T(128)} %refs_0_.1, s32[1]{0:T(128)S(6)} %copy.7.refs_1_, s32[8]{0:T(128)} %refs_2_.1, s32[16]{0:T(128)} %refs_3_.1, bf16[8,32,128]{2,1,0:T(8,128)(2,1)} %refs_4_.1), custom_call_target="tpu_custom_call" | custom-call | flops 1073741824 | bytes 1048576 | tf_op jit(solution)/shard_map/route/pallas_call | solution.py:205
  5.6 0.0 copy-start
  5.6 2.3 %collective-permute-done.far_ref = bf16[8,32,128]{2,1,0:T(8,128)(2,1)S(1)} collective-permute-done((bf16[8,32,128]{2,1,0:T(8,128)(2,1)}, bf16[8,32,128]{2,1,0:T(8,128)(2,1)S(1)}, u32[]{:S(2)}, u32[]{:S(2)}) %collective-permute-start) | collective-permute-done | bytes 65568 | tf_op jit(solution)/shard_map/ppermute | solution.py:198
  7.9 0.2 %pack.1 = bf16[1056,128]{1,0:T(8,128)(2,1)S(1)} custom-call(bf16[256,256]{1,0:T(8,128)(2,1)S(1)} %get-tuple-element.8.order_ref, bf16[8,128]{1,0:T(8,128)(2,1)S(1)} %get-tuple-element.9.label_ref, bf16[8,32,128]{2,1,0:T(8,128)(2,1)S(1)} %get-tuple-element.10.near_ref, bf16[8,32,128]{2,1,0:T(8,128)(2,1)S(1)} %collective-permute-done.far_ref), custom_call_target="tpu_custom_call" | custom-call | tf_op jit(solution)/shard_map/pack/pallas_call | solution.py:220
  8.1 9.9 %all_to_all.5 = bf16[16,33,2,128]{3,2,1,0:T(2,128)(2,1)S(1)} all-to-all(bf16[16,33,2,128]{3,2,1,0:T(2,128)(2,1)S(1)} %bitcast.3), channel_id=1, replica_groups={{16,17,20,21,8,9,12,13,24,25,28,29,0,1,4,5},{18,19,22,23,10,11,14,15,26..., dimensions={0} | all-to-all | bytes 540672 | tf_op jit(solution)/shard_map/all_to_all | solution.py:236
  18.0 0.0 copy-done
  18.0 1.3 %ladder.1 = f32[512,256]{1,0:T(8,128)} custom-call(bf16[512,1024]{1,0:T(8,128)(2,1)S(1)} %copy-done, bf16[1056,128]{1,0:T(8,128)(2,1)S(1)} %bitcast.2), custom_call_target="tpu_custom_call" | custom-call | tf_op jit(solution)/shard_map/ladder/pallas_call | solution.py:244
Async XLA Ops:
  0.0 7.9 %collective-permute-start = (bf16[8,32,128]{2,1,0:T(8,128)(2,1)}, bf16[8,32,128]{2,1,0:T(8,128)(2,1)S(1)}, u32[]{:S(2)}, u32[]{:S(2)}) collective-permute-start(bf16[8,32,128]{2,1,0:T(8,128)(2,1)} %refs_4_.1), channel_id=1, source_target_pairs={{0,2},{1,3},{2,0},{3,1},{4,6},{5,7},{6,4},{7,5},{8,10},{9,11},{10,... | collective-permute-start | bytes 196616 | tf_op jit(solution)/shard_map/ppermute | solution.py:198
  5.6 12.4 %copy-start = (bf16[512,1024]{1,0:T(8,128)(2,1)S(1)}, bf16[512,1024]{1,0:T(8,128)(2,1)}, u32[]{:S(2)}) copy-start(bf16[512,1024]{1,0:T(8,128)(2,1)} %amp_ref.1) | copy-start | bytes 3145732

commit v25 on v24

--- a/solution.py
+++ b/solution.py
@@ -116,7 +116,9 @@
     wide_count = seen.shape[0]
     width = got_ref.shape[1]
     length = got_ref.shape[0] // (wide_count * near_count)
-    upper = lax.axis_index("narrow") >= near_count
+    half_size = near_count * rows
+    upper = (lax.axis_index("narrow") >= near_count).astype(jnp.int32)
+    near_at, far_at = upper * half_size, (1 - upper) * half_size
     tiles[...] = jnp.zeros_like(tiles)
     for u in range(recv_count):
         column[u] = 0
@@ -138,19 +140,15 @@
 
     def keep(w, label, found):
         live = jnp.minimum(label, 1)
-        at = jnp.minimum(found, recv_count)
-        place = jnp.maximum(label - 1, 0)
-        column[at] = lax.div(place, own_count)
-        spot = lax.rem(place, own_count)
+        at = jnp.where(label > 0, jnp.minimum(found, recv_count), recv_count)
+        code = jnp.maximum(label - 1, 0)
+        column[at] = lax.div(code, own_count)
+        spot = pl.ds(pl.multiple_of(lax.rem(code, own_count) * width, width), width)
         parts = [message(w, z) for z in range(near_count)]
-        near = jnp.concatenate([part[0] for part in parts], axis=0).astype(tiles.dtype)
-        far = jnp.concatenate([part[1] for part in parts], axis=0).astype(tiles.dtype)
-        halves = [jnp.where(upper, far, near), jnp.where(upper, near, far)]
-        tile = jnp.concatenate(halves, axis=0)
-        at = pl.multiple_of(at * width, width)
-        for q in range(own_count):
-            kept = jnp.where((live > 0) & (spot == q), tile, jnp.zeros_like(tile))
-            tiles[pl.ds(at, width), q * width : (q + 1) * width] = kept
+        for side in range(2):
+            half = jnp.concatenate([part[side] for part in parts], axis=0).astype(tiles.dtype)
+            start = at * width + (near_at if side == 0 else far_at)
+            tiles[pl.ds(pl.multiple_of(start, half_size), half_size), spot] = half
         return found + live
 
     if wide_count <= UNROLL:

time: 19.5 us -> 19.5 us (level)
  no operation moved by 1% of the time
where the time goes in v25:
time: 19.5 us; the launch traced here: 19.3 us
  blocking collectives  9.87 us (51%)
  starting transfers between devices  4.04 us (21%)
  Pallas kernels  2.42 us (12%)
  waiting for transfers between devices  2.3 us (12%)
  between operations  0.68 us (3%)
    all_to_all x1, blocking collectives, shards(): lax.all_to_all(send.reshape(message_count, length // PAIR, PAIR, width),...  9.87 us
    ppermute x1, starting transfers between devices, shards(): far = lax.ppermute(integrals, 'narrow', across)  4.04 us
    ppermute x1, waiting for transfers between devices, shards(): far = lax.ppermute(integrals, 'narrow', across)  2.3 us
    pallas_call x1, Pallas kernels, shards(): pl.pallas_call(functools.partial(ladder_kernel, rows, near_count, own_cou...  1.3 us
    pallas_call x1, Pallas kernels, shards(): pl.pallas_call(functools.partial(route_kernel, own_count, wide_count), ou...  0.89 us
  transfers between devices with their start and end apart: 1, of which 1 were waited for; matrix products, arithmetic and copies ran while one was open for 0% of the time, Pallas kernels for 5%

profile of v25, /device:TPU:0, one launch (start us, length us, event | category | flops | bytes accessed | tf_op | source)
XLA Modules:
  0.0 19.3 jit_solution(15762212234909161030)
XLA Ops:
  0.0 4.0 %collective-permute-start = (bf16[8,32,128]{2,1,0:T(8,128)(2,1)}, bf16[8,32,128]{2,1,0:T(8,128)(2,1)S(1)}, u32[]{:S(2)}, u32[]{:S(2)}) collective-permute-start(bf16[8,32,128]{2,1,0:T(8,128)(2,1)} %refs_4_.1), channel_id=1, source_target_pairs={{0,2},{1,3},{2,0},{3,1},{4,6},{5,7},{6,4},{7,5},{8,10},{9,11},{10,... | collective-permute-start | bytes 196616 | tf_op jit(solution)/shard_map/ppermute | solution.py:196
  4.7 0.9 %route.1 = (bf16[256,256]{1,0:T(8,128)(2,1)S(1)}, bf16[8,128]{1,0:T(8,128)(2,1)S(1)}, bf16[8,32,128]{2,1,0:T(8,128)(2,1)S(1)}) custom-call(s32[8]{0:T(128)} %refs_0_.1, s32[1]{0:T(128)S(6)} %copy.7.refs_1_, s32[8]{0:T(128)} %refs_2_.1, s32[16]{0:T(128)} %refs_3_.1, bf16[8,32,128]{2,1,0:T(8,128)(2,1)} %refs_4_.1), custom_call_target="tpu_custom_call" | custom-call | flops 1073741824 | bytes 1048576 | tf_op jit(solution)/shard_map/route/pallas_call | solution.py:203
  5.6 0.0 copy-start
  5.6 2.3 %collective-permute-done.far_ref = bf16[8,32,128]{2,1,0:T(8,128)(2,1)S(1)} collective-permute-done((bf16[8,32,128]{2,1,0:T(8,128)(2,1)}, bf16[8,32,128]{2,1,0:T(8,128)(2,1)S(1)}, u32[]{:S(2)}, u32[]{:S(2)}) %collective-permute-start) | collective-permute-done | bytes 65568 | tf_op jit(solution)/shard_map/ppermute | solution.py:196
  7.9 0.2 %pack.1 = bf16[1056,128]{1,0:T(8,128)(2,1)S(1)} custom-call(bf16[256,256]{1,0:T(8,128)(2,1)S(1)} %get-tuple-element.8.order_ref, bf16[8,128]{1,0:T(8,128)(2,1)S(1)} %get-tuple-element.9.label_ref, bf16[8,32,128]{2,1,0:T(8,128)(2,1)S(1)} %get-tuple-element.10.near_ref, bf16[8,32,128]{2,1,0:T(8,128)(2,1)S(1)} %collective-permute-done.far_ref), custom_call_target="tpu_custom_call" | custom-call | tf_op jit(solution)/shard_map/pack/pallas_call | solution.py:218
  8.1 9.9 %all_to_all.5 = bf16[16,33,2,128]{3,2,1,0:T(2,128)(2,1)S(1)} all-to-all(bf16[16,33,2,128]{3,2,1,0:T(2,128)(2,1)S(1)} %bitcast.3), channel_id=1, replica_groups={{16,17,20,21,8,9,12,13,24,25,28,29,0,1,4,5},{18,19,22,23,10,11,14,15,26..., dimensions={0} | all-to-all | bytes 540672 | tf_op jit(solution)/shard_map/all_to_all | solution.py:234
  18.0 0.0 copy-done
  18.0 1.3 %ladder.1 = f32[512,256]{1,0:T(8,128)} custom-call(bf16[512,1024]{1,0:T(8,128)(2,1)S(1)} %copy-done, bf16[1056,128]{1,0:T(8,128)(2,1)S(1)} %bitcast.2), custom_call_target="tpu_custom_call" | custom-call | tf_op jit(solution)/shard_map/ladder/pallas_call | solution.py:242
Async XLA Ops:
  0.0 7.9 %collective-permute-start = (bf16[8,32,128]{2,1,0:T(8,128)(2,1)}, bf16[8,32,128]{2,1,0:T(8,128)(2,1)S(1)}, u32[]{:S(2)}, u32[]{:S(2)}) collective-permute-start(bf16[8,32,128]{2,1,0:T(8,128)(2,1)} %refs_4_.1), channel_id=1, source_target_pairs={{0,2},{1,3},{2,0},{3,1},{4,6},{5,7},{6,4},{7,5},{8,10},{9,11},{10,... | collective-permute-start | bytes 196616 | tf_op jit(solution)/shard_map/ppermute | solution.py:196
  5.6 12.4 %copy-start = (bf16[512,1024]{1,0:T(8,128)(2,1)S(1)}, bf16[512,1024]{1,0:T(8,128)(2,1)}, u32[]{:S(2)}) copy-start(bf16[512,1024]{1,0:T(8,128)(2,1)} %amp_ref.1) | copy-start | bytes 3145732

commit v26 on v25

--- a/solution.py
+++ b/solution.py
@@ -186,9 +186,7 @@
     near_count = depth_count // 2
     kind = integrals.dtype
     message_count = wide_count * near_count
-    length = 2 * rows + PAIR
-    if wide_count > UNROLL or length % PAIR != 0 or message_count * length % 16 != 0:
-        length = -(-length // 16) * 16
+    length = -(-(2 * rows + 1) // 16) * 16
     hbm = pl.BlockSpec(memory_space=pltpu.HBM)
     vmem = pl.BlockSpec(memory_space=pltpu.VMEM)
     limit = pltpu.CompilerParams(vmem_limit_bytes=32 * 2**20)

time: 19.5 us -> 20.1 us (1.031)
  blocking collectives: 9.87 us -> 10.5 us
    all_to_all x1, blocking collectives: 9.87 us -> 10.5 us  [shards(): lax.all_to_all(send.reshape(message_count, length // PAIR, PAIR, width),...]
  transfers between devices with their start and end apart: 1 -> 1, of which waited for: 1 -> 1; matrix products, arithmetic and copies ran while one was open for 0% -> 0% of each run, Pallas kernels for 5% -> 4%
where the time goes in v26:
time: 20.1 us; the launch traced here: 19.9 us
  blocking collectives  10.5 us (52%)
  starting transfers between devices  4.04 us (20%)
  Pallas kernels  2.39 us (12%)
  waiting for transfers between devices  2.3 us (11%)
  between operations  0.68 us (3%)
    all_to_all x1, blocking collectives, shards(): lax.all_to_all(send.reshape(message_count, length // PAIR, PAIR, width),...  10.5 us
    ppermute x1, starting transfers between devices, shards(): far = lax.ppermute(integrals, 'narrow', across)  4.04 us
    ppermute x1, waiting for transfers between devices, shards(): far = lax.ppermute(integrals, 'narrow', across)  2.3 us
    pallas_call x1, Pallas kernels, shards(): pl.pallas_call(functools.partial(ladder_kernel, rows, near_count, own_cou...  1.3 us
    pallas_call x1, Pallas kernels, shards(): pl.pallas_call(functools.partial(route_kernel, own_count, wide_count), ou...  0.89 us
  transfers between devices with their start and end apart: 1, of which 1 were waited for; matrix products, arithmetic and copies ran while one was open for 0% of the time, Pallas kernels for 4%

profile of v26, /device:TPU:0, one launch (start us, length us, event | category | flops | bytes accessed | tf_op | source)
XLA Modules:
  0.0 19.9 jit_solution(11631935799426049312)
XLA Ops:
  0.0 4.0 %collective-permute-start = (bf16[8,32,128]{2,1,0:T(8,128)(2,1)}, bf16[8,32,128]{2,1,0:T(8,128)(2,1)S(1)}, u32[]{:S(2)}, u32[]{:S(2)}) collective-permute-start(bf16[8,32,128]{2,1,0:T(8,128)(2,1)} %refs_4_.1), channel_id=1, source_target_pairs={{0,2},{1,3},{2,0},{3,1},{4,6},{5,7},{6,4},{7,5},{8,10},{9,11},{10,... | collective-permute-start | bytes 196616 | tf_op jit(solution)/shard_map/ppermute | solution.py:194
  4.7 0.9 %route.1 = (bf16[256,256]{1,0:T(8,128)(2,1)S(1)}, bf16[8,128]{1,0:T(8,128)(2,1)S(1)}, bf16[8,32,128]{2,1,0:T(8,128)(2,1)S(1)}) custom-call(s32[8]{0:T(128)} %refs_0_.1, s32[1]{0:T(128)S(6)} %copy.7.refs_1_, s32[8]{0:T(128)} %refs_2_.1, s32[16]{0:T(128)} %refs_3_.1, bf16[8,32,128]{2,1,0:T(8,128)(2,1)} %refs_4_.1), custom_call_target="tpu_custom_call" | custom-call | flops 1073741824 | bytes 1048576 | tf_op jit(solution)/shard_map/route/pallas_call | solution.py:201
  5.6 0.0 copy-start
  5.6 2.3 %collective-permute-done.far_ref = bf16[8,32,128]{2,1,0:T(8,128)(2,1)S(1)} collective-permute-done((bf16[8,32,128]{2,1,0:T(8,128)(2,1)}, bf16[8,32,128]{2,1,0:T(8,128)(2,1)S(1)}, u32[]{:S(2)}, u32[]{:S(2)}) %collective-permute-start) | collective-permute-done | bytes 65568 | tf_op jit(solution)/shard_map/ppermute | solution.py:194
  7.9 0.2 %pack.1 = bf16[1280,128]{1,0:T(8,128)(2,1)S(1)} custom-call(bf16[256,256]{1,0:T(8,128)(2,1)S(1)} %get-tuple-element.8.order_ref, bf16[8,128]{1,0:T(8,128)(2,1)S(1)} %get-tuple-element.9.label_ref, bf16[8,32,128]{2,1,0:T(8,128)(2,1)S(1)} %get-tuple-element.10.near_ref, bf16[8,32,128]{2,1,0:T(8,128)(2,1)S(1)} %collective-permute-done.far_ref), custom_call_target="tpu_custom_call" | custom-call | tf_op jit(solution)/shard_map/pack/pallas_call | solution.py:216
  8.1 10.5 %all_to_all.5 = bf16[16,40,2,128]{3,2,1,0:T(2,128)(2,1)S(1)} all-to-all(bf16[16,40,2,128]{3,2,1,0:T(2,128)(2,1)S(1)} %bitcast.2), channel_id=1, replica_groups={{16,17,20,21,8,9,12,13,24,25,28,29,0,1,4,5},{18,19,22,23,10,11,14,15,26..., dimensions={0} | all-to-all | bytes 655360 | tf_op jit(solution)/shard_map/all_to_all | solution.py:232
  18.6 0.0 copy-done
  18.6 1.3 %ladder.1 = f32[512,256]{1,0:T(8,128)} custom-call(bf16[512,1024]{1,0:T(8,128)(2,1)S(1)} %copy-done, bf16[1280,128]{1,0:T(8,128)(2,1)S(1)} %bitcast.3), custom_call_target="tpu_custom_call" | custom-call | tf_op jit(solution)/shard_map/ladder/pallas_call | solution.py:240
Async XLA Ops:
  0.0 7.9 %collective-permute-start = (bf16[8,32,128]{2,1,0:T(8,128)(2,1)}, bf16[8,32,128]{2,1,0:T(8,128)(2,1)S(1)}, u32[]{:S(2)}, u32[]{:S(2)}) collective-permute-start(bf16[8,32,128]{2,1,0:T(8,128)(2,1)} %refs_4_.1), channel_id=1, source_target_pairs={{0,2},{1,3},{2,0},{3,1},{4,6},{5,7},{6,4},{7,5},{8,10},{9,11},{10,... | collective-permute-start | bytes 196616 | tf_op jit(solution)/shard_map/ppermute | solution.py:194
  5.6 13.0 %copy-start = (bf16[512,1024]{1,0:T(8,128)(2,1)S(1)}, bf16[512,1024]{1,0:T(8,128)(2,1)}, u32[]{:S(2)}) copy-start(bf16[512,1024]{1,0:T(8,128)(2,1)} %amp_ref.1) | copy-start | bytes 3145732

commit v27 on v25

--- a/solution.py
+++ b/solution.py
@@ -25,9 +25,9 @@
     chip_count = wide_count // CORES
     if wide_count > UNROLL:
         return list(range(chip_count))
-    bits = (chip_count - 1).bit_length()
-    flipped = [int(format(chip, "b").zfill(bits)[::-1], 2) for chip in range(2**bits)]
-    return [chip for chip in flipped[1:] if chip < chip_count] + [0]
+    size = 2 ** (chip_count - 1).bit_length()
+    ring = [step ^ (step >> 1) for step in range(1, size)]
+    return [chip for chip in ring if chip < chip_count] + [0]
 
 
 def group_places(wide_count, near_count):

time: 19.5 us -> 19.5 us (level)
  no operation moved by 1% of the time
where the time goes in v27:
time: 19.5 us; the launch traced here: 19.3 us
  blocking collectives  9.87 us (51%)
  starting transfers between devices  4.04 us (21%)
  Pallas kernels  2.42 us (12%)
  waiting for transfers between devices  2.3 us (12%)
  between operations  0.68 us (3%)
    all_to_all x1, blocking collectives, shards(): lax.all_to_all(send.reshape(message_count, length // PAIR, PAIR, width),...  9.87 us
    ppermute x1, starting transfers between devices, shards(): far = lax.ppermute(integrals, 'narrow', across)  4.04 us
    ppermute x1, waiting for transfers between devices, shards(): far = lax.ppermute(integrals, 'narrow', across)  2.3 us
    pallas_call x1, Pallas kernels, shards(): pl.pallas_call(functools.partial(ladder_kernel, rows, near_count, own_cou...  1.3 us
    pallas_call x1, Pallas kernels, shards(): pl.pallas_call(functools.partial(route_kernel, own_count, wide_count), ou...  0.89 us
  transfers between devices with their start and end apart: 1, of which 1 were waited for; matrix products, arithmetic and copies ran while one was open for 0% of the time, Pallas kernels for 5%

profile of v27, /device:TPU:0, one launch (start us, length us, event | category | flops | bytes accessed | tf_op | source)
XLA Modules:
  0.0 19.3 jit_solution(15612395958024105128)
XLA Ops:
  0.0 4.0 %collective-permute-start = (bf16[8,32,128]{2,1,0:T(8,128)(2,1)}, bf16[8,32,128]{2,1,0:T(8,128)(2,1)S(1)}, u32[]{:S(2)}, u32[]{:S(2)}) collective-permute-start(bf16[8,32,128]{2,1,0:T(8,128)(2,1)} %refs_4_.1), channel_id=1, source_target_pairs={{0,2},{1,3},{2,0},{3,1},{4,6},{5,7},{6,4},{7,5},{8,10},{9,11},{10,... | collective-permute-start | bytes 196616 | tf_op jit(solution)/shard_map/ppermute | solution.py:196
  4.7 0.9 %route.1 = (bf16[256,256]{1,0:T(8,128)(2,1)S(1)}, bf16[8,128]{1,0:T(8,128)(2,1)S(1)}, bf16[8,32,128]{2,1,0:T(8,128)(2,1)S(1)}) custom-call(s32[8]{0:T(128)} %refs_0_.1, s32[1]{0:T(128)S(6)} %copy.7.refs_1_, s32[8]{0:T(128)} %refs_2_.1, s32[16]{0:T(128)} %refs_3_.1, bf16[8,32,128]{2,1,0:T(8,128)(2,1)} %refs_4_.1), custom_call_target="tpu_custom_call" | custom-call | flops 1073741824 | bytes 1048576 | tf_op jit(solution)/shard_map/route/pallas_call | solution.py:203
  5.6 0.0 copy-start
  5.6 2.3 %collective-permute-done.far_ref = bf16[8,32,128]{2,1,0:T(8,128)(2,1)S(1)} collective-permute-done((bf16[8,32,128]{2,1,0:T(8,128)(2,1)}, bf16[8,32,128]{2,1,0:T(8,128)(2,1)S(1)}, u32[]{:S(2)}, u32[]{:S(2)}) %collective-permute-start) | collective-permute-done | bytes 65568 | tf_op jit(solution)/shard_map/ppermute | solution.py:196
  7.9 0.2 %pack.1 = bf16[1056,128]{1,0:T(8,128)(2,1)S(1)} custom-call(bf16[256,256]{1,0:T(8,128)(2,1)S(1)} %get-tuple-element.8.order_ref, bf16[8,128]{1,0:T(8,128)(2,1)S(1)} %get-tuple-element.9.label_ref, bf16[8,32,128]{2,1,0:T(8,128)(2,1)S(1)} %get-tuple-element.10.near_ref, bf16[8,32,128]{2,1,0:T(8,128)(2,1)S(1)} %collective-permute-done.far_ref), custom_call_target="tpu_custom_call" | custom-call | tf_op jit(solution)/shard_map/pack/pallas_call | solution.py:218
  8.1 9.9 %all_to_all.5 = bf16[16,33,2,128]{3,2,1,0:T(2,128)(2,1)S(1)} all-to-all(bf16[16,33,2,128]{3,2,1,0:T(2,128)(2,1)S(1)} %bitcast.3), channel_id=1, replica_groups={{8,9,12,13,24,25,28,29,16,17,20,21,0,1,4,5},{10,11,14,15,26,27,30,31,18..., dimensions={0} | all-to-all | bytes 540672 | tf_op jit(solution)/shard_map/all_to_all | solution.py:234
  18.0 0.0 copy-done
  18.0 1.3 %ladder.1 = f32[512,256]{1,0:T(8,128)} custom-call(bf16[512,1024]{1,0:T(8,128)(2,1)S(1)} %copy-done, bf16[1056,128]{1,0:T(8,128)(2,1)S(1)} %bitcast.2), custom_call_target="tpu_custom_call" | custom-call | tf_op jit(solution)/shard_map/ladder/pallas_call | solution.py:242
Async XLA Ops:
  0.0 7.9 %collective-permute-start = (bf16[8,32,128]{2,1,0:T(8,128)(2,1)}, bf16[8,32,128]{2,1,0:T(8,128)(2,1)S(1)}, u32[]{:S(2)}, u32[]{:S(2)}) collective-permute-start(bf16[8,32,128]{2,1,0:T(8,128)(2,1)} %refs_4_.1), channel_id=1, source_target_pairs={{0,2},{1,3},{2,0},{3,1},{4,6},{5,7},{6,4},{7,5},{8,10},{9,11},{10,... | collective-permute-start | bytes 196616 | tf_op jit(solution)/shard_map/ppermute | solution.py:196
  5.6 12.4 %copy-start = (bf16[512,1024]{1,0:T(8,128)(2,1)S(1)}, bf16[512,1024]{1,0:T(8,128)(2,1)}, u32[]{:S(2)}) copy-start(bf16[512,1024]{1,0:T(8,128)(2,1)} %amp_ref.1) | copy-start | bytes 3145732

commit v28 on v25

--- a/solution.py
+++ b/solution.py
@@ -11,6 +11,7 @@
 GROUP = 4
 UNROLL = 8
 CORES = 2
+PARTS = 2
 
 
 def each(count, body, start):
@@ -43,18 +44,32 @@
     return pl.multiple_of(place * length, length)
 
 
+def stage_kernel(source, *refs):
+    *targets, sems = refs
+    size = targets[0].shape[0]
+    copies = [
+        pltpu.make_async_copy(source.at[pl.ds(i * size, size)], target, sems.at[i])
+        for i, target in enumerate(targets)
+    ]
+    for copy in copies:
+        copy.start()
+    for copy in copies:
+        copy.wait()
+
+
 def route_kernel(own_count, wide_count, *refs):
-    sources, (order_ref, label_ref, near_ref), targets, sems = refs[:5], refs[5:8], refs[8:12], refs[12]
+    sources, (order_ref, label_ref), targets, sems = refs[:4], refs[4:6], refs[6:10], refs[10]
     in_tile, counts, out_tile, owner_map = targets
     copies = [
         pltpu.make_async_copy(source, target, sems.at[i])
-        for i, (source, target) in enumerate(zip(sources, (*targets, near_ref)))
+        for i, (source, target) in enumerate(zip(sources, targets))
     ]
     for copy in copies:
         copy.start()
-    for copy in copies[:4]:
+    for copy in copies:
         copy.wait()
-    slot_count, rows, width = near_ref.shape
+    slot_count = in_tile.shape[0]
+    rows, width = order_ref.shape[0] // wide_count, label_ref.shape[1]
     column = lax.broadcasted_iota(jnp.int32, (1, slot_count * rows), 1)
     owners = lax.broadcasted_iota(jnp.int32, (wide_count, width), 0)
 
@@ -73,18 +88,21 @@
     row = lax.broadcasted_iota(jnp.int32, (wide_count * rows, 1), 0)
     hit = row == owner_of * rows + lax.rem(column, rows)
     order_ref[...] = hit.astype(jnp.float32).astype(order_ref.dtype)
-    copies[4].wait()
-
-
-def pack_kernel(wide_count, near_count, order_ref, label_ref, near_ref, far_ref, send_ref, both, ordered):
-    slot_count, rows, width = near_ref.shape
+
+
+def pack_kernel(wide_count, near_count, order_ref, label_ref, *refs):
+    *given, send_ref, both, ordered = refs
+    part_count = len(given) // 2
+    slots, rows, width = given[0].shape
     length = send_ref.shape[0] // (wide_count * near_count)
-    for side, ref in enumerate((near_ref, far_ref)):
+    for i, ref in enumerate(given):
+        side, part = divmod(i, part_count)
         block = ref[...]
         if rows % 16 != 0:
             block = block.astype(jnp.float32)
-        block = block.reshape(slot_count * rows, width).astype(both.dtype)
-        both[:, side * width : (side + 1) * width] = block
+        block = block.reshape(slots * rows, width).astype(both.dtype)
+        at = slice(part * slots * rows, (part + 1) * slots * rows)
+        both[at, side * width : (side + 1) * width] = block
     ordered[...] = jnp.dot(order_ref[...], both[...], preferred_element_type=jnp.float32)
     labels = label_ref[...].astype(jnp.float32)
     ids = lax.broadcasted_iota(jnp.int32, labels.shape, 0)
@@ -193,23 +211,32 @@
     vmem = pl.BlockSpec(memory_space=pltpu.VMEM)
     limit = pltpu.CompilerParams(vmem_limit_bytes=32 * 2**20)
     across = [(z, (z + near_count) % depth_count) for z in range(depth_count)]
-    far = lax.ppermute(integrals, "narrow", across)
-    given = [in_tile, counts, out_tile, owner_map, integrals]
+    part_shape = jax.ShapeDtypeStruct((slot_count // PARTS, rows, width), kind)
+    near = pl.pallas_call(
+        stage_kernel,
+        out_shape=[part_shape] * PARTS,
+        in_specs=[hbm],
+        out_specs=[vmem] * PARTS,
+        scratch_shapes=[pltpu.SemaphoreType.DMA((PARTS,))],
+        compiler_params=limit,
+        name="stage",
+    )(pltpu.with_memory_space_constraint(integrals, pltpu.HBM))
+    far = [lax.ppermute(part, "narrow", across) for part in near]
+    given = [in_tile, counts, out_tile, owner_map]
     given = [
         value if value.size == 1 else pltpu.with_memory_space_constraint(value, pltpu.HBM)
         for value in given
     ]
     ordered, sent = wide_count * rows, slot_count * rows
-    order, labels, near = pl.pallas_call(
+    order, labels = pl.pallas_call(
         functools.partial(route_kernel, own_count, wide_count),
         out_shape=[
             jax.ShapeDtypeStruct((ordered, sent), kind),
             jax.ShapeDtypeStruct((wide_count, width), kind),
-            jax.ShapeDtypeStruct(integrals.shape, kind),
         ],
         in_specs=[hbm] * len(given),
-        out_specs=[vmem] * 3,
-        scratch_shapes=[pltpu.SMEM(value.shape, value.dtype) for value in given[:-1]]
+        out_specs=[vmem] * 2,
+        scratch_shapes=[pltpu.SMEM(value.shape, value.dtype) for value in given]
         + [pltpu.SemaphoreType.DMA((len(given),))],
         compiler_params=limit,
         cost_estimate=pl.CostEstimate(flops=2**30, bytes_accessed=2**20, transcendentals=0),
@@ -218,7 +245,7 @@
     send = pl.pallas_call(
         functools.partial(pack_kernel, wide_count, near_count),
         out_shape=jax.ShapeDtypeStruct((message_count * length, width), kind),
-        in_specs=[vmem] * 4,
+        in_specs=[vmem] * (2 + 2 * PARTS),
         out_specs=vmem,
         scratch_shapes=[
             pltpu.VMEM((sent, 2 * width), kind),
@@ -226,7 +253,7 @@
         ],
         compiler_params=limit,
         name="pack",
-    )(order, labels, near, far)
+    )(order, labels, *near, *far)
     places = group_places(wide_count, near_count)
     groups = [
         [w * depth_count + half * near_count + z for w, z in places] for half in range(2)

time: 19.5 us -> 22.2 us (1.14)
  waiting for transfers between devices: 2.3 us -> 3.28 us
  blocking collectives: 9.87 us -> 10.7 us
  Pallas kernels: 2.42 us -> 3.1 us
    ppermute x1 -> x2, waiting for transfers between devices: 2.3 us -> 3.28 us  [shards(): far = [lax.ppermute(part, 'narrow', across) for part in near]]
    all_to_all x1, blocking collectives: 9.87 us -> 10.7 us  [shards(): lax.all_to_all(send.reshape(message_count, length // PAIR, PAIR, width),...]
    pallas_call x0 -> x1, Pallas kernels: none -> 0.79 us  [shards(): pl.pallas_call(stage_kernel, out_shape=[part_shape] * PARTS, in_specs=[hb...]
    ppermute x1 -> x2, starting transfers between devices: 4.04 us -> 4.18 us  [shards(): far = [lax.ppermute(part, 'narrow', across) for part in near]]
  transfers between devices with their start and end apart: 1 -> 2, of which waited for: 1 -> 2; matrix products, arithmetic and copies ran while one was open for 0% -> 0% of each run, Pallas kernels for 5% -> 4%
where the time goes in v28:
time: 22.2 us; the launch traced here: 21.9 us
  blocking collectives  10.7 us (48%)
  starting transfers between devices  4.18 us (19%)
  waiting for transfers between devices  3.28 us (15%)
  Pallas kernels  3.1 us (14%)
  between operations  0.69 us (3%)
    all_to_all x1, blocking collectives, shards(): lax.all_to_all(send.reshape(message_count, length // PAIR, PAIR, width),...  10.7 us
    ppermute x2, starting transfers between devices, shards(): far = [lax.ppermute(part, 'narrow', across) for part in near]  4.18 us
    ppermute x2, waiting for transfers between devices, shards(): far = [lax.ppermute(part, 'narrow', across) for part in near]  3.28 us
    pallas_call x1, Pallas kernels, shards(): pl.pallas_call(functools.partial(ladder_kernel, rows, near_count, own_cou...  1.3 us
    pallas_call x1, Pallas kernels, shards(): pl.pallas_call(stage_kernel, out_shape=[part_shape] * PARTS, in_specs=[hb...  0.79 us
    pallas_call x1, Pallas kernels, shards(): pl.pallas_call(functools.partial(route_kernel, own_count, wide_count), ou...  0.78 us
  transfers between devices with their start and end apart: 2, of which 2 were waited for; matrix products, arithmetic and copies ran while one was open for 0% of the time, Pallas kernels for 4%

profile of v28, /device:TPU:0, one launch (start us, length us, event | category | flops | bytes accessed | tf_op | source)
XLA Modules:
  0.0 21.9 jit_solution(4127919209433940359)
XLA Ops:
  0.0 0.8 %stage.1 = (bf16[4,32,128]{2,1,0:T(8,128)(2,1)S(1)}, bf16[4,32,128]{2,1,0:T(8,128)(2,1)S(1)}) custom-call(bf16[8,32,128]{2,1,0:T(8,128)(2,1)} %source.1), custom_call_target="tpu_custom_call" | custom-call | tf_op jit(solution)/shard_map/stage/pallas_call | solution.py:215
  0.8 4.1 %collective-permute-start = (bf16[4,32,128]{2,1,0:T(8,128)(2,1)S(1)}, bf16[4,32,128]{2,1,0:T(8,128)(2,1)S(1)}, u32[]{:S(2)}, u32[]{:S(2)}) collective-permute-start(bf16[4,32,128]{2,1,0:T(8,128)(2,1)S(1)} %get-tuple-element.11.refs_0_), channel_id=1, source_target_pairs={{0,2},{1,3},{2,0},{3,1},{4,6},{5,7},{6,4},{7,5},{8,10},{9,11},{10,... | collective-permute-start | bytes 98312 | tf_op jit(solution)/shard_map/ppermute | solution.py:224
  4.9 0.1 collective-permute-start.1
  5.6 0.8 %route.1 = (bf16[256,256]{1,0:T(8,128)(2,1)S(1)}, bf16[8,128]{1,0:T(8,128)(2,1)S(1)}) custom-call(s32[8]{0:T(128)} %refs_0_.1, s32[1]{0:T(128)S(6)} %copy.7.refs_1_, s32[8]{0:T(128)} %refs_2_.1, s32[16]{0:T(128)} %refs_3_.1), custom_call_target="tpu_custom_call" | custom-call | flops 1073741824 | bytes 1048576 | tf_op jit(solution)/shard_map/route/pallas_call | solution.py:231
  6.4 0.0 copy-start
  6.4 0.7 %collective-permute-done.refs_2_ = bf16[4,32,128]{2,1,0:T(8,128)(2,1)S(1)} collective-permute-done((bf16[4,32,128]{2,1,0:T(8,128)(2,1)S(1)}, bf16[4,32,128]{2,1,0:T(8,128)(2,1)S(1)}, u32[]{:S(2)}, u32[]{:S(2)}) %collective-permute-start) | collective-permute-done | bytes 32800 | tf_op jit(solution)/shard_map/ppermute | solution.py:224
  7.1 2.6 %collective-permute-done.1.refs_3_ = bf16[4,32,128]{2,1,0:T(8,128)(2,1)S(1)} collective-permute-done((bf16[4,32,128]{2,1,0:T(8,128)(2,1)S(1)}, bf16[4,32,128]{2,1,0:T(8,128)(2,1)S(1)}, u32[]{:S(2)}, u32[]{:S(2)}) %collective-permute-start.1) | collective-permute-done | bytes 32800 | tf_op jit(solution)/shard_map/ppermute | solution.py:224
  9.7 0.2 %pack.1 = bf16[1056,128]{1,0:T(8,128)(2,1)S(1)} custom-call(bf16[256,256]{1,0:T(8,128)(2,1)S(1)} %get-tuple-element.9.order_ref, bf16[8,128]{1,0:T(8,128)(2,1)S(1)} %get-tuple-element.10.label_ref, bf16[4,32,128]{2,1,0:T(8,128)(2,1)S(1)} %get-tuple-element.11.refs_0_, bf16[4,32,128]{2,1,0:T(8,128)(2,1)S(1)} %get-tuple-element.12.refs_1_, ...), custom_call_target="tpu_custom_call" | custom-call | tf_op jit(solution)/shard_map/pack/pallas_call | solution.py:245
  9.9 10.7 %all_to_all.5 = bf16[16,33,2,128]{3,2,1,0:T(2,128)(2,1)S(1)} all-to-all(bf16[16,33,2,128]{3,2,1,0:T(2,128)(2,1)S(1)} %bitcast.3), channel_id=1, replica_groups={{16,17,20,21,8,9,12,13,24,25,28,29,0,1,4,5},{18,19,22,23,10,11,14,15,26..., dimensions={0} | all-to-all | bytes 540672 | tf_op jit(solution)/shard_map/all_to_all | solution.py:261
  20.6 0.0 copy-done
  20.6 1.3 %ladder.1 = f32[512,256]{1,0:T(8,128)} custom-call(bf16[512,1024]{1,0:T(8,128)(2,1)S(1)} %copy-done, bf16[1056,128]{1,0:T(8,128)(2,1)S(1)} %bitcast.2), custom_call_target="tpu_custom_call" | custom-call | tf_op jit(solution)/shard_map/ladder/pallas_call | solution.py:269
Async XLA Ops:
  0.8 6.3 %collective-permute-start = (bf16[4,32,128]{2,1,0:T(8,128)(2,1)S(1)}, bf16[4,32,128]{2,1,0:T(8,128)(2,1)S(1)}, u32[]{:S(2)}, u32[]{:S(2)}) collective-permute-start(bf16[4,32,128]{2,1,0:T(8,128)(2,1)S(1)} %get-tuple-element.11.refs_0_), channel_id=1, source_target_pairs={{0,2},{1,3},{2,0},{3,1},{4,6},{5,7},{6,4},{7,5},{8,10},{9,11},{10,... | collective-permute-start | bytes 98312 | tf_op jit(solution)/shard_map/ppermute | solution.py:224
  4.9 4.8 %collective-permute-start.1 = (bf16[4,32,128]{2,1,0:T(8,128)(2,1)S(1)}, bf16[4,32,128]{2,1,0:T(8,128)(2,1)S(1)}, u32[]{:S(2)}, u32[]{:S(2)}) collective-permute-start(bf16[4,32,128]{2,1,0:T(8,128)(2,1)S(1)} %get-tuple-element.12.refs_1_), channel_id=1, source_target_pairs={{0,2},{1,3},{2,0},{3,1},{4,6},{5,7},{6,4},{7,5},{8,10},{9,11},{10,... | collective-permute-start | bytes 98312 | tf_op jit(solution)/shard_map/ppermute | solution.py:224
  6.4 14.2 %copy-start = (bf16[512,1024]{1,0:T(8,128)(2,1)S(1)}, bf16[512,1024]{1,0:T(8,128)(2,1)}, u32[]{:S(2)}) copy-start(bf16[512,1024]{1,0:T(8,128)(2,1)} %amp_ref.1) | copy-start | bytes 3145732

commit v29 on v25

--- a/solution.py
+++ b/solution.py
@@ -146,7 +146,8 @@
         spot = pl.ds(pl.multiple_of(lax.rem(code, own_count) * width, width), width)
         parts = [message(w, z) for z in range(near_count)]
         for side in range(2):
-            half = jnp.concatenate([part[side] for part in parts], axis=0).astype(tiles.dtype)
+            order = parts if side == 0 else parts[::-1]
+            half = jnp.concatenate([part[side] for part in order], axis=0).astype(tiles.dtype)
             start = at * width + (near_at if side == 0 else far_at)
             tiles[pl.ds(pl.multiple_of(start, half_size), half_size), spot] = half
         return found + live
@@ -192,7 +193,7 @@
     hbm = pl.BlockSpec(memory_space=pltpu.HBM)
     vmem = pl.BlockSpec(memory_space=pltpu.VMEM)
     limit = pltpu.CompilerParams(vmem_limit_bytes=32 * 2**20)
-    across = [(z, (z + near_count) % depth_count) for z in range(depth_count)]
+    across = [(z, depth_count - 1 - z) for z in range(depth_count)]
     far = lax.ppermute(integrals, "narrow", across)
     given = [in_tile, counts, out_tile, owner_map, integrals]
     given = [

time: 19.5 us -> 19.4 us (level)
  waiting for transfers between devices: 2.3 us -> 0.95 us
  starting transfers between devices: 4.04 us -> 5.05 us
  blocking collectives: 9.87 us -> 10.2 us
    ppermute x1, waiting for transfers between devices: 2.3 us -> 0.95 us  [shards(): far = lax.ppermute(integrals, 'narrow', across)]
    ppermute x1, starting transfers between devices: 4.04 us -> 5.05 us  [shards(): far = lax.ppermute(integrals, 'narrow', across)]
    all_to_all x1, blocking collectives: 9.87 us -> 10.2 us  [shards(): lax.all_to_all(send.reshape(message_count, length // PAIR, PAIR, width),...]
where the time goes in v29:
time: 19.4 us; the launch traced here: 19.2 us
  blocking collectives  10.2 us (53%)
  starting transfers between devices  5.05 us (26%)
  Pallas kernels  2.42 us (12%)
  waiting for transfers between devices  0.95 us (5%)
  between operations  0.68 us (4%)
    all_to_all x1, blocking collectives, shards(): lax.all_to_all(send.reshape(message_count, length // PAIR, PAIR, width),...  10.2 us
    ppermute x1, starting transfers between devices, shards(): far = lax.ppermute(integrals, 'narrow', across)  5.05 us
    pallas_call x1, Pallas kernels, shards(): pl.pallas_call(functools.partial(ladder_kernel, rows, near_count, own_cou...  1.3 us
    ppermute x1, waiting for transfers between devices, shards(): far = lax.ppermute(integrals, 'narrow', across)  0.95 us
    pallas_call x1, Pallas kernels, shards(): pl.pallas_call(functools.partial(route_kernel, own_count, wide_count), ou...  0.89 us
  transfers between devices with their start and end apart: 1, of which 1 were waited for; matrix products, arithmetic and copies ran while one was open for 0% of the time, Pallas kernels for 5%

profile of v29, /device:TPU:0, one launch (start us, length us, event | category | flops | bytes accessed | tf_op | source)
XLA Modules:
  0.0 19.2 jit_solution(8299349791100644239)
XLA Ops:
  0.0 5.0 %collective-permute-start = (bf16[8,32,128]{2,1,0:T(8,128)(2,1)}, bf16[8,32,128]{2,1,0:T(8,128)(2,1)S(1)}, u32[]{:S(2)}, u32[]{:S(2)}) collective-permute-start(bf16[8,32,128]{2,1,0:T(8,128)(2,1)} %refs_4_.1), channel_id=1, source_target_pairs={{0,3},{1,2},{2,1},{3,0},{4,7},{5,6},{6,5},{7,4},{8,11},{9,10},{10,... | collective-permute-start | bytes 196616 | tf_op jit(solution)/shard_map/ppermute | solution.py:197
  5.7 0.9 %route.1 = (bf16[256,256]{1,0:T(8,128)(2,1)S(1)}, bf16[8,128]{1,0:T(8,128)(2,1)S(1)}, bf16[8,32,128]{2,1,0:T(8,128)(2,1)S(1)}) custom-call(s32[8]{0:T(128)} %refs_0_.1, s32[1]{0:T(128)S(6)} %copy.7.refs_1_, s32[8]{0:T(128)} %refs_2_.1, s32[16]{0:T(128)} %refs_3_.1, bf16[8,32,128]{2,1,0:T(8,128)(2,1)} %refs_4_.1), custom_call_target="tpu_custom_call" | custom-call | flops 1073741824 | bytes 1048576 | tf_op jit(solution)/shard_map/route/pallas_call | solution.py:204
  6.6 0.0 copy-start
  6.6 0.9 %collective-permute-done.far_ref = bf16[8,32,128]{2,1,0:T(8,128)(2,1)S(1)} collective-permute-done((bf16[8,32,128]{2,1,0:T(8,128)(2,1)}, bf16[8,32,128]{2,1,0:T(8,128)(2,1)S(1)}, u32[]{:S(2)}, u32[]{:S(2)}) %collective-permute-start) | collective-permute-done | bytes 65568 | tf_op jit(solution)/shard_map/ppermute | solution.py:197
  7.6 0.2 %pack.1 = bf16[1056,128]{1,0:T(8,128)(2,1)S(1)} custom-call(bf16[256,256]{1,0:T(8,128)(2,1)S(1)} %get-tuple-element.8.order_ref, bf16[8,128]{1,0:T(8,128)(2,1)S(1)} %get-tuple-element.9.label_ref, bf16[8,32,128]{2,1,0:T(8,128)(2,1)S(1)} %get-tuple-element.10.near_ref, bf16[8,32,128]{2,1,0:T(8,128)(2,1)S(1)} %collective-permute-done.far_ref), custom_call_target="tpu_custom_call" | custom-call | tf_op jit(solution)/shard_map/pack/pallas_call | solution.py:219
  7.8 10.2 %all_to_all.5 = bf16[16,33,2,128]{3,2,1,0:T(2,128)(2,1)S(1)} all-to-all(bf16[16,33,2,128]{3,2,1,0:T(2,128)(2,1)S(1)} %bitcast.3), channel_id=1, replica_groups={{16,17,20,21,8,9,12,13,24,25,28,29,0,1,4,5},{18,19,22,23,10,11,14,15,26..., dimensions={0} | all-to-all | bytes 540672 | tf_op jit(solution)/shard_map/all_to_all | solution.py:235
  17.9 0.0 copy-done
  17.9 1.3 %ladder.1 = f32[512,256]{1,0:T(8,128)} custom-call(bf16[512,1024]{1,0:T(8,128)(2,1)S(1)} %copy-done, bf16[1056,128]{1,0:T(8,128)(2,1)S(1)} %bitcast.2), custom_call_target="tpu_custom_call" | custom-call | tf_op jit(solution)/shard_map/ladder/pallas_call | solution.py:243
Async XLA Ops:
  0.0 7.6 %collective-permute-start = (bf16[8,32,128]{2,1,0:T(8,128)(2,1)}, bf16[8,32,128]{2,1,0:T(8,128)(2,1)S(1)}, u32[]{:S(2)}, u32[]{:S(2)}) collective-permute-start(bf16[8,32,128]{2,1,0:T(8,128)(2,1)} %refs_4_.1), channel_id=1, source_target_pairs={{0,3},{1,2},{2,1},{3,0},{4,7},{5,6},{6,5},{7,4},{8,11},{9,10},{10,... | collective-permute-start | bytes 196616 | tf_op jit(solution)/shard_map/ppermute | solution.py:197
  6.6 11.3 %copy-start = (bf16[512,1024]{1,0:T(8,128)(2,1)S(1)}, bf16[512,1024]{1,0:T(8,128)(2,1)}, u32[]{:S(2)}) copy-start(bf16[512,1024]{1,0:T(8,128)(2,1)} %amp_ref.1) | copy-start | bytes 3145732

commit v30 on v27

--- a/solution.py
+++ b/solution.py
@@ -146,7 +146,8 @@
         spot = pl.ds(pl.multiple_of(lax.rem(code, own_count) * width, width), width)
         parts = [message(w, z) for z in range(near_count)]
         for side in range(2):
-            half = jnp.concatenate([part[side] for part in parts], axis=0).astype(tiles.dtype)
+            order = parts if side == 0 else parts[::-1]
+            half = jnp.concatenate([part[side] for part in order], axis=0).astype(tiles.dtype)
             start = at * width + (near_at if side == 0 else far_at)
             tiles[pl.ds(pl.multiple_of(start, half_size), half_size), spot] = half
         return found + live
@@ -192,7 +193,7 @@
     hbm = pl.BlockSpec(memory_space=pltpu.HBM)
     vmem = pl.BlockSpec(memory_space=pltpu.VMEM)
     limit = pltpu.CompilerParams(vmem_limit_bytes=32 * 2**20)
-    across = [(z, (z + near_count) % depth_count) for z in range(depth_count)]
+    across = [(z, depth_count - 1 - z) for z in range(depth_count)]
     far = lax.ppermute(integrals, "narrow", across)
     given = [in_tile, counts, out_tile, owner_map, integrals]
     given = [

time: 19.5 us -> 19.4 us (level)
  waiting for transfers between devices: 2.3 us -> 0.95 us
  starting transfers between devices: 4.04 us -> 5.05 us
  blocking collectives: 9.87 us -> 10.2 us
    ppermute x1, waiting for transfers between devices: 2.3 us -> 0.95 us  [shards(): far = lax.ppermute(integrals, 'narrow', across)]
    ppermute x1, starting transfers between devices: 4.04 us -> 5.05 us  [shards(): far = lax.ppermute(integrals, 'narrow', across)]
    all_to_all x1, blocking collectives: 9.87 us -> 10.2 us  [shards(): lax.all_to_all(send.reshape(message_count, length // PAIR, PAIR, width),...]
where the time goes in v30:
time: 19.4 us; the launch traced here: 19.3 us
  blocking collectives  10.2 us (53%)
  starting transfers between devices  5.05 us (26%)
  Pallas kernels  2.42 us (12%)
  waiting for transfers between devices  0.95 us (5%)
  between operations  0.68 us (4%)
    all_to_all x1, blocking collectives, shards(): lax.all_to_all(send.reshape(message_count, length // PAIR, PAIR, width),...  10.2 us
    ppermute x1, starting transfers between devices, shards(): far = lax.ppermute(integrals, 'narrow', across)  5.05 us
    pallas_call x1, Pallas kernels, shards(): pl.pallas_call(functools.partial(ladder_kernel, rows, near_count, own_cou...  1.3 us
    ppermute x1, waiting for transfers between devices, shards(): far = lax.ppermute(integrals, 'narrow', across)  0.95 us
    pallas_call x1, Pallas kernels, shards(): pl.pallas_call(functools.partial(route_kernel, own_count, wide_count), ou...  0.89 us
  transfers between devices with their start and end apart: 1, of which 1 were waited for; matrix products, arithmetic and copies ran while one was open for 0% of the time, Pallas kernels for 5%

profile of v30, /device:TPU:0, one launch (start us, length us, event | category | flops | bytes accessed | tf_op | source)
XLA Modules:
  0.0 19.3 jit_solution(4340543283226380605)
XLA Ops:
  0.0 5.0 %collective-permute-start = (bf16[8,32,128]{2,1,0:T(8,128)(2,1)}, bf16[8,32,128]{2,1,0:T(8,128)(2,1)S(1)}, u32[]{:S(2)}, u32[]{:S(2)}) collective-permute-start(bf16[8,32,128]{2,1,0:T(8,128)(2,1)} %refs_4_.1), channel_id=1, source_target_pairs={{0,3},{1,2},{2,1},{3,0},{4,7},{5,6},{6,5},{7,4},{8,11},{9,10},{10,... | collective-permute-start | bytes 196616 | tf_op jit(solution)/shard_map/ppermute | solution.py:197
  5.7 0.9 %route.1 = (bf16[256,256]{1,0:T(8,128)(2,1)S(1)}, bf16[8,128]{1,0:T(8,128)(2,1)S(1)}, bf16[8,32,128]{2,1,0:T(8,128)(2,1)S(1)}) custom-call(s32[8]{0:T(128)} %refs_0_.1, s32[1]{0:T(128)S(6)} %copy.7.refs_1_, s32[8]{0:T(128)} %refs_2_.1, s32[16]{0:T(128)} %refs_3_.1, bf16[8,32,128]{2,1,0:T(8,128)(2,1)} %refs_4_.1), custom_call_target="tpu_custom_call" | custom-call | flops 1073741824 | bytes 1048576 | tf_op jit(solution)/shard_map/route/pallas_call | solution.py:204
  6.6 0.0 copy-start
  6.6 0.9 %collective-permute-done.far_ref = bf16[8,32,128]{2,1,0:T(8,128)(2,1)S(1)} collective-permute-done((bf16[8,32,128]{2,1,0:T(8,128)(2,1)}, bf16[8,32,128]{2,1,0:T(8,128)(2,1)S(1)}, u32[]{:S(2)}, u32[]{:S(2)}) %collective-permute-start) | collective-permute-done | bytes 65568 | tf_op jit(solution)/shard_map/ppermute | solution.py:197
  7.6 0.2 %pack.1 = bf16[1056,128]{1,0:T(8,128)(2,1)S(1)} custom-call(bf16[256,256]{1,0:T(8,128)(2,1)S(1)} %get-tuple-element.8.order_ref, bf16[8,128]{1,0:T(8,128)(2,1)S(1)} %get-tuple-element.9.label_ref, bf16[8,32,128]{2,1,0:T(8,128)(2,1)S(1)} %get-tuple-element.10.near_ref, bf16[8,32,128]{2,1,0:T(8,128)(2,1)S(1)} %collective-permute-done.far_ref), custom_call_target="tpu_custom_call" | custom-call | tf_op jit(solution)/shard_map/pack/pallas_call | solution.py:219
  7.8 10.2 %all_to_all.5 = bf16[16,33,2,128]{3,2,1,0:T(2,128)(2,1)S(1)} all-to-all(bf16[16,33,2,128]{3,2,1,0:T(2,128)(2,1)S(1)} %bitcast.3), channel_id=1, replica_groups={{8,9,12,13,24,25,28,29,16,17,20,21,0,1,4,5},{10,11,14,15,26,27,30,31,18..., dimensions={0} | all-to-all | bytes 540672 | tf_op jit(solution)/shard_map/all_to_all | solution.py:235
  17.9 0.0 copy-done
  17.9 1.3 %ladder.1 = f32[512,256]{1,0:T(8,128)} custom-call(bf16[512,1024]{1,0:T(8,128)(2,1)S(1)} %copy-done, bf16[1056,128]{1,0:T(8,128)(2,1)S(1)} %bitcast.2), custom_call_target="tpu_custom_call" | custom-call | tf_op jit(solution)/shard_map/ladder/pallas_call | solution.py:243
Async XLA Ops:
  0.0 7.6 %collective-permute-start = (bf16[8,32,128]{2,1,0:T(8,128)(2,1)}, bf16[8,32,128]{2,1,0:T(8,128)(2,1)S(1)}, u32[]{:S(2)}, u32[]{:S(2)}) collective-permute-start(bf16[8,32,128]{2,1,0:T(8,128)(2,1)} %refs_4_.1), channel_id=1, source_target_pairs={{0,3},{1,2},{2,1},{3,0},{4,7},{5,6},{6,5},{7,4},{8,11},{9,10},{10,... | collective-permute-start | bytes 196616 | tf_op jit(solution)/shard_map/ppermute | solution.py:197
  6.6 11.3 %copy-start = (bf16[512,1024]{1,0:T(8,128)(2,1)S(1)}, bf16[512,1024]{1,0:T(8,128)(2,1)}, u32[]{:S(2)}) copy-start(bf16[512,1024]{1,0:T(8,128)(2,1)} %amp_ref.1) | copy-start | bytes 3145732

commit v31 on v29

--- a/solution.py
+++ b/solution.py
@@ -136,7 +136,7 @@
             label = got_ref[pl.ds(start, length)].astype(jnp.float32)[2 * rows :]
         else:
             label = got_ref[pl.ds(start + 2 * rows, length - 2 * rows)].astype(jnp.float32)
-        return jnp.max(label).astype(jnp.int32)
+        return label[0, 0].astype(jnp.int32)
 
     def keep(w, label, found):
         live = jnp.minimum(label, 1)

time: 19.4 us -> 19.4 us (level)
  no operation moved by 1% of the time
where the time goes in v31:
time: 19.4 us; the launch traced here: 19.2 us
  blocking collectives  10.2 us (53%)
  starting transfers between devices  5.05 us (26%)
  Pallas kernels  2.34 us (12%)
  waiting for transfers between devices  0.95 us (5%)
  between operations  0.68 us (4%)
    all_to_all x1, blocking collectives, shards(): lax.all_to_all(send.reshape(message_count, length // PAIR, PAIR, width),...  10.2 us
    ppermute x1, starting transfers between devices, shards(): far = lax.ppermute(integrals, 'narrow', across)  5.05 us
    pallas_call x1, Pallas kernels, shards(): pl.pallas_call(functools.partial(ladder_kernel, rows, near_count, own_cou...  1.23 us
    ppermute x1, waiting for transfers between devices, shards(): far = lax.ppermute(integrals, 'narrow', across)  0.95 us
    pallas_call x1, Pallas kernels, shards(): pl.pallas_call(functools.partial(route_kernel, own_count, wide_count), ou...  0.89 us
  transfers between devices with their start and end apart: 1, of which 1 were waited for; matrix products, arithmetic and copies ran while one was open for 0% of the time, Pallas kernels for 5%

profile of v31, /device:TPU:0, one launch (start us, length us, event | category | flops | bytes accessed | tf_op | source)
XLA Modules:
  0.0 19.2 jit_solution(5599902053242474813)
XLA Ops:
  0.0 5.0 %collective-permute-start = (bf16[8,32,128]{2,1,0:T(8,128)(2,1)}, bf16[8,32,128]{2,1,0:T(8,128)(2,1)S(1)}, u32[]{:S(2)}, u32[]{:S(2)}) collective-permute-start(bf16[8,32,128]{2,1,0:T(8,128)(2,1)} %refs_4_.1), channel_id=1, source_target_pairs={{0,3},{1,2},{2,1},{3,0},{4,7},{5,6},{6,5},{7,4},{8,11},{9,10},{10,... | collective-permute-start | bytes 196616 | tf_op jit(solution)/shard_map/ppermute | solution.py:197
  5.7 0.9 %route.1 = (bf16[256,256]{1,0:T(8,128)(2,1)S(1)}, bf16[8,128]{1,0:T(8,128)(2,1)S(1)}, bf16[8,32,128]{2,1,0:T(8,128)(2,1)S(1)}) custom-call(s32[8]{0:T(128)} %refs_0_.1, s32[1]{0:T(128)S(6)} %copy.7.refs_1_, s32[8]{0:T(128)} %refs_2_.1, s32[16]{0:T(128)} %refs_3_.1, bf16[8,32,128]{2,1,0:T(8,128)(2,1)} %refs_4_.1), custom_call_target="tpu_custom_call" | custom-call | flops 1073741824 | bytes 1048576 | tf_op jit(solution)/shard_map/route/pallas_call | solution.py:204
  6.6 0.0 copy-start
  6.6 0.9 %collective-permute-done.far_ref = bf16[8,32,128]{2,1,0:T(8,128)(2,1)S(1)} collective-permute-done((bf16[8,32,128]{2,1,0:T(8,128)(2,1)}, bf16[8,32,128]{2,1,0:T(8,128)(2,1)S(1)}, u32[]{:S(2)}, u32[]{:S(2)}) %collective-permute-start) | collective-permute-done | bytes 65568 | tf_op jit(solution)/shard_map/ppermute | solution.py:197
  7.6 0.2 %pack.1 = bf16[1056,128]{1,0:T(8,128)(2,1)S(1)} custom-call(bf16[256,256]{1,0:T(8,128)(2,1)S(1)} %get-tuple-element.8.order_ref, bf16[8,128]{1,0:T(8,128)(2,1)S(1)} %get-tuple-element.9.label_ref, bf16[8,32,128]{2,1,0:T(8,128)(2,1)S(1)} %get-tuple-element.10.near_ref, bf16[8,32,128]{2,1,0:T(8,128)(2,1)S(1)} %collective-permute-done.far_ref), custom_call_target="tpu_custom_call" | custom-call | tf_op jit(solution)/shard_map/pack/pallas_call | solution.py:219
  7.8 10.2 %all_to_all.5 = bf16[16,33,2,128]{3,2,1,0:T(2,128)(2,1)S(1)} all-to-all(bf16[16,33,2,128]{3,2,1,0:T(2,128)(2,1)S(1)} %bitcast.3), channel_id=1, replica_groups={{16,17,20,21,8,9,12,13,24,25,28,29,0,1,4,5},{18,19,22,23,10,11,14,15,26..., dimensions={0} | all-to-all | bytes 540672 | tf_op jit(solution)/shard_map/all_to_all | solution.py:235
  17.9 0.0 copy-done
  17.9 1.2 %ladder.1 = f32[512,256]{1,0:T(8,128)} custom-call(bf16[512,1024]{1,0:T(8,128)(2,1)S(1)} %copy-done, bf16[1056,128]{1,0:T(8,128)(2,1)S(1)} %bitcast.2), custom_call_target="tpu_custom_call" | custom-call | tf_op jit(solution)/shard_map/ladder/pallas_call | solution.py:243
Async XLA Ops:
  0.0 7.6 %collective-permute-start = (bf16[8,32,128]{2,1,0:T(8,128)(2,1)}, bf16[8,32,128]{2,1,0:T(8,128)(2,1)S(1)}, u32[]{:S(2)}, u32[]{:S(2)}) collective-permute-start(bf16[8,32,128]{2,1,0:T(8,128)(2,1)} %refs_4_.1), channel_id=1, source_target_pairs={{0,3},{1,2},{2,1},{3,0},{4,7},{5,6},{6,5},{7,4},{8,11},{9,10},{10,... | collective-permute-start | bytes 196616 | tf_op jit(solution)/shard_map/ppermute | solution.py:197
  6.6 11.3 %copy-start = (bf16[512,1024]{1,0:T(8,128)(2,1)S(1)}, bf16[512,1024]{1,0:T(8,128)(2,1)}, u32[]{:S(2)}) copy-start(bf16[512,1024]{1,0:T(8,128)(2,1)} %amp_ref.1) | copy-start | bytes 3145732

commit v32 on v31

--- a/solution.py
+++ b/solution.py
@@ -32,14 +32,14 @@
 
 def group_places(wide_count, near_count):
     cores = range(CORES)
-    depths = range(near_count)
-    return [(chip * CORES + core, z) for chip in chip_order(wide_count) for core in cores for z in depths]
+    depths = reversed(range(near_count))
+    return [(chip * CORES + core, z) for z in depths for chip in chip_order(wide_count) for core in cores]
 
 
 def message_at(w, z, wide_count, near_count, length):
     if isinstance(w, int):
         return group_places(wide_count, near_count).index((w, z)) * length
-    place = w * near_count + z
+    place = (near_count - 1 - z) * wide_count + w
     return pl.multiple_of(place * length, length)
 
 

time: 19.4 us -> 19.8 us (1.021)
  blocking collectives: 10.2 us -> 10.6 us
    all_to_all x1, blocking collectives: 10.2 us -> 10.6 us  [shards(): lax.all_to_all(send.reshape(message_count, length // PAIR, PAIR, width),...]
where the time goes in v32:
time: 19.8 us; the launch traced here: 19.6 us
  blocking collectives  10.6 us (54%)
  starting transfers between devices  5.05 us (26%)
  Pallas kernels  2.33 us (12%)
  waiting for transfers between devices  0.95 us (5%)
  between operations  0.68 us (3%)
    all_to_all x1, blocking collectives, shards(): lax.all_to_all(send.reshape(message_count, length // PAIR, PAIR, width),...  10.6 us
    ppermute x1, starting transfers between devices, shards(): far = lax.ppermute(integrals, 'narrow', across)  5.05 us
    pallas_call x1, Pallas kernels, shards(): pl.pallas_call(functools.partial(ladder_kernel, rows, near_count, own_cou...  1.23 us
    ppermute x1, waiting for transfers between devices, shards(): far = lax.ppermute(integrals, 'narrow', across)  0.95 us
    pallas_call x1, Pallas kernels, shards(): pl.pallas_call(functools.partial(route_kernel, own_count, wide_count), ou...  0.89 us
  transfers between devices with their start and end apart: 1, of which 1 were waited for; matrix products, arithmetic and copies ran while one was open for 0% of the time, Pallas kernels for 5%

profile of v32, /device:TPU:0, one launch (start us, length us, event | category | flops | bytes accessed | tf_op | source)
XLA Modules:
  0.0 19.6 jit_solution(11626867705441579866)
XLA Ops:
  0.0 5.0 %collective-permute-start = (bf16[8,32,128]{2,1,0:T(8,128)(2,1)}, bf16[8,32,128]{2,1,0:T(8,128)(2,1)S(1)}, u32[]{:S(2)}, u32[]{:S(2)}) collective-permute-start(bf16[8,32,128]{2,1,0:T(8,128)(2,1)} %refs_4_.1), channel_id=1, source_target_pairs={{0,3},{1,2},{2,1},{3,0},{4,7},{5,6},{6,5},{7,4},{8,11},{9,10},{10,... | collective-permute-start | bytes 196616 | tf_op jit(solution)/shard_map/ppermute | solution.py:197
  5.7 0.9 %route.1 = (bf16[256,256]{1,0:T(8,128)(2,1)S(1)}, bf16[8,128]{1,0:T(8,128)(2,1)S(1)}, bf16[8,32,128]{2,1,0:T(8,128)(2,1)S(1)}) custom-call(s32[8]{0:T(128)} %refs_0_.1, s32[1]{0:T(128)S(6)} %copy.7.refs_1_, s32[8]{0:T(128)} %refs_2_.1, s32[16]{0:T(128)} %refs_3_.1, bf16[8,32,128]{2,1,0:T(8,128)(2,1)} %refs_4_.1), custom_call_target="tpu_custom_call" | custom-call | flops 1073741824 | bytes 1048576 | tf_op jit(solution)/shard_map/route/pallas_call | solution.py:204
  6.6 0.0 copy-start
  6.6 0.9 %collective-permute-done.far_ref = bf16[8,32,128]{2,1,0:T(8,128)(2,1)S(1)} collective-permute-done((bf16[8,32,128]{2,1,0:T(8,128)(2,1)}, bf16[8,32,128]{2,1,0:T(8,128)(2,1)S(1)}, u32[]{:S(2)}, u32[]{:S(2)}) %collective-permute-start) | collective-permute-done | bytes 65568 | tf_op jit(solution)/shard_map/ppermute | solution.py:197
  7.6 0.2 %pack.1 = bf16[1056,128]{1,0:T(8,128)(2,1)S(1)} custom-call(bf16[256,256]{1,0:T(8,128)(2,1)S(1)} %get-tuple-element.8.order_ref, bf16[8,128]{1,0:T(8,128)(2,1)S(1)} %get-tuple-element.9.label_ref, bf16[8,32,128]{2,1,0:T(8,128)(2,1)S(1)} %get-tuple-element.10.near_ref, bf16[8,32,128]{2,1,0:T(8,128)(2,1)S(1)} %collective-permute-done.far_ref), custom_call_target="tpu_custom_call" | custom-call | tf_op jit(solution)/shard_map/pack/pallas_call | solution.py:219
  7.8 10.6 %all_to_all.5 = bf16[16,33,2,128]{3,2,1,0:T(2,128)(2,1)S(1)} all-to-all(bf16[16,33,2,128]{3,2,1,0:T(2,128)(2,1)S(1)} %bitcast.3), channel_id=1, replica_groups={{17,21,9,13,25,29,1,5,16,20,8,12,24,28,0,4},{19,23,11,15,27,31,3,7,18,2..., dimensions={0} | all-to-all | bytes 540672 | tf_op jit(solution)/shard_map/all_to_all | solution.py:235
  18.4 0.0 copy-done
  18.4 1.2 %ladder.1 = f32[512,256]{1,0:T(8,128)} custom-call(bf16[512,1024]{1,0:T(8,128)(2,1)S(1)} %copy-done, bf16[1056,128]{1,0:T(8,128)(2,1)S(1)} %bitcast.2), custom_call_target="tpu_custom_call" | custom-call | tf_op jit(solution)/shard_map/ladder/pallas_call | solution.py:243
Async XLA Ops:
  0.0 7.6 %collective-permute-start = (bf16[8,32,128]{2,1,0:T(8,128)(2,1)}, bf16[8,32,128]{2,1,0:T(8,128)(2,1)S(1)}, u32[]{:S(2)}, u32[]{:S(2)}) collective-permute-start(bf16[8,32,128]{2,1,0:T(8,128)(2,1)} %refs_4_.1), channel_id=1, source_target_pairs={{0,3},{1,2},{2,1},{3,0},{4,7},{5,6},{6,5},{7,4},{8,11},{9,10},{10,... | collective-permute-start | bytes 196616 | tf_op jit(solution)/shard_map/ppermute | solution.py:197
  6.6 11.8 %copy-start = (bf16[512,1024]{1,0:T(8,128)(2,1)S(1)}, bf16[512,1024]{1,0:T(8,128)(2,1)}, u32[]{:S(2)}) copy-start(bf16[512,1024]{1,0:T(8,128)(2,1)} %amp_ref.1) | copy-start | bytes 3145732

commit v33 on v32

--- a/solution.py
+++ b/solution.py
@@ -25,9 +25,8 @@
     chip_count = wide_count // CORES
     if wide_count > UNROLL:
         return list(range(chip_count))
-    bits = (chip_count - 1).bit_length()
-    flipped = [int(format(chip, "b").zfill(bits)[::-1], 2) for chip in range(2**bits)]
-    return [chip for chip in flipped[1:] if chip < chip_count] + [0]
+    first = chip_count // 2
+    return [first] + [chip for chip in range(chip_count) if chip != first]
 
 
 def group_places(wide_count, near_count):

time: 19.8 us -> 19.8 us (level)
  no operation moved by 1% of the time
where the time goes in v33:
time: 19.8 us; the launch traced here: 19.6 us
  blocking collectives  10.6 us (54%)
  starting transfers between devices  5.05 us (26%)
  Pallas kernels  2.33 us (12%)
  waiting for transfers between devices  0.95 us (5%)
  between operations  0.68 us (3%)
    all_to_all x1, blocking collectives, shards(): lax.all_to_all(send.reshape(message_count, length // PAIR, PAIR, width),...  10.6 us
    ppermute x1, starting transfers between devices, shards(): far = lax.ppermute(integrals, 'narrow', across)  5.05 us
    pallas_call x1, Pallas kernels, shards(): pl.pallas_call(functools.partial(ladder_kernel, rows, near_count, own_cou...  1.23 us
    ppermute x1, waiting for transfers between devices, shards(): far = lax.ppermute(integrals, 'narrow', across)  0.95 us
    pallas_call x1, Pallas kernels, shards(): pl.pallas_call(functools.partial(route_kernel, own_count, wide_count), ou...  0.89 us
  transfers between devices with their start and end apart: 1, of which 1 were waited for; matrix products, arithmetic and copies ran while one was open for 0% of the time, Pallas kernels for 5%

profile of v33, /device:TPU:0, one launch (start us, length us, event | category | flops | bytes accessed | tf_op | source)
XLA Modules:
  0.0 19.6 jit_solution(18049191345745619050)
XLA Ops:
  0.0 5.0 %collective-permute-start = (bf16[8,32,128]{2,1,0:T(8,128)(2,1)}, bf16[8,32,128]{2,1,0:T(8,128)(2,1)S(1)}, u32[]{:S(2)}, u32[]{:S(2)}) collective-permute-start(bf16[8,32,128]{2,1,0:T(8,128)(2,1)} %refs_4_.1), channel_id=1, source_target_pairs={{0,3},{1,2},{2,1},{3,0},{4,7},{5,6},{6,5},{7,4},{8,11},{9,10},{10,... | collective-permute-start | bytes 196616 | tf_op jit(solution)/shard_map/ppermute | solution.py:196
  5.7 0.9 %route.1 = (bf16[256,256]{1,0:T(8,128)(2,1)S(1)}, bf16[8,128]{1,0:T(8,128)(2,1)S(1)}, bf16[8,32,128]{2,1,0:T(8,128)(2,1)S(1)}) custom-call(s32[8]{0:T(128)} %refs_0_.1, s32[1]{0:T(128)S(6)} %copy.7.refs_1_, s32[8]{0:T(128)} %refs_2_.1, s32[16]{0:T(128)} %refs_3_.1, bf16[8,32,128]{2,1,0:T(8,128)(2,1)} %refs_4_.1), custom_call_target="tpu_custom_call" | custom-call | flops 1073741824 | bytes 1048576 | tf_op jit(solution)/shard_map/route/pallas_call | solution.py:203
  6.6 0.0 copy-start
  6.6 0.9 %collective-permute-done.far_ref = bf16[8,32,128]{2,1,0:T(8,128)(2,1)S(1)} collective-permute-done((bf16[8,32,128]{2,1,0:T(8,128)(2,1)}, bf16[8,32,128]{2,1,0:T(8,128)(2,1)S(1)}, u32[]{:S(2)}, u32[]{:S(2)}) %collective-permute-start) | collective-permute-done | bytes 65568 | tf_op jit(solution)/shard_map/ppermute | solution.py:196
  7.6 0.2 %pack.1 = bf16[1056,128]{1,0:T(8,128)(2,1)S(1)} custom-call(bf16[256,256]{1,0:T(8,128)(2,1)S(1)} %get-tuple-element.8.order_ref, bf16[8,128]{1,0:T(8,128)(2,1)S(1)} %get-tuple-element.9.label_ref, bf16[8,32,128]{2,1,0:T(8,128)(2,1)S(1)} %get-tuple-element.10.near_ref, bf16[8,32,128]{2,1,0:T(8,128)(2,1)S(1)} %collective-permute-done.far_ref), custom_call_target="tpu_custom_call" | custom-call | tf_op jit(solution)/shard_map/pack/pallas_call | solution.py:218
  7.8 10.6 %all_to_all.5 = bf16[16,33,2,128]{3,2,1,0:T(2,128)(2,1)S(1)} all-to-all(bf16[16,33,2,128]{3,2,1,0:T(2,128)(2,1)S(1)} %bitcast.3), channel_id=1, replica_groups={{17,21,1,5,9,13,25,29,16,20,0,4,8,12,24,28},{19,23,3,7,11,15,27,31,18,2..., dimensions={0} | all-to-all | bytes 540672 | tf_op jit(solution)/shard_map/all_to_all | solution.py:234
  18.4 0.0 copy-done
  18.4 1.2 %ladder.1 = f32[512,256]{1,0:T(8,128)} custom-call(bf16[512,1024]{1,0:T(8,128)(2,1)S(1)} %copy-done, bf16[1056,128]{1,0:T(8,128)(2,1)S(1)} %bitcast.2), custom_call_target="tpu_custom_call" | custom-call | tf_op jit(solution)/shard_map/ladder/pallas_call | solution.py:242
Async XLA Ops:
  0.0 7.6 %collective-permute-start = (bf16[8,32,128]{2,1,0:T(8,128)(2,1)}, bf16[8,32,128]{2,1,0:T(8,128)(2,1)S(1)}, u32[]{:S(2)}, u32[]{:S(2)}) collective-permute-start(bf16[8,32,128]{2,1,0:T(8,128)(2,1)} %refs_4_.1), channel_id=1, source_target_pairs={{0,3},{1,2},{2,1},{3,0},{4,7},{5,6},{6,5},{7,4},{8,11},{9,10},{10,... | collective-permute-start | bytes 196616 | tf_op jit(solution)/shard_map/ppermute | solution.py:196
  6.6 11.8 %copy-start = (bf16[512,1024]{1,0:T(8,128)(2,1)S(1)}, bf16[512,1024]{1,0:T(8,128)(2,1)}, u32[]{:S(2)}) copy-start(bf16[512,1024]{1,0:T(8,128)(2,1)} %amp_ref.1) | copy-start | bytes 3145732

commit v34 on v31

--- a/solution.py
+++ b/solution.py
@@ -33,13 +33,13 @@
 def group_places(wide_count, near_count):
     cores = range(CORES)
     depths = range(near_count)
-    return [(chip * CORES + core, z) for chip in chip_order(wide_count) for core in cores for z in depths]
+    return [(chip * CORES + core, z) for chip in chip_order(wide_count) for z in depths for core in cores]
 
 
 def message_at(w, z, wide_count, near_count, length):
     if isinstance(w, int):
         return group_places(wide_count, near_count).index((w, z)) * length
-    place = w * near_count + z
+    place = (w // CORES * near_count + z) * CORES + w % CORES
     return pl.multiple_of(place * length, length)
 
 

time: 19.4 us -> 20.3 us (1.046)
  blocking collectives: 10.2 us -> 11 us
    all_to_all x1, blocking collectives: 10.2 us -> 11 us  [shards(): lax.all_to_all(send.reshape(message_count, length // PAIR, PAIR, width),...]
  transfers between devices with their start and end apart: 1 -> 1, of which waited for: 1 -> 1; matrix products, arithmetic and copies ran while one was open for 0% -> 0% of each run, Pallas kernels for 5% -> 4%
where the time goes in v34:
time: 20.3 us; the launch traced here: 20.1 us
  blocking collectives  11 us (54%)
  starting transfers between devices  5.05 us (25%)
  Pallas kernels  2.34 us (12%)
  waiting for transfers between devices  0.95 us (5%)
  between operations  0.68 us (3%)
    all_to_all x1, blocking collectives, shards(): lax.all_to_all(send.reshape(message_count, length // PAIR, PAIR, width),...  11 us
    ppermute x1, starting transfers between devices, shards(): far = lax.ppermute(integrals, 'narrow', across)  5.05 us
    pallas_call x1, Pallas kernels, shards(): pl.pallas_call(functools.partial(ladder_kernel, rows, near_count, own_cou...  1.23 us
    ppermute x1, waiting for transfers between devices, shards(): far = lax.ppermute(integrals, 'narrow', across)  0.95 us
    pallas_call x1, Pallas kernels, shards(): pl.pallas_call(functools.partial(route_kernel, own_count, wide_count), ou...  0.89 us
  transfers between devices with their start and end apart: 1, of which 1 were waited for; matrix products, arithmetic and copies ran while one was open for 0% of the time, Pallas kernels for 4%

profile of v34, /device:TPU:0, one launch (start us, length us, event | category | flops | bytes accessed | tf_op | source)
XLA Modules:
  0.0 20.1 jit_solution(14434561724264455183)
XLA Ops:
  0.0 5.0 %collective-permute-start = (bf16[8,32,128]{2,1,0:T(8,128)(2,1)}, bf16[8,32,128]{2,1,0:T(8,128)(2,1)S(1)}, u32[]{:S(2)}, u32[]{:S(2)}) collective-permute-start(bf16[8,32,128]{2,1,0:T(8,128)(2,1)} %refs_4_.1), channel_id=1, source_target_pairs={{0,3},{1,2},{2,1},{3,0},{4,7},{5,6},{6,5},{7,4},{8,11},{9,10},{10,... | collective-permute-start | bytes 196616 | tf_op jit(solution)/shard_map/ppermute | solution.py:197
  5.7 0.9 %route.1 = (bf16[256,256]{1,0:T(8,128)(2,1)S(1)}, bf16[8,128]{1,0:T(8,128)(2,1)S(1)}, bf16[8,32,128]{2,1,0:T(8,128)(2,1)S(1)}) custom-call(s32[8]{0:T(128)} %refs_0_.1, s32[1]{0:T(128)S(6)} %copy.7.refs_1_, s32[8]{0:T(128)} %refs_2_.1, s32[16]{0:T(128)} %refs_3_.1, bf16[8,32,128]{2,1,0:T(8,128)(2,1)} %refs_4_.1), custom_call_target="tpu_custom_call" | custom-call | flops 1073741824 | bytes 1048576 | tf_op jit(solution)/shard_map/route/pallas_call | solution.py:204
  6.6 0.0 copy-start
  6.6 0.9 %collective-permute-done.far_ref = bf16[8,32,128]{2,1,0:T(8,128)(2,1)S(1)} collective-permute-done((bf16[8,32,128]{2,1,0:T(8,128)(2,1)}, bf16[8,32,128]{2,1,0:T(8,128)(2,1)S(1)}, u32[]{:S(2)}, u32[]{:S(2)}) %collective-permute-start) | collective-permute-done | bytes 65568 | tf_op jit(solution)/shard_map/ppermute | solution.py:197
  7.6 0.2 %pack.1 = bf16[1056,128]{1,0:T(8,128)(2,1)S(1)} custom-call(bf16[256,256]{1,0:T(8,128)(2,1)S(1)} %get-tuple-element.8.order_ref, bf16[8,128]{1,0:T(8,128)(2,1)S(1)} %get-tuple-element.9.label_ref, bf16[8,32,128]{2,1,0:T(8,128)(2,1)S(1)} %get-tuple-element.10.near_ref, bf16[8,32,128]{2,1,0:T(8,128)(2,1)S(1)} %collective-permute-done.far_ref), custom_call_target="tpu_custom_call" | custom-call | tf_op jit(solution)/shard_map/pack/pallas_call | solution.py:219
  7.8 11.0 %all_to_all.5 = bf16[16,33,2,128]{3,2,1,0:T(2,128)(2,1)S(1)} all-to-all(bf16[16,33,2,128]{3,2,1,0:T(2,128)(2,1)S(1)} %bitcast.3), channel_id=1, replica_groups={{16,20,17,21,8,12,9,13,24,28,25,29,0,4,1,5},{18,22,19,23,10,14,11,15,26..., dimensions={0} | all-to-all | bytes 540672 | tf_op jit(solution)/shard_map/all_to_all | solution.py:235
  18.8 0.0 copy-done
  18.8 1.2 %ladder.1 = f32[512,256]{1,0:T(8,128)} custom-call(bf16[512,1024]{1,0:T(8,128)(2,1)S(1)} %copy-done, bf16[1056,128]{1,0:T(8,128)(2,1)S(1)} %bitcast.2), custom_call_target="tpu_custom_call" | custom-call | tf_op jit(solution)/shard_map/ladder/pallas_call | solution.py:243
Async XLA Ops:
  0.0 7.6 %collective-permute-start = (bf16[8,32,128]{2,1,0:T(8,128)(2,1)}, bf16[8,32,128]{2,1,0:T(8,128)(2,1)S(1)}, u32[]{:S(2)}, u32[]{:S(2)}) collective-permute-start(bf16[8,32,128]{2,1,0:T(8,128)(2,1)} %refs_4_.1), channel_id=1, source_target_pairs={{0,3},{1,2},{2,1},{3,0},{4,7},{5,6},{6,5},{7,4},{8,11},{9,10},{10,... | collective-permute-start | bytes 196616 | tf_op jit(solution)/shard_map/ppermute | solution.py:197
  6.6 12.2 %copy-start = (bf16[512,1024]{1,0:T(8,128)(2,1)S(1)}, bf16[512,1024]{1,0:T(8,128)(2,1)}, u32[]{:S(2)}) copy-start(bf16[512,1024]{1,0:T(8,128)(2,1)} %amp_ref.1) | copy-start | bytes 3145732

commit v35 on v34

--- a/solution.py
+++ b/solution.py
@@ -32,14 +32,14 @@
 
 def group_places(wide_count, near_count):
     cores = range(CORES)
-    depths = range(near_count)
+    depths = list(reversed(range(near_count)))
     return [(chip * CORES + core, z) for chip in chip_order(wide_count) for z in depths for core in cores]
 
 
 def message_at(w, z, wide_count, near_count, length):
     if isinstance(w, int):
         return group_places(wide_count, near_count).index((w, z)) * length
-    place = (w // CORES * near_count + z) * CORES + w % CORES
+    place = (w // CORES * near_count + near_count - 1 - z) * CORES + w % CORES
     return pl.multiple_of(place * length, length)
 
 

time: 20.3 us -> 19.2 us (0.946)
  blocking collectives: 11 us -> 9.93 us
    all_to_all x1, blocking collectives: 11 us -> 9.93 us  [shards(): lax.all_to_all(send.reshape(message_count, length // PAIR, PAIR, width),...]
  transfers between devices with their start and end apart: 1 -> 1, of which waited for: 1 -> 1; matrix products, arithmetic and copies ran while one was open for 0% -> 0% of each run, Pallas kernels for 4% -> 5%
where the time goes in v35:
time: 19.2 us; the launch traced here: 19 us
  blocking collectives  9.93 us (52%)
  starting transfers between devices  5.05 us (26%)
  Pallas kernels  2.34 us (12%)
  waiting for transfers between devices  0.95 us (5%)
  between operations  0.68 us (4%)
    all_to_all x1, blocking collectives, shards(): lax.all_to_all(send.reshape(message_count, length // PAIR, PAIR, width),...  9.93 us
    ppermute x1, starting transfers between devices, shards(): far = lax.ppermute(integrals, 'narrow', across)  5.05 us
    pallas_call x1, Pallas kernels, shards(): pl.pallas_call(functools.partial(ladder_kernel, rows, near_count, own_cou...  1.23 us
    ppermute x1, waiting for transfers between devices, shards(): far = lax.ppermute(integrals, 'narrow', across)  0.95 us
    pallas_call x1, Pallas kernels, shards(): pl.pallas_call(functools.partial(route_kernel, own_count, wide_count), ou...  0.89 us
  transfers between devices with their start and end apart: 1, of which 1 were waited for; matrix products, arithmetic and copies ran while one was open for 0% of the time, Pallas kernels for 5%

profile of v35, /device:TPU:0, one launch (start us, length us, event | category | flops | bytes accessed | tf_op | source)
XLA Modules:
  0.0 19.0 jit_solution(1294234673977852067)
XLA Ops:
  0.0 5.0 %collective-permute-start = (bf16[8,32,128]{2,1,0:T(8,128)(2,1)}, bf16[8,32,128]{2,1,0:T(8,128)(2,1)S(1)}, u32[]{:S(2)}, u32[]{:S(2)}) collective-permute-start(bf16[8,32,128]{2,1,0:T(8,128)(2,1)} %refs_4_.1), channel_id=1, source_target_pairs={{0,3},{1,2},{2,1},{3,0},{4,7},{5,6},{6,5},{7,4},{8,11},{9,10},{10,... | collective-permute-start | bytes 196616 | tf_op jit(solution)/shard_map/ppermute | solution.py:197
  5.7 0.9 %route.1 = (bf16[256,256]{1,0:T(8,128)(2,1)S(1)}, bf16[8,128]{1,0:T(8,128)(2,1)S(1)}, bf16[8,32,128]{2,1,0:T(8,128)(2,1)S(1)}) custom-call(s32[8]{0:T(128)} %refs_0_.1, s32[1]{0:T(128)S(6)} %copy.7.refs_1_, s32[8]{0:T(128)} %refs_2_.1, s32[16]{0:T(128)} %refs_3_.1, bf16[8,32,128]{2,1,0:T(8,128)(2,1)} %refs_4_.1), custom_call_target="tpu_custom_call" | custom-call | flops 1073741824 | bytes 1048576 | tf_op jit(solution)/shard_map/route/pallas_call | solution.py:204
  6.6 0.0 copy-start
  6.6 0.9 %collective-permute-done.far_ref = bf16[8,32,128]{2,1,0:T(8,128)(2,1)S(1)} collective-permute-done((bf16[8,32,128]{2,1,0:T(8,128)(2,1)}, bf16[8,32,128]{2,1,0:T(8,128)(2,1)S(1)}, u32[]{:S(2)}, u32[]{:S(2)}) %collective-permute-start) | collective-permute-done | bytes 65568 | tf_op jit(solution)/shard_map/ppermute | solution.py:197
  7.6 0.2 %pack.1 = bf16[1056,128]{1,0:T(8,128)(2,1)S(1)} custom-call(bf16[256,256]{1,0:T(8,128)(2,1)S(1)} %get-tuple-element.8.order_ref, bf16[8,128]{1,0:T(8,128)(2,1)S(1)} %get-tuple-element.9.label_ref, bf16[8,32,128]{2,1,0:T(8,128)(2,1)S(1)} %get-tuple-element.10.near_ref, bf16[8,32,128]{2,1,0:T(8,128)(2,1)S(1)} %collective-permute-done.far_ref), custom_call_target="tpu_custom_call" | custom-call | tf_op jit(solution)/shard_map/pack/pallas_call | solution.py:219
  7.8 9.9 %all_to_all.5 = bf16[16,33,2,128]{3,2,1,0:T(2,128)(2,1)S(1)} all-to-all(bf16[16,33,2,128]{3,2,1,0:T(2,128)(2,1)S(1)} %bitcast.3), channel_id=1, replica_groups={{17,21,16,20,9,13,8,12,25,29,24,28,1,5,0,4},{19,23,18,22,11,15,10,14,27..., dimensions={0} | all-to-all | bytes 540672 | tf_op jit(solution)/shard_map/all_to_all | solution.py:235
  17.7 0.0 copy-done
  17.7 1.2 %ladder.1 = f32[512,256]{1,0:T(8,128)} custom-call(bf16[512,1024]{1,0:T(8,128)(2,1)S(1)} %copy-done, bf16[1056,128]{1,0:T(8,128)(2,1)S(1)} %bitcast.2), custom_call_target="tpu_custom_call" | custom-call | tf_op jit(solution)/shard_map/ladder/pallas_call | solution.py:243
Async XLA Ops:
  0.0 7.6 %collective-permute-start = (bf16[8,32,128]{2,1,0:T(8,128)(2,1)}, bf16[8,32,128]{2,1,0:T(8,128)(2,1)S(1)}, u32[]{:S(2)}, u32[]{:S(2)}) collective-permute-start(bf16[8,32,128]{2,1,0:T(8,128)(2,1)} %refs_4_.1), channel_id=1, source_target_pairs={{0,3},{1,2},{2,1},{3,0},{4,7},{5,6},{6,5},{7,4},{8,11},{9,10},{10,... | collective-permute-start | bytes 196616 | tf_op jit(solution)/shard_map/ppermute | solution.py:197
  6.6 11.1 %copy-start = (bf16[512,1024]{1,0:T(8,128)(2,1)S(1)}, bf16[512,1024]{1,0:T(8,128)(2,1)}, u32[]{:S(2)}) copy-start(bf16[512,1024]{1,0:T(8,128)(2,1)} %amp_ref.1) | copy-start | bytes 3145732

commit v36 on v35

--- a/solution.py
+++ b/solution.py
@@ -25,9 +25,9 @@
     chip_count = wide_count // CORES
     if wide_count > UNROLL:
         return list(range(chip_count))
-    bits = (chip_count - 1).bit_length()
-    flipped = [int(format(chip, "b").zfill(bits)[::-1], 2) for chip in range(2**bits)]
-    return [chip for chip in flipped[1:] if chip < chip_count] + [0]
+    size = 2 ** (chip_count - 1).bit_length()
+    ring = [step ^ (step >> 1) for step in range(1, size)]
+    return [chip for chip in ring if chip < chip_count] + [0]
 
 
 def group_places(wide_count, near_count):

time: 19.2 us -> 19.8 us (1.031)
  blocking collectives: 9.93 us -> 10.6 us
    all_to_all x1, blocking collectives: 9.93 us -> 10.6 us  [shards(): lax.all_to_all(send.reshape(message_count, length // PAIR, PAIR, width),...]
where the time goes in v36:
time: 19.8 us; the launch traced here: 19.6 us
  blocking collectives  10.6 us (54%)
  starting transfers between devices  5.05 us (26%)
  Pallas kernels  2.34 us (12%)
  waiting for transfers between devices  0.95 us (5%)
  between operations  0.68 us (3%)
    all_to_all x1, blocking collectives, shards(): lax.all_to_all(send.reshape(message_count, length // PAIR, PAIR, width),...  10.6 us
    ppermute x1, starting transfers between devices, shards(): far = lax.ppermute(integrals, 'narrow', across)  5.05 us
    pallas_call x1, Pallas kernels, shards(): pl.pallas_call(functools.partial(ladder_kernel, rows, near_count, own_cou...  1.22 us
    ppermute x1, waiting for transfers between devices, shards(): far = lax.ppermute(integrals, 'narrow', across)  0.95 us
    pallas_call x1, Pallas kernels, shards(): pl.pallas_call(functools.partial(route_kernel, own_count, wide_count), ou...  0.89 us
  transfers between devices with their start and end apart: 1, of which 1 were waited for; matrix products, arithmetic and copies ran while one was open for 0% of the time, Pallas kernels for 5%

profile of v36, /device:TPU:0, one launch (start us, length us, event | category | flops | bytes accessed | tf_op | source)
XLA Modules:
  0.0 19.6 jit_solution(9422465712098625276)
XLA Ops:
  0.0 5.0 %collective-permute-start = (bf16[8,32,128]{2,1,0:T(8,128)(2,1)}, bf16[8,32,128]{2,1,0:T(8,128)(2,1)S(1)}, u32[]{:S(2)}, u32[]{:S(2)}) collective-permute-start(bf16[8,32,128]{2,1,0:T(8,128)(2,1)} %refs_4_.1), channel_id=1, source_target_pairs={{0,3},{1,2},{2,1},{3,0},{4,7},{5,6},{6,5},{7,4},{8,11},{9,10},{10,... | collective-permute-start | bytes 196616 | tf_op jit(solution)/shard_map/ppermute | solution.py:197
  5.7 0.9 %route.1 = (bf16[256,256]{1,0:T(8,128)(2,1)S(1)}, bf16[8,128]{1,0:T(8,128)(2,1)S(1)}, bf16[8,32,128]{2,1,0:T(8,128)(2,1)S(1)}) custom-call(s32[8]{0:T(128)} %refs_0_.1, s32[1]{0:T(128)S(6)} %copy.7.refs_1_, s32[8]{0:T(128)} %refs_2_.1, s32[16]{0:T(128)} %refs_3_.1, bf16[8,32,128]{2,1,0:T(8,128)(2,1)} %refs_4_.1), custom_call_target="tpu_custom_call" | custom-call | flops 1073741824 | bytes 1048576 | tf_op jit(solution)/shard_map/route/pallas_call | solution.py:204
  6.6 0.0 copy-start
  6.6 0.9 %collective-permute-done.far_ref = bf16[8,32,128]{2,1,0:T(8,128)(2,1)S(1)} collective-permute-done((bf16[8,32,128]{2,1,0:T(8,128)(2,1)}, bf16[8,32,128]{2,1,0:T(8,128)(2,1)S(1)}, u32[]{:S(2)}, u32[]{:S(2)}) %collective-permute-start) | collective-permute-done | bytes 65568 | tf_op jit(solution)/shard_map/ppermute | solution.py:197
  7.6 0.2 %pack.1 = bf16[1056,128]{1,0:T(8,128)(2,1)S(1)} custom-call(bf16[256,256]{1,0:T(8,128)(2,1)S(1)} %get-tuple-element.8.order_ref, bf16[8,128]{1,0:T(8,128)(2,1)S(1)} %get-tuple-element.9.label_ref, bf16[8,32,128]{2,1,0:T(8,128)(2,1)S(1)} %get-tuple-element.10.near_ref, bf16[8,32,128]{2,1,0:T(8,128)(2,1)S(1)} %collective-permute-done.far_ref), custom_call_target="tpu_custom_call" | custom-call | tf_op jit(solution)/shard_map/pack/pallas_call | solution.py:219
  7.8 10.6 %all_to_all.5 = bf16[16,33,2,128]{3,2,1,0:T(2,128)(2,1)S(1)} all-to-all(bf16[16,33,2,128]{3,2,1,0:T(2,128)(2,1)S(1)} %bitcast.3), channel_id=1, replica_groups={{9,13,8,12,25,29,24,28,17,21,16,20,1,5,0,4},{11,15,10,14,27,31,26,30,19..., dimensions={0} | all-to-all | bytes 540672 | tf_op jit(solution)/shard_map/all_to_all | solution.py:235
  18.4 0.0 copy-done
  18.4 1.2 %ladder.1 = f32[512,256]{1,0:T(8,128)} custom-call(bf16[512,1024]{1,0:T(8,128)(2,1)S(1)} %copy-done, bf16[1056,128]{1,0:T(8,128)(2,1)S(1)} %bitcast.2), custom_call_target="tpu_custom_call" | custom-call | tf_op jit(solution)/shard_map/ladder/pallas_call | solution.py:243
Async XLA Ops:
  0.0 7.6 %collective-permute-start = (bf16[8,32,128]{2,1,0:T(8,128)(2,1)}, bf16[8,32,128]{2,1,0:T(8,128)(2,1)S(1)}, u32[]{:S(2)}, u32[]{:S(2)}) collective-permute-start(bf16[8,32,128]{2,1,0:T(8,128)(2,1)} %refs_4_.1), channel_id=1, source_target_pairs={{0,3},{1,2},{2,1},{3,0},{4,7},{5,6},{6,5},{7,4},{8,11},{9,10},{10,... | collective-permute-start | bytes 196616 | tf_op jit(solution)/shard_map/ppermute | solution.py:197
  6.6 11.8 %copy-start = (bf16[512,1024]{1,0:T(8,128)(2,1)S(1)}, bf16[512,1024]{1,0:T(8,128)(2,1)}, u32[]{:S(2)}) copy-start(bf16[512,1024]{1,0:T(8,128)(2,1)} %amp_ref.1) | copy-start | bytes 3145732

commit v37 on v36

--- a/solution.py
+++ b/solution.py
@@ -25,9 +25,7 @@
     chip_count = wide_count // CORES
     if wide_count > UNROLL:
         return list(range(chip_count))
-    size = 2 ** (chip_count - 1).bit_length()
-    ring = [step ^ (step >> 1) for step in range(1, size)]
-    return [chip for chip in ring if chip < chip_count] + [0]
+    return list(range(1, chip_count)) + [0]
 
 
 def group_places(wide_count, near_count):

time: 19.8 us -> 19.9 us (level)
  no operation moved by 1% of the time
where the time goes in v37:
time: 19.9 us; the launch traced here: 19.7 us
  blocking collectives  10.7 us (54%)
  starting transfers between devices  5.05 us (25%)
  Pallas kernels  2.34 us (12%)
  waiting for transfers between devices  0.95 us (5%)
  between operations  0.68 us (3%)
    all_to_all x1, blocking collectives, shards(): lax.all_to_all(send.reshape(message_count, length // PAIR, PAIR, width),...  10.7 us
    ppermute x1, starting transfers between devices, shards(): far = lax.ppermute(integrals, 'narrow', across)  5.05 us
    pallas_call x1, Pallas kernels, shards(): pl.pallas_call(functools.partial(ladder_kernel, rows, near_count, own_cou...  1.22 us
    ppermute x1, waiting for transfers between devices, shards(): far = lax.ppermute(integrals, 'narrow', across)  0.95 us
    pallas_call x1, Pallas kernels, shards(): pl.pallas_call(functools.partial(route_kernel, own_count, wide_count), ou...  0.89 us
  transfers between devices with their start and end apart: 1, of which 1 were waited for; matrix products, arithmetic and copies ran while one was open for 0% of the time, Pallas kernels for 5%

profile of v37, /device:TPU:0, one launch (start us, length us, event | category | flops | bytes accessed | tf_op | source)
XLA Modules:
  0.0 19.7 jit_solution(6195796506923166235)
XLA Ops:
  0.0 5.0 %collective-permute-start = (bf16[8,32,128]{2,1,0:T(8,128)(2,1)}, bf16[8,32,128]{2,1,0:T(8,128)(2,1)S(1)}, u32[]{:S(2)}, u32[]{:S(2)}) collective-permute-start(bf16[8,32,128]{2,1,0:T(8,128)(2,1)} %refs_4_.1), channel_id=1, source_target_pairs={{0,3},{1,2},{2,1},{3,0},{4,7},{5,6},{6,5},{7,4},{8,11},{9,10},{10,... | collective-permute-start | bytes 196616 | tf_op jit(solution)/shard_map/ppermute | solution.py:195
  5.7 0.9 %route.1 = (bf16[256,256]{1,0:T(8,128)(2,1)S(1)}, bf16[8,128]{1,0:T(8,128)(2,1)S(1)}, bf16[8,32,128]{2,1,0:T(8,128)(2,1)S(1)}) custom-call(s32[8]{0:T(128)} %refs_0_.1, s32[1]{0:T(128)S(6)} %copy.7.refs_1_, s32[8]{0:T(128)} %refs_2_.1, s32[16]{0:T(128)} %refs_3_.1, bf16[8,32,128]{2,1,0:T(8,128)(2,1)} %refs_4_.1), custom_call_target="tpu_custom_call" | custom-call | flops 1073741824 | bytes 1048576 | tf_op jit(solution)/shard_map/route/pallas_call | solution.py:202
  6.6 0.0 copy-start
  6.6 0.9 %collective-permute-done.far_ref = bf16[8,32,128]{2,1,0:T(8,128)(2,1)S(1)} collective-permute-done((bf16[8,32,128]{2,1,0:T(8,128)(2,1)}, bf16[8,32,128]{2,1,0:T(8,128)(2,1)S(1)}, u32[]{:S(2)}, u32[]{:S(2)}) %collective-permute-start) | collective-permute-done | bytes 65568 | tf_op jit(solution)/shard_map/ppermute | solution.py:195
  7.6 0.2 %pack.1 = bf16[1056,128]{1,0:T(8,128)(2,1)S(1)} custom-call(bf16[256,256]{1,0:T(8,128)(2,1)S(1)} %get-tuple-element.8.order_ref, bf16[8,128]{1,0:T(8,128)(2,1)S(1)} %get-tuple-element.9.label_ref, bf16[8,32,128]{2,1,0:T(8,128)(2,1)S(1)} %get-tuple-element.10.near_ref, bf16[8,32,128]{2,1,0:T(8,128)(2,1)S(1)} %collective-permute-done.far_ref), custom_call_target="tpu_custom_call" | custom-call | tf_op jit(solution)/shard_map/pack/pallas_call | solution.py:217
  7.8 10.7 %all_to_all.5 = bf16[16,33,2,128]{3,2,1,0:T(2,128)(2,1)S(1)} all-to-all(bf16[16,33,2,128]{3,2,1,0:T(2,128)(2,1)S(1)} %bitcast.3), channel_id=1, replica_groups={{9,13,8,12,17,21,16,20,25,29,24,28,1,5,0,4},{11,15,10,14,19,23,18,22,27..., dimensions={0} | all-to-all | bytes 540672 | tf_op jit(solution)/shard_map/all_to_all | solution.py:233
  18.5 0.0 copy-done
  18.5 1.2 %ladder.1 = f32[512,256]{1,0:T(8,128)} custom-call(bf16[512,1024]{1,0:T(8,128)(2,1)S(1)} %copy-done, bf16[1056,128]{1,0:T(8,128)(2,1)S(1)} %bitcast.2), custom_call_target="tpu_custom_call" | custom-call | tf_op jit(solution)/shard_map/ladder/pallas_call | solution.py:241
Async XLA Ops:
  0.0 7.6 %collective-permute-start = (bf16[8,32,128]{2,1,0:T(8,128)(2,1)}, bf16[8,32,128]{2,1,0:T(8,128)(2,1)S(1)}, u32[]{:S(2)}, u32[]{:S(2)}) collective-permute-start(bf16[8,32,128]{2,1,0:T(8,128)(2,1)} %refs_4_.1), channel_id=1, source_target_pairs={{0,3},{1,2},{2,1},{3,0},{4,7},{5,6},{6,5},{7,4},{8,11},{9,10},{10,... | collective-permute-start | bytes 196616 | tf_op jit(solution)/shard_map/ppermute | solution.py:195
  6.6 11.9 %copy-start = (bf16[512,1024]{1,0:T(8,128)(2,1)S(1)}, bf16[512,1024]{1,0:T(8,128)(2,1)}, u32[]{:S(2)}) copy-start(bf16[512,1024]{1,0:T(8,128)(2,1)} %amp_ref.1) | copy-start | bytes 3145732

commit v38 on v35

--- a/solution.py
+++ b/solution.py
@@ -31,7 +31,7 @@
 
 
 def group_places(wide_count, near_count):
-    cores = range(CORES)
+    cores = list(reversed(range(CORES)))
     depths = list(reversed(range(near_count)))
     return [(chip * CORES + core, z) for chip in chip_order(wide_count) for z in depths for core in cores]
 
@@ -39,7 +39,7 @@
 def message_at(w, z, wide_count, near_count, length):
     if isinstance(w, int):
         return group_places(wide_count, near_count).index((w, z)) * length
-    place = (w // CORES * near_count + near_count - 1 - z) * CORES + w % CORES
+    place = (w // CORES * near_count + near_count - 1 - z) * CORES + CORES - 1 - w % CORES
     return pl.multiple_of(place * length, length)
 
 

time: 19.2 us -> 18.9 us (0.984)
  blocking collectives: 9.93 us -> 9.56 us
    all_to_all x1, blocking collectives: 9.93 us -> 9.56 us  [shards(): lax.all_to_all(send.reshape(message_count, length // PAIR, PAIR, width),...]
where the time goes in v38:
time: 18.9 us; the launch traced here: 18.6 us
  blocking collectives  9.56 us (51%)
  starting transfers between devices  5.05 us (27%)
  Pallas kernels  2.34 us (12%)
  waiting for transfers between devices  0.95 us (5%)
  between operations  0.68 us (4%)
    all_to_all x1, blocking collectives, shards(): lax.all_to_all(send.reshape(message_count, length // PAIR, PAIR, width),...  9.56 us
    ppermute x1, starting transfers between devices, shards(): far = lax.ppermute(integrals, 'narrow', across)  5.05 us
    pallas_call x1, Pallas kernels, shards(): pl.pallas_call(functools.partial(ladder_kernel, rows, near_count, own_cou...  1.22 us
    ppermute x1, waiting for transfers between devices, shards(): far = lax.ppermute(integrals, 'narrow', across)  0.95 us
    pallas_call x1, Pallas kernels, shards(): pl.pallas_call(functools.partial(route_kernel, own_count, wide_count), ou...  0.89 us
  transfers between devices with their start and end apart: 1, of which 1 were waited for; matrix products, arithmetic and copies ran while one was open for 0% of the time, Pallas kernels for 5%

profile of v38, /device:TPU:0, one launch (start us, length us, event | category | flops | bytes accessed | tf_op | source)
XLA Modules:
  0.0 18.6 jit_solution(1685660905259655738)
XLA Ops:
  0.0 5.0 %collective-permute-start = (bf16[8,32,128]{2,1,0:T(8,128)(2,1)}, bf16[8,32,128]{2,1,0:T(8,128)(2,1)S(1)}, u32[]{:S(2)}, u32[]{:S(2)}) collective-permute-start(bf16[8,32,128]{2,1,0:T(8,128)(2,1)} %refs_4_.1), channel_id=1, source_target_pairs={{0,3},{1,2},{2,1},{3,0},{4,7},{5,6},{6,5},{7,4},{8,11},{9,10},{10,... | collective-permute-start | bytes 196616 | tf_op jit(solution)/shard_map/ppermute | solution.py:197
  5.7 0.9 %route.1 = (bf16[256,256]{1,0:T(8,128)(2,1)S(1)}, bf16[8,128]{1,0:T(8,128)(2,1)S(1)}, bf16[8,32,128]{2,1,0:T(8,128)(2,1)S(1)}) custom-call(s32[8]{0:T(128)} %refs_0_.1, s32[1]{0:T(128)S(6)} %copy.7.refs_1_, s32[8]{0:T(128)} %refs_2_.1, s32[16]{0:T(128)} %refs_3_.1, bf16[8,32,128]{2,1,0:T(8,128)(2,1)} %refs_4_.1), custom_call_target="tpu_custom_call" | custom-call | flops 1073741824 | bytes 1048576 | tf_op jit(solution)/shard_map/route/pallas_call | solution.py:204
  6.6 0.0 copy-start
  6.6 0.9 %collective-permute-done.far_ref = bf16[8,32,128]{2,1,0:T(8,128)(2,1)S(1)} collective-permute-done((bf16[8,32,128]{2,1,0:T(8,128)(2,1)}, bf16[8,32,128]{2,1,0:T(8,128)(2,1)S(1)}, u32[]{:S(2)}, u32[]{:S(2)}) %collective-permute-start) | collective-permute-done | bytes 65568 | tf_op jit(solution)/shard_map/ppermute | solution.py:197
  7.6 0.2 %pack.1 = bf16[1056,128]{1,0:T(8,128)(2,1)S(1)} custom-call(bf16[256,256]{1,0:T(8,128)(2,1)S(1)} %get-tuple-element.8.order_ref, bf16[8,128]{1,0:T(8,128)(2,1)S(1)} %get-tuple-element.9.label_ref, bf16[8,32,128]{2,1,0:T(8,128)(2,1)S(1)} %get-tuple-element.10.near_ref, bf16[8,32,128]{2,1,0:T(8,128)(2,1)S(1)} %collective-permute-done.far_ref), custom_call_target="tpu_custom_call" | custom-call | tf_op jit(solution)/shard_map/pack/pallas_call | solution.py:219
  7.8 9.6 %all_to_all.5 = bf16[16,33,2,128]{3,2,1,0:T(2,128)(2,1)S(1)} all-to-all(bf16[16,33,2,128]{3,2,1,0:T(2,128)(2,1)S(1)} %bitcast.3), channel_id=1, replica_groups={{21,17,20,16,13,9,12,8,29,25,28,24,5,1,4,0},{23,19,22,18,15,11,14,10,31..., dimensions={0} | all-to-all | bytes 540672 | tf_op jit(solution)/shard_map/all_to_all | solution.py:235
  17.4 0.0 copy-done
  17.4 1.2 %ladder.1 = f32[512,256]{1,0:T(8,128)} custom-call(bf16[512,1024]{1,0:T(8,128)(2,1)S(1)} %copy-done, bf16[1056,128]{1,0:T(8,128)(2,1)S(1)} %bitcast.2), custom_call_target="tpu_custom_call" | custom-call | tf_op jit(solution)/shard_map/ladder/pallas_call | solution.py:243
Async XLA Ops:
  0.0 7.6 %collective-permute-start = (bf16[8,32,128]{2,1,0:T(8,128)(2,1)}, bf16[8,32,128]{2,1,0:T(8,128)(2,1)S(1)}, u32[]{:S(2)}, u32[]{:S(2)}) collective-permute-start(bf16[8,32,128]{2,1,0:T(8,128)(2,1)} %refs_4_.1), channel_id=1, source_target_pairs={{0,3},{1,2},{2,1},{3,0},{4,7},{5,6},{6,5},{7,4},{8,11},{9,10},{10,... | collective-permute-start | bytes 196616 | tf_op jit(solution)/shard_map/ppermute | solution.py:197
  6.6 10.8 %copy-start = (bf16[512,1024]{1,0:T(8,128)(2,1)S(1)}, bf16[512,1024]{1,0:T(8,128)(2,1)}, u32[]{:S(2)}) copy-start(bf16[512,1024]{1,0:T(8,128)(2,1)} %amp_ref.1) | copy-start | bytes 3145732
